TPU v7x, 512 devices: a whole 4x8x8 slice. The times are simulated.
512 devices in a mesh: band: 64 (over x, y, core), tp: 8 (over z).
Axes of the slice: x: 4, y: 8, z: 8, core: 2. Of those that a mesh axis runs over, the one named last changes fastest.
Arguments:
- control: float32 [69, 2, 512, 384], P(None, None, ('band', 'tp')), may hold values from -6 to 6
- spec_sigma: float32 [69, 512, 384], P(None, ('band', 'tp')), may hold values from 0.02 to 0.12
- prior_mean_field: float32 [69, 512, 1440], P(None, ('band', 'tp')), may hold values from -6 to 6
- magnitude_factor: float32 [69], replicated, may hold values from 0.25 to 1.75
- w_in: bfloat16 [69, 768], P(None, 'tp'), may hold values from -0.75 to 0.75
- w_out: bfloat16 [768, 69], P('tp'), may hold values from -0.21875 to 0.21875
- obs_band: int32 [64, 8, 1024, 1], P('band', 'tp'), may hold values from 0 to 63; in each aligned block of 1024 rows (0 to 1023, 1024 to 2047, ..., all dimensions but the last counted through in order) at most 64 rows name the same one
- obs_cell: int32 [64, 8, 1024], P('band', 'tp'), may hold values from 0 to 99359
- obs_value: float32 [64, 8, 1024], P('band', 'tp'), may hold values from -8 to 8
- obs_weight: float32 [64, 8, 1024], P('band', 'tp'), may hold values from 0.25 to 4
- obs_offset: float32 [64, 8, 1024], P('band', 'tp'), may hold values from 0 to 1
Outputs:
- grad_control: float32 [69, 2, 512, 384], P(None, None, ('band', 'tp'))
Inputs may be any that keep to these rules, and one draw needn't show every extreme that they name: `obs_band`: among the observations of one device, at most 64 lie in any one band, and in every draw some device has exactly 64 in some band. The observed channel is obs_cell // 1440 and the stencil longitude obs_cell % 1440.
All inputs are finite; a program needn't handle non-finite values.
Results may differ from a plain program's by a relative error of at most 0.0016.
Values may be sent and summed in bfloat16 or wider, within the bound.
No kernel may reach another device: no remote copies, remote signals or barrier semaphores. Data moves between devices by JAX's collectives and lax.ppermute only.
A program may use at most 64 MiB of HBM per device.

v0:
```python
import math

import jax
import jax.numpy as jnp
import ml_dtypes
import numpy as np
from jax import lax
from jax.experimental import pallas as pl
from jax.experimental.pallas import tpu as pltpu
from jax.sharding import PartitionSpec as P

EPSILON = 1e-06
BF16 = jnp.bfloat16
F32 = jnp.float32

BLOCKS = 6
STRIDE = 240
WIDTH = 256
ROWS = 72
LANES = 128
BANDS = 64
TPS = 8
SLOTS = 64
FIELDS = 8
ROW_SHIFT = 256
OBS_CHUNK = 512


def split_np(table):
    high = table.astype(np.float32).astype(ml_dtypes.bfloat16)
    low = (table - high.astype(np.float64)).astype(np.float32).astype(ml_dtypes.bfloat16)
    return high, low


def legendre_np(wave_count, lat_count):
    cycles = np.arange(lat_count)
    tables = []
    for parity in range(2):
        frequency = np.arange(wave_count) + parity
        phases = (2 * cycles[:, None] + 1) * frequency[None, :] % (4 * lat_count)
        angles = phases * (math.pi / (2 * lat_count))
        basis = np.sin(angles) if parity else np.cos(angles)
        tables.append(basis * math.sqrt(2.0 / lat_count))
    return split_np(np.stack(tables))


def zonal_np(orders, lon_count):
    phases = np.arange(orders)[:, None] * np.arange(WIDTH)[None, :] % lon_count
    angles = phases * (2.0 * math.pi / lon_count)
    return split_np(np.concatenate([np.cos(angles), np.sin(angles)], axis=0))


def turn_np(orders, lon_count):
    phases = np.arange(BLOCKS)[:, None] * STRIDE * np.arange(orders)[None, :] % lon_count
    angles = phases * (2.0 * math.pi / lon_count)
    pad = np.zeros((8 - BLOCKS, orders))
    return np.concatenate([np.cos(angles), pad, np.sin(angles), pad]).astype(np.float32)


def split(values):
    high = values.astype(BF16)
    low = (values - high.astype(F32)).astype(BF16)
    return high, low


NN = (((1,), (0,)), ((), ()))
NT = (((1,), (1,)), ((), ()))


def dot(left, right, dims=NN):
    return lax.dot_general(left, right, dims, preferred_element_type=F32)


def dot3(left, right, dims=NN):
    return (
        dot(left[0], right[0], dims) + dot(left[0], right[1], dims) + dot(left[1], right[0], dims)
    )


def lane_ids(shape):
    return lax.broadcasted_iota(jnp.int32, shape, len(shape) - 1)


SEND_ROWS = 224
REST_LANE = 96


def synthesis_kernel(parity, control, sigma, w_in, w_out, table_high, table_low, out, coef, modes):
    channels = w_in.shape[0]
    coef[...] = jnp.zeros_like(coef)
    for block in range(3):
        lanes = pl.ds(block * LANES, LANES)
        deviation = sigma[pl.ds(block, channels, stride=3), :]
        first = deviation * control[pl.ds(block, channels, stride=6), :]
        second = deviation * control[pl.ds(3 + block, channels, stride=6), :]
        coef[0:channels, lanes] = first
        coef[ROWS:LANES, lanes] = second[: LANES - ROWS]
        tail = channels - (LANES - ROWS)
        coef[LANES + REST_LANE : LANES + REST_LANE + tail, lanes] = second[LANES - ROWS :]
    parts = split(coef[...])
    whole = dot3((table_high[0], table_low[0]), parts, NT)
    modes[0] = whole[:, 0:LANES]
    modes[1] = whole[:, LANES:]
    in_rows = jnp.pad(w_in[...].astype(F32), ((0, 80 - channels), (0, LANES - w_in.shape[1])))
    out_rows = jnp.pad(w_out[...].astype(F32), ((0, 80 - channels), (0, LANES - w_in.shape[1])))
    out_rows = out_rows.astype(BF16)
    for dest in range(TPS):
        whole = modes[0, pl.ds(dest, BANDS, stride=TPS), :]
        rest = modes[1, pl.ds(dest, BANDS, stride=TPS), :]
        out[dest, 0:BANDS, :] = whole.astype(BF16)
        out[dest, BANDS : 2 * BANDS, :] = (rest + in_rows[0:BANDS]).astype(BF16)
        out[dest, 2 * BANDS : 144, :] = in_rows[BANDS:].astype(BF16)
        out[dest, 144:SEND_ROWS, :] = out_rows


def synthesis(parity, control, sigma, w_in, w_out_t, table):
    wave_count = table[0].shape[2]
    lat_count = table[0].shape[1]
    whole = lambda shape: pl.BlockSpec(shape, lambda i, p: (0,) * len(shape))
    chosen = pl.BlockSpec((1, lat_count, wave_count), lambda i, p: (p[0], 0, 0))
    return pl.pallas_call(
        synthesis_kernel,
        out_shape=jax.ShapeDtypeStruct((TPS, SEND_ROWS, LANES), BF16),
        grid_spec=pltpu.PrefetchScalarGridSpec(
            num_scalar_prefetch=1,
            grid=(1,),
            in_specs=[
                whole(control.shape),
                whole(sigma.shape),
                whole(w_in.shape),
                whole(w_out_t.shape),
                chosen,
                chosen,
            ],
            out_specs=whole((TPS, SEND_ROWS, LANES)),
            scratch_shapes=[
                pltpu.VMEM((2 * LANES, wave_count), F32),
                pltpu.VMEM((2, lat_count, LANES), F32),
            ],
        ),
        cost_estimate=pl.CostEstimate(flops=400_000_000, bytes_accessed=2_000_000, transcendentals=0),
        name="synthesis",
    )(parity, control, sigma, w_in, w_out_t, *table)


def pack_kernel(band, cell, value, weight, offset, out):
    blocks = band.shape[0]
    cells = cell[...].astype(F32)
    channel = jnp.floor((cells + 0.5) * (1.0 / 1440.0))
    start = cells - 1440.0 * channel - 1.0
    start = jnp.where(start < 0.0, start + 1440.0, start)
    part = jnp.floor((start + 0.5) * (1.0 / STRIDE))
    fields = []
    for source in (value, weight, offset):
        high = source[...].astype(BF16).astype(F32)
        fields += [high, source[...] - high]
    fields += [part * ROWS + channel - ROW_SHIFT, start - part * STRIDE]
    band_ids = lax.broadcasted_iota(jnp.int32, (BANDS, LANES), 0)
    hits = [band_ids == band[i : i + 1, :] for i in range(blocks)]
    ones = [jnp.where(hit, 1.0, 0.0) for hit in hits]
    square = (LANES, 2 * LANES)
    row, column = lax.broadcasted_iota(jnp.int32, square, 0), lane_ids(square)
    before = jnp.where((row < column) | (column >= LANES), 1.0, 0.0).astype(BF16)
    counts = dot(jnp.concatenate(ones, axis=0).astype(BF16), before)
    slot_ids = lax.broadcasted_iota(jnp.int32, (LANES, LANES), 0).astype(F32)
    taken = jnp.zeros((BANDS, LANES), F32)
    total = jnp.zeros((BANDS, FIELDS * LANES), F32)
    for i in range(blocks):
        within = counts[i * BANDS : (i + 1) * BANDS, :]
        rank = jnp.sum(ones[i] * (within[:, :LANES] + taken), axis=0, keepdims=True)
        taken = taken + within[:, LANES:]
        here = slot_ids == rank + (LANES - SLOTS)
        spread = [jnp.where(here, field[i : i + 1, :], 0.0).astype(BF16) for field in fields]
        total = total + dot(ones[i].astype(BF16), jnp.concatenate(spread, axis=0), NT)
    out[...] = total


def pack_obs(band, cell, value, weight, offset):
    return pl.pallas_call(
        pack_kernel,
        out_shape=jax.ShapeDtypeStruct((BANDS, FIELDS * LANES), F32),
        cost_estimate=pl.CostEstimate(flops=200_000_000, bytes_accessed=300_000, transcendentals=0),
        name="pack_obs",
    )(band, cell, value, weight, offset)


def regroup_kernel(arrived, obs, out, rows):
    lanes = lane_ids((BANDS, LANES))
    for t in range(TPS):
        rows[pl.ds(t, BANDS, stride=16), :] = arrived[t, 0:BANDS, :].astype(F32)
        rest = pltpu.roll(arrived[t, BANDS : 2 * BANDS, :].astype(F32), LANES - REST_LANE, 1)
        rest = jnp.where(lanes < 16, rest, obs[:, t * LANES : (t + 1) * LANES])
        rows[pl.ds(8 + t, BANDS, stride=16), :] = rest
    out[...] = rows[...].astype(BF16)


def regroup(arrived, obs):
    return pl.pallas_call(
        regroup_kernel,
        out_shape=jax.ShapeDtypeStruct((BANDS * 16, LANES), BF16),
        scratch_shapes=[pltpu.VMEM((BANDS * 16, LANES), F32)],
        cost_estimate=pl.CostEstimate(flops=300_000, bytes_accessed=800_000, transcendentals=0),
        name="regroup",
    )(arrived, obs)


def weights_kernel(arrived, in_rows, in_columns, out_rows, out_columns):
    for columns, rows, start in ((in_columns, in_rows, BANDS), (out_columns, out_rows, 144)):
        pieces = []
        for t in range(TPS):
            piece = arrived[t, start : start + 80, :].astype(F32)
            piece = jnp.concatenate([piece, jnp.zeros((LANES - 80, LANES), F32)], axis=0)
            pieces.append(piece.T[0:96])
        upright = jnp.concatenate(pieces, axis=0)
        columns[...] = upright.astype(BF16)
        rows[...] = upright.T[0:80].astype(BF16)


def gather_weights(arrived):
    hidden = TPS * 96
    return pl.pallas_call(
        weights_kernel,
        out_shape=(
            jax.ShapeDtypeStruct((80, hidden), BF16),
            jax.ShapeDtypeStruct((hidden, LANES), BF16),
            jax.ShapeDtypeStruct((80, hidden), BF16),
            jax.ShapeDtypeStruct((hidden, LANES), BF16),
        ),
        cost_estimate=pl.CostEstimate(flops=1_000_000, bytes_accessed=1_500_000, transcendentals=0),
        name="weights",
    )(arrived)


GELU_SCALE = math.sqrt(2.0 / math.pi)
GELU_CUBE = 0.044715


def lagrange_rows(offset):
    return (
        -offset * (offset - 1.0) * (offset - 2.0) / 6.0,
        (offset + 1.0) * (offset - 1.0) * (offset - 2.0) / 2.0,
        -(offset + 1.0) * offset * (offset - 2.0) / 2.0,
        (offset + 1.0) * offset * (offset - 1.0) / 6.0,
    )


def cycle_kernel(
    channels,
    arrived,
    prior,
    gains,
    in_rows,
    in_columns,
    out_rows,
    out_columns,
    table_high,
    table_low,
    turns,
    out,
    state,
    forecast_t,
    slopes,
    obs,
    forcing,
    paired,
):
    orders = turns.shape[1]
    table = (table_high[...], table_low[...])
    slices = arrived[...].astype(F32)
    rest = slices[:, 8:16, :]
    cos_sin = slices[:, 0:8, :].reshape(orders, LANES).T
    tail = rest.reshape(orders, LANES).T
    cos_part = cos_sin[0:ROWS]
    sin_part = jnp.concatenate([cos_sin[ROWS:LANES], tail[0:16]], axis=0)
    pairs = rest.reshape(BANDS // 2, 2, FIELDS, LANES)
    near = pltpu.roll(pairs[:, 0].reshape(BANDS // 2 * FIELDS, LANES), LANES - SLOTS, 1)
    near = near.reshape(BANDS // 2, FIELDS, LANES)
    lanes = lane_ids(near.shape)
    obs[...] = jnp.where(lanes < SLOTS, near, pairs[:, 1])

    for a in range(BLOCKS):
        turn_cos, turn_sin = turns[a : a + 1, :], turns[8 + a : 9 + a, :]
        turned = jnp.concatenate(
            [cos_part * turn_cos + sin_part * turn_sin, sin_part * turn_cos - cos_part * turn_sin],
            axis=1,
        )
        field = prior[a] + dot3(split(turned), table)
        state[a] = field
        mean_sq = jnp.sum(field * field, axis=0, keepdims=True) * (1.0 / channels)
        unit = (field * gains[...] * lax.rsqrt(mean_sq + EPSILON)).astype(BF16)
        pre = dot(in_columns[:, 0:ROWS], unit)
        square = pre * pre
        inner = pre * (GELU_SCALE + (GELU_SCALE * GELU_CUBE) * square)
        half = 0.5 + 0.5 * jnp.tanh(inner)
        hidden = pre * half
        slopes[a] = half + hidden * (1.0 - half) * (
            2.0 * GELU_SCALE + (6.0 * GELU_SCALE * GELU_CUBE) * square
        )
        ahead = field + dot(out_rows[...], hidden.astype(BF16))[0:ROWS]
        ahead_t = ahead.T
        high = ahead_t.astype(BF16)
        forecast_t[0:WIDTH, a * ROWS : (a + 1) * ROWS] = high
        forecast_t[WIDTH : 2 * WIDTH, a * ROWS : (a + 1) * ROWS] = (
            ahead_t - high.astype(F32)
        ).astype(BF16)

    forcing[...] = jnp.zeros_like(forcing)
    row_ids = lax.broadcasted_iota(jnp.int32, (BLOCKS * ROWS, OBS_CHUNK), 0).astype(F32)
    place_ids = lax.broadcasted_iota(jnp.int32, (WIDTH, OBS_CHUNK), 0).astype(F32)
    per_chunk = OBS_CHUNK // LANES

    def observe(chunk, carry):
        fields = [obs[chunk * per_chunk + i] for i in range(per_chunk)]
        fields = jnp.concatenate(fields, axis=1)
        value = fields[0:1] + fields[1:2]
        weight = fields[2:3] + fields[3:4]
        offset = fields[4:5] + fields[5:6]
        row = fields[6:7] + float(ROW_SHIFT)
        place = place_ids - fields[7:8]
        chosen = jnp.where(row_ids == row, 1.0, 0.0).astype(BF16)
        picked = dot(forecast_t[...], chosen)
        w_left, w_here, w_right, w_far = lagrange_rows(offset)
        stencil = jnp.where(
            place == 0.0,
            w_left,
            jnp.where(
                place == 1.0,
                w_here,
                jnp.where(place == 2.0, w_right, jnp.where(place == 3.0, w_far, 0.0)),
            ),
        )
        reading = jnp.sum(stencil * (picked[0:WIDTH] + picked[WIDTH:]), axis=0, keepdims=True)
        spread = stencil * (weight * (reading - value))
        high, low = split(spread)
        forcing[...] += dot(chosen, jnp.concatenate([high, low], axis=0), NT)
        return carry

    lax.fori_loop(0, obs.shape[0] // per_chunk, observe, 0)

    lanes = lane_ids((ROWS, WIDTH))
    halos = []
    source = []
    for a in range(BLOCKS):
        rows = slice(a * ROWS, (a + 1) * ROWS)
        both = forcing[rows, 0:WIDTH] + forcing[rows, WIDTH : 2 * WIDTH]
        halos.append(pltpu.roll(both, WIDTH - STRIDE, 1))
        source.append(both)
    grad_cos = jnp.zeros((ROWS, orders), F32)
    grad_sin = jnp.zeros((ROWS, orders), F32)
    for a in range(BLOCKS):
        force = jnp.where(lanes < STRIDE, source[a], 0.0)
        force = force + jnp.where(lanes < 3, halos[a - 1], 0.0)
        grad_hidden = dot(out_columns[:, 0:ROWS], force.astype(BF16))
        grad_pre = (grad_hidden * slopes[a]).astype(BF16)
        grad_unit = dot(in_rows[...], grad_pre)[0:ROWS]
        field = state[a]
        mean_sq = jnp.sum(field * field, axis=0, keepdims=True) * (1.0 / channels)
        inverse = lax.rsqrt(mean_sq + EPSILON)
        scaled = grad_unit * gains[...]
        along = jnp.sum(scaled * field, axis=0, keepdims=True) * (1.0 / channels)
        costate = force + scaled * inverse - field * (along * inverse * inverse * inverse)
        block = dot3(split(costate), table, NT)
        turn_cos, turn_sin = turns[a : a + 1, :], turns[8 + a : 9 + a, :]
        block_cos, block_sin = block[:, 0:orders], block[:, orders:]
        grad_cos = grad_cos + turn_cos * block_cos - turn_sin * block_sin
        grad_sin = grad_sin + turn_sin * block_cos + turn_cos * block_sin

    lanes = lane_ids((orders, LANES))
    pad = jnp.zeros((LANES - ROWS, orders), F32)
    for r, grad in ((0, grad_cos), (1, grad_sin)):
        upright = jnp.concatenate([grad, pad], axis=0).T
        high = upright.astype(BF16).astype(F32)
        low = pltpu.roll(upright - high, channels, 1)
        paired[pl.ds(r, orders, stride=2), :] = jnp.where(lanes < channels, high, low)
    out[...] = paired[...].astype(BF16)


def run_cycle(channels, arrived, prior, gains, weights, table, turns):
    orders = turns.shape[1]
    hidden = weights[1].shape[0]
    return pl.pallas_call(
        lambda *refs: cycle_kernel(channels, *refs),
        out_shape=jax.ShapeDtypeStruct((2 * orders, LANES), BF16),
        scratch_shapes=[
            pltpu.VMEM((BLOCKS, ROWS, WIDTH), F32),
            pltpu.VMEM((2 * WIDTH, BLOCKS * ROWS), BF16),
            pltpu.VMEM((BLOCKS, hidden, WIDTH), F32),
            pltpu.VMEM((BANDS // 2, FIELDS, LANES), F32),
            pltpu.VMEM((BLOCKS * ROWS, 2 * WIDTH), F32),
            pltpu.VMEM((2 * orders, LANES), F32),
        ],
        compiler_params=pltpu.CompilerParams(vmem_limit_bytes=40 * 1024 * 1024),
        cost_estimate=pl.CostEstimate(
            flops=8_000_000_000, bytes_accessed=4_000_000, transcendentals=1_200_000
        ),
        name="cycle",
    )(arrived, prior, gains, *weights, *table, turns)


def analysis_kernel(parity, arrived, control, sigma, table_high, table_low, out, rows):
    channels = sigma.shape[0] // 3
    orders = arrived.shape[0] // 2
    rows[...] = arrived[...].astype(F32)
    lanes = lane_ids((orders, LANES))
    for r in range(2):
        both = rows[pl.ds(r, orders, stride=2), :]
        low = pltpu.roll(both, LANES - channels, 1)
        grad = jnp.where(lanes < channels, both, 0.0)
        grad = grad + jnp.where(lanes < LANES - channels, low, 0.0)
        grad_t = split(grad.T[0:ROWS])
        projected = dot3(grad_t, (table_high[0], table_low[0]))
        for block in range(3):
            deviation = sigma[pl.ds(block, channels, stride=3), :]
            place = pl.ds(3 * r + block, channels, stride=6)
            step = projected[0:channels, block * LANES : (block + 1) * LANES]
            out[place, :] = control[place, :] + deviation * step


def analysis(parity, arrived, control, sigma, table):
    wave_count = table[0].shape[2]
    lat_count = table[0].shape[1]
    whole = lambda shape: pl.BlockSpec(shape, lambda i, p: (0,) * len(shape))
    chosen = pl.BlockSpec((1, lat_count, wave_count), lambda i, p: (p[0], 0, 0))
    return pl.pallas_call(
        analysis_kernel,
        out_shape=jax.ShapeDtypeStruct(control.shape, F32),
        grid_spec=pltpu.PrefetchScalarGridSpec(
            num_scalar_prefetch=1,
            grid=(1,),
            in_specs=[
                whole(arrived.shape),
                whole(control.shape),
                whole(sigma.shape),
                chosen,
                chosen,
            ],
            out_specs=whole(control.shape),
            scratch_shapes=[pltpu.VMEM(arrived.shape, F32)],
        ),
        cost_estimate=pl.CostEstimate(flops=400_000_000, bytes_accessed=2_000_000, transcendentals=0),
        name="analysis",
    )(parity, arrived, control, sigma, *table)


def shards(
    control,
    spec_sigma,
    prior_mean_field,
    magnitude_factor,
    w_in,
    w_out,
    obs_band,
    obs_cell,
    obs_value,
    obs_weight,
    obs_offset,
):
    channels, _, _, wave_count = control.shape
    lat_count = BANDS * TPS
    lon_count = prior_mean_field.shape[2]
    legendre = legendre_np(wave_count, lat_count)
    zonal = zonal_np(lat_count, lon_count)
    turns = turn_np(lat_count, lon_count)
    parity = (lax.axis_index("tp") % 2).astype(jnp.int32).reshape(1)
    control_rows = control.reshape(-1, LANES)
    sigma_rows = spec_sigma.reshape(-1, LANES)

    send = synthesis(parity, control_rows, sigma_rows, w_in, w_out.T, legendre)
    got = lax.all_to_all(send, "tp", split_axis=0, concat_axis=0, tiled=True)
    obs = pack_obs(
        *(
            field.reshape(-1, LANES)
            for field in (obs_band, obs_cell, obs_value, obs_weight, obs_offset)
        )
    )
    send = regroup(got, obs).reshape(BANDS, 16, LANES)
    arrived = lax.all_to_all(send, "band", split_axis=0, concat_axis=0, tiled=True)
    weights = gather_weights(got)
    prior = jnp.pad(prior_mean_field[:, 0, :], ((0, ROWS - channels), (0, 0)))
    prior = jnp.concatenate([prior, prior[:, : WIDTH - STRIDE]], axis=1)
    prior = jnp.stack([prior[:, a * STRIDE : a * STRIDE + WIDTH] for a in range(BLOCKS)])
    gains = jnp.broadcast_to(
        jnp.pad(magnitude_factor, (0, ROWS - channels))[:, None], (ROWS, WIDTH)
    )
    modes = run_cycle(channels, arrived, prior, gains, weights, zonal, turns)
    modes = lax.all_to_all(
        modes.reshape(lat_count, 2, LANES),
        ("band", "tp"),
        split_axis=0,
        concat_axis=0,
        tiled=True,
    )
    result = analysis(
        parity, modes.reshape(2 * lat_count, LANES), control_rows, sigma_rows, legendre
    )
    return result.reshape(control.shape)


def solution(mesh):
    placed = (
        P(None, None, ("band", "tp"), None),
        P(None, ("band", "tp"), None),
        P(None, ("band", "tp"), None),
        P(),
        P(None, "tp"),
        P("tp", None),
        P("band", "tp", None, None),
        P("band", "tp", None),
        P("band", "tp", None),
        P("band", "tp", None),
        P("band", "tp", None),
    )
    return jax.shard_map(
        shards,
        mesh=mesh,
        in_specs=placed,
        out_specs=P(None, None, ("band", "tp"), None),
        check_vma=False,
    )
```

profile of v0, /device:TPU:1, one launch (start us, length us, event | category | flops | bytes accessed | tf_op | source)
XLA Modules:
  0.0 114.7 jit_solution(1415682998704641225)
XLA Ops:
  0.0 0.0 copy-start.9
  0.0 1.2 %reduce.1 = f32[69,384]{1,0:T(8,128)S(1)} reduce(f32[69,1,384]{2,1,0:T(1,128)} %param.17, f32[]{:T(128)} %constant.47), dimensions={1}, to_apply=%param.17.reduce_sub_computation | reduce | bytes 211972 | tf_op args[1]
  1.2 0.6 reshape.39.sigma
  1.8 0.0 copy-done.9
  1.8 0.6 reduce
  2.5 0.9 reshape.38.control
  3.3 2.7 %synthesis.1 = bf16[8,224,128]{2,1,0:T(8,128)(2,1)} custom-call(s32[1]{0:T(128)} %bitcast.parity, f32[414,128]{1,0:T(8,128)} %reshape.38.control, f32[207,128]{1,0:T(8,128)} %reshape.39.sigma, bf16[69,96]{1,0:T(8,128)(2,1)} %w_in.1, bf16[69,96]{1,0:T(8,128)(2,1)} %bitcast.37, bf16[2,512,384]{2,1,0:T(8,128)(2,1)} %constant.30.clone.table_high, ...), custom_call_target="tpu_custom_call" | custom-call | flops 400000000 | bytes 2000000 | tf_op jit(solution)/shard_map/synthesis/pallas_call | solution.py:121
  6.0 0.0 copy-start.8
  6.0 11.0 %all-to-all-start = ((bf16[8,224,128]{2,1,0:T(8,128)(2,1)}), bf16[8,224,128]{2,1,0:T(8,128)(2,1)S(1)}, u32[]{:S(2)}, u32[]{:S(2)}) async-start(bf16[8,224,128]{2,1,0:T(8,128)(2,1)} %synthesis.1), calls=%async_computation | async-start | bytes 917504 | tf_op jit(solution)/shard_map/all_to_all | solution.py:469
  17.0 0.0 copy-done.8
  17.1 0.0 copy-start.10
  17.1 0.6 copy-done.10
  17.7 2.6 %pack_obs.1.obs = f32[64,1024]{1,0:T(8,128)} custom-call(s32[8,128]{1,0:T(8,128)} %bitcast.38, s32[8,128]{1,0:T(8,128)} %bitcast.39, f32[8,128]{1,0:T(8,128)} %bitcast.40, f32[8,128]{1,0:T(8,128)} %bitcast.41, f32[8,128]{1,0:T(8,128)} %bitcast.42), custom_call_target="tpu_custom_call" | custom-call | flops 200000000 | bytes 300000 | tf_op jit(solution)/shard_map/pack_obs/pallas_call | solution.py:179
  20.3 0.1 bitcast_dynamic-update-slice_fusion.3
  20.4 13.1 %all-to-all-done.arrived = bf16[8,224,128]{2,1,0:T(8,128)(2,1)S(1)} async-done(((bf16[8,224,128]{2,1,0:T(8,128)(2,1)}), bf16[8,224,128]{2,1,0:T(8,128)(2,1)S(1)}, u32[]{:S(2)}, u32[]{:S(2)}) %all-to-all-start) | async-done | bytes 458784 | tf_op jit(solution)/shard_map/all_to_all | solution.py:469
  33.5 0.0 copy-start.7
  33.5 0.8 copy-done.7
  34.3 2.0 %regroup.1 = bf16[1024,128]{1,0:T(8,128)(2,1)} custom-call(bf16[8,224,128]{2,1,0:T(8,128)(2,1)} %copy-done.7, f32[64,1024]{1,0:T(8,128)} %pack_obs.1.obs), custom_call_target="tpu_custom_call" | custom-call | flops 300000 | bytes 800000 | tf_op jit(solution)/shard_map/regroup/pallas_call | solution.py:198
  36.3 10.7 %all-to-all-start.1 = ((bf16[64,16,128]{2,1,0:T(8,128)(2,1)}), bf16[64,16,128]{2,1,0:T(8,128)(2,1)S(1)}, u32[]{:S(2)}, u32[]{:S(2)}) async-start(bf16[64,16,128]{2,1,0:T(8,128)(2,1)} %bitcast.35), calls=%async_computation.1 | async-start | bytes 524288 | tf_op jit(solution)/shard_map/all_to_all | solution.py:477
  47.0 0.1 bitcast_dynamic-update-slice_fusion.2
  47.1 0.1 bitcast_dynamic-update-slice_fusion.1
  47.2 0.1 bitcast_dynamic-update-slice_fusion
  47.3 0.0 copy-start.4
  47.3 0.0 copy-start.5
  47.3 0.1 fusion.1.refs_1_
  47.4 2.1 %weights.1 = (bf16[80,768]{1,0:T(8,128)(2,1)}, bf16[768,128]{1,0:T(8,128)(2,1)}, bf16[80,768]{1,0:T(8,128)(2,1)}, bf16[768,128]{1,0:T(8,128)(2,1)}) custom-call(bf16[8,224,128]{2,1,0:T(8,128)(2,1)} %copy-done.7), custom_call_target="tpu_custom_call" | custom-call | flops 1000000 | bytes 1500000 | tf_op jit(solution)/shard_map/weights/pallas_call | solution.py:221
  49.5 0.0 copy-start.6
  49.5 9.5 %all-to-all-done.1.refs_0_ = bf16[64,16,128]{2,1,0:T(8,128)(2,1)S(1)} async-done(((bf16[64,16,128]{2,1,0:T(8,128)(2,1)}), bf16[64,16,128]{2,1,0:T(8,128)(2,1)S(1)}, u32[]{:S(2)}, u32[]{:S(2)}) %all-to-all-start.1) | async-done | bytes 262176 | tf_op jit(solution)/shard_map/all_to_all | solution.py:477
  59.0 0.1 broadcast_in_dim.2.refs_2_
  59.1 0.0 copy-done.4
  59.1 0.0 copy-done.5
  59.1 0.0 copy-done.6
  59.1 0.0 copy-start
  59.1 0.9 copy-done
  60.1 0.0 copy-start.1
  60.1 0.9 copy-done.1
  61.0 0.0 copy-start.2
  61.0 0.9 copy-done.2
  61.9 0.0 copy-start.3
  61.9 0.9 copy-done.3
  62.8 20.2 %cycle.1 = bf16[1024,128]{1,0:T(8,128)(2,1)S(1)} custom-call(bf16[64,16,128]{2,1,0:T(8,128)(2,1)S(1)} %all-to-all-done.1.refs_0_, f32[6,72,256]{2,1,0:T(8,128)S(1)} %fusion.1.refs_1_, f32[72,256]{1,0:T(8,128)S(1)} %broadcast_in_dim.2.refs_2_, bf16[80,768]{1,0:T(8,128)(2,1)S(1)} %copy-done.2, bf16[768,128]{1,0:T(8,128)(2,1)S(1)} %copy-done, ...), custom_call_target="tpu_custom_call" | custom-call | flops 8000000000 | bytes 4000000 | tf_op jit(solution)/shard_map/cycle/pallas_call | solution.py:381
  83.0 27.2 %all_to_all.15 = bf16[512,2,128]{2,1,0:T(2,128)(2,1)} all-to-all(bf16[512,2,128]{2,1,0:T(2,128)(2,1)S(1)} %bitcast.27), channel_id=1, replica_groups=mesh['band'=64,'tp'=8] {'band','tp'}, dimensions={0} | all-to-all | bytes 524288 | tf_op jit(solution)/shard_map/all_to_all | solution.py:486
  110.2 2.7 %analysis.1 = f32[414,128]{1,0:T(8,128)} custom-call(s32[1]{0:T(128)} %bitcast.parity, bf16[1024,128]{1,0:T(8,128)(2,1)} %bitcast.36, f32[414,128]{1,0:T(8,128)} %reshape.38.control, f32[207,128]{1,0:T(8,128)} %reshape.39.sigma, bf16[2,512,384]{2,1,0:T(8,128)(2,1)} %constant.30.clone.table_high, bf16[2,512,384]{2,1,0:T(8,128)(2,1)} %constant.31.clone.table_low), custom_call_target="tpu_custom_call" | custom-call | flops 400000000 | bytes 2000000 | tf_op jit(solution)/shard_map/analysis/pallas_call | solution.py:424
  112.9 1.8 %reshape.49 = f32[69,2,1,384]{3,2,1,0:T(1,128)} reshape(f32[414,128]{1,0:T(8,128)} %analysis.1) | data formatting | bytes 423936 | tf_op jit(solution)/shard_map/reshape | solution.py:496
  (5 shorter events, 0.1 us)
Async XLA Ops:
  0.0 1.8 %copy-start.9 = (f32[69,2,1,384]{3,2,1,0:T(1,128)S(1)}, f32[69,2,1,384]{3,2,1,0:T(1,128)}, u32[]{:S(2)}) copy-start(f32[69,2,1,384]{3,2,1,0:T(1,128)} %param.16) | copy-start | bytes 635908
  6.0 11.0 %copy-start.8 = (f32[69,1,1440]{2,1,0:T(1,128)S(1)}, f32[69,1,1440]{2,1,0:T(1,128)}, u32[]{:S(2)}) copy-start(f32[69,1,1440]{2,1,0:T(1,128)} %param.18) | copy-start | bytes 1192324
  6.0 27.5 %all-to-all-start = ((bf16[8,224,128]{2,1,0:T(8,128)(2,1)}), bf16[8,224,128]{2,1,0:T(8,128)(2,1)S(1)}, u32[]{:S(2)}, u32[]{:S(2)}) async-start(bf16[8,224,128]{2,1,0:T(8,128)(2,1)} %synthesis.1), calls=%async_computation | async-start | bytes 917504 | tf_op jit(solution)/shard_map/all_to_all | solution.py:469
  17.1 0.7 copy-start.10
  33.5 0.8 copy-start.7
  36.3 22.7 %all-to-all-start.1 = ((bf16[64,16,128]{2,1,0:T(8,128)(2,1)}), bf16[64,16,128]{2,1,0:T(8,128)(2,1)S(1)}, u32[]{:S(2)}, u32[]{:S(2)}) async-start(bf16[64,16,128]{2,1,0:T(8,128)(2,1)} %bitcast.35), calls=%async_computation.1 | async-start | bytes 524288 | tf_op jit(solution)/shard_map/all_to_all | solution.py:477
  47.3 11.8 %copy-start.4 = (bf16[1024,256]{1,0:T(8,128)(2,1)S(1)}, bf16[1024,256]{1,0:T(8,128)(2,1)}, u32[]{:S(2)}) copy-start(bf16[1024,256]{1,0:T(8,128)(2,1)} %constant.33.clone.refs_8_) | copy-start | bytes 1572868
  47.3 11.8 %copy-start.5 = (bf16[1024,256]{1,0:T(8,128)(2,1)S(1)}, bf16[1024,256]{1,0:T(8,128)(2,1)}, u32[]{:S(2)}) copy-start(bf16[1024,256]{1,0:T(8,128)(2,1)} %constant.32.clone.refs_7_) | copy-start | bytes 1572868
  49.5 9.6 %copy-start.6 = (f32[16,512]{1,0:T(8,128)S(1)}, f32[16,512]{1,0:T(8,128)}, u32[]{:S(2)}) copy-start(f32[16,512]{1,0:T(8,128)} %constant.34.clone.refs_9_) | copy-start | bytes 98308
  59.1 0.9 copy-start
  60.1 0.9 copy-start.1
  61.0 0.9 copy-start.2
  61.9 0.9 copy-start.3
where the time goes:
time: 115 us
  Pallas kernels  32.3 us (28%)
  blocking collectives  27.2 us (24%)
  waiting for transfers between devices  22.6 us (20%)
  starting transfers between devices  21.7 us (19%)
  local copies, waits for them, and re-layouts  8.86 us (8%)
  other arithmetic  1.91 us (2%)
    all_to_all x1, blocking collectives, shards(): lax.all_to_all(modes.reshape(lat_count, 2, LANES), ('band', 'tp'), split_...  27.2 us
    pallas_call x1, Pallas kernels, run_cycle(): pl.pallas_call(lambda *refs: cycle_kernel(channels, *refs), out_shape=jax...  20.2 us
    all_to_all x1, waiting for transfers between devices, shards(): got = lax.all_to_all(send, 'tp', split_axis=0, concat_axis=0, tiled=True)  13.1 us
    all_to_all x1, starting transfers between devices, shards(): got = lax.all_to_all(send, 'tp', split_axis=0, concat_axis=0, tiled=True)  11 us
    all_to_all x1, starting transfers between devices, shards(): lax.all_to_all(send, 'band', split_axis=0, concat_axis=0, tiled=True)  10.7 us
    all_to_all x1, waiting for transfers between devices, shards(): lax.all_to_all(send, 'band', split_axis=0, concat_axis=0, tiled=True)  9.5 us
    unnamed x28, local copies, waits for them, and re-layouts  5.43 us
    pallas_call x1, Pallas kernels, analysis(): pl.pallas_call(analysis_kernel, out_shape=jax.ShapeDtypeStruct(control.sh...  2.73 us
  transfers between devices with their start and end apart: 2, of which 2 were waited for; matrix products, arithmetic and copies ran while one was open for 0% of the time, Pallas kernels for 4%

commit v1 on v0

--- a/solution.py
+++ b/solution.py
@@ -24,6 +24,7 @@
 FIELDS = 8
 ROW_SHIFT = 256
 OBS_CHUNK = 512
+MIB = 1024 * 1024
 
 
 def split_np(table):
@@ -47,7 +48,8 @@
 def zonal_np(orders, lon_count):
     phases = np.arange(orders)[:, None] * np.arange(WIDTH)[None, :] % lon_count
     angles = phases * (2.0 * math.pi / lon_count)
-    return split_np(np.concatenate([np.cos(angles), np.sin(angles)], axis=0))
+    high, low = split_np(np.concatenate([np.cos(angles), np.sin(angles)], axis=0))
+    return high, low, np.ascontiguousarray(high.T), np.ascontiguousarray(low.T)
 
 
 def turn_np(orders, lon_count):
@@ -88,15 +90,13 @@
 def synthesis_kernel(parity, control, sigma, w_in, w_out, table_high, table_low, out, coef, modes):
     channels = w_in.shape[0]
     coef[...] = jnp.zeros_like(coef)
-    for block in range(3):
-        lanes = pl.ds(block * LANES, LANES)
-        deviation = sigma[pl.ds(block, channels, stride=3), :]
-        first = deviation * control[pl.ds(block, channels, stride=6), :]
-        second = deviation * control[pl.ds(3 + block, channels, stride=6), :]
-        coef[0:channels, lanes] = first
-        coef[ROWS:LANES, lanes] = second[: LANES - ROWS]
-        tail = channels - (LANES - ROWS)
-        coef[LANES + REST_LANE : LANES + REST_LANE + tail, lanes] = second[LANES - ROWS :]
+    deviation = sigma[:, 0, :]
+    first = deviation * control[:, 0, 0, :]
+    second = deviation * control[:, 1, 0, :]
+    coef[0:channels, :] = first
+    coef[ROWS:LANES, :] = second[: LANES - ROWS]
+    tail = channels - (LANES - ROWS)
+    coef[LANES + REST_LANE : LANES + REST_LANE + tail, :] = second[LANES - ROWS :]
     parts = split(coef[...])
     whole = dot3((table_high[0], table_low[0]), parts, NT)
     modes[0] = whole[:, 0:LANES]
@@ -139,6 +139,7 @@
             ],
         ),
         cost_estimate=pl.CostEstimate(flops=400_000_000, bytes_accessed=2_000_000, transcendentals=0),
+        compiler_params=pltpu.CompilerParams(vmem_limit_bytes=12 * MIB),
         name="synthesis",
     )(parity, control, sigma, w_in, w_out_t, *table)
 
@@ -180,6 +181,7 @@
         pack_kernel,
         out_shape=jax.ShapeDtypeStruct((BANDS, FIELDS * LANES), F32),
         cost_estimate=pl.CostEstimate(flops=200_000_000, bytes_accessed=300_000, transcendentals=0),
+        compiler_params=pltpu.CompilerParams(vmem_limit_bytes=8 * MIB),
         name="pack_obs",
     )(band, cell, value, weight, offset)
 
@@ -200,6 +202,7 @@
         out_shape=jax.ShapeDtypeStruct((BANDS * 16, LANES), BF16),
         scratch_shapes=[pltpu.VMEM((BANDS * 16, LANES), F32)],
         cost_estimate=pl.CostEstimate(flops=300_000, bytes_accessed=800_000, transcendentals=0),
+        compiler_params=pltpu.CompilerParams(vmem_limit_bytes=8 * MIB),
         name="regroup",
     )(arrived, obs)
 
@@ -227,6 +230,7 @@
             jax.ShapeDtypeStruct((hidden, LANES), BF16),
         ),
         cost_estimate=pl.CostEstimate(flops=1_000_000, bytes_accessed=1_500_000, transcendentals=0),
+        compiler_params=pltpu.CompilerParams(vmem_limit_bytes=8 * MIB),
         name="weights",
     )(arrived)
 
@@ -255,17 +259,18 @@
     out_columns,
     table_high,
     table_low,
+    wide_high,
+    wide_low,
     turns,
     out,
     state,
-    forecast_t,
     slopes,
     obs,
-    forcing,
+    chosen_all,
+    spread_all,
     paired,
 ):
     orders = turns.shape[1]
-    table = (table_high[...], table_low[...])
     slices = arrived[...].astype(F32)
     rest = slices[:, 8:16, :]
     cos_sin = slices[:, 0:8, :].reshape(orders, LANES).T
@@ -275,17 +280,22 @@
     pairs = rest.reshape(BANDS // 2, 2, FIELDS, LANES)
     near = pltpu.roll(pairs[:, 0].reshape(BANDS // 2 * FIELDS, LANES), LANES - SLOTS, 1)
     near = near.reshape(BANDS // 2, FIELDS, LANES)
-    lanes = lane_ids(near.shape)
-    obs[...] = jnp.where(lanes < SLOTS, near, pairs[:, 1])
-
+    obs[...] = jnp.where(lane_ids(near.shape) < SLOTS, near, pairs[:, 1])
+
+    turned = []
     for a in range(BLOCKS):
         turn_cos, turn_sin = turns[a : a + 1, :], turns[8 + a : 9 + a, :]
-        turned = jnp.concatenate(
-            [cos_part * turn_cos + sin_part * turn_sin, sin_part * turn_cos - cos_part * turn_sin],
-            axis=1,
-        )
-        field = prior[a] + dot3(split(turned), table)
-        state[a] = field
+        turned_cos = cos_part * turn_cos + sin_part * turn_sin
+        turned_sin = sin_part * turn_cos - cos_part * turn_sin
+        turned.append(jnp.concatenate([turned_cos, turned_sin], axis=1))
+    turned = split(jnp.concatenate(turned, axis=0))
+    state[...] = prior[...].reshape(BLOCKS * ROWS, WIDTH) + dot3(
+        turned, (table_high[...], table_low[...])
+    )
+
+    forecast = []
+    for a in range(BLOCKS):
+        field = state[a * ROWS : (a + 1) * ROWS, :]
         mean_sq = jnp.sum(field * field, axis=0, keepdims=True) * (1.0 / channels)
         unit = (field * gains[...] * lax.rsqrt(mean_sq + EPSILON)).astype(BF16)
         pre = dot(in_columns[:, 0:ROWS], unit)
@@ -296,29 +306,44 @@
         slopes[a] = half + hidden * (1.0 - half) * (
             2.0 * GELU_SCALE + (6.0 * GELU_SCALE * GELU_CUBE) * square
         )
-        ahead = field + dot(out_rows[...], hidden.astype(BF16))[0:ROWS]
-        ahead_t = ahead.T
-        high = ahead_t.astype(BF16)
-        forecast_t[0:WIDTH, a * ROWS : (a + 1) * ROWS] = high
-        forecast_t[WIDTH : 2 * WIDTH, a * ROWS : (a + 1) * ROWS] = (
-            ahead_t - high.astype(F32)
-        ).astype(BF16)
-
-    forcing[...] = jnp.zeros_like(forcing)
-    row_ids = lax.broadcasted_iota(jnp.int32, (BLOCKS * ROWS, OBS_CHUNK), 0).astype(F32)
-    place_ids = lax.broadcasted_iota(jnp.int32, (WIDTH, OBS_CHUNK), 0).astype(F32)
+        forecast.append(field + dot(out_rows[...], hidden.astype(BF16))[0:ROWS])
+    forecast = split(jnp.concatenate(forecast, axis=0).T)
+    forecast = jnp.concatenate(forecast, axis=0)
+
     per_chunk = OBS_CHUNK // LANES
-
-    def observe(chunk, carry):
+    low_ids = lax.broadcasted_iota(jnp.int32, (16, OBS_CHUNK), 0).astype(F32)
+    near_ids = lax.broadcasted_iota(jnp.int32, (32, OBS_CHUNK), 0).astype(F32)
+    none = jnp.zeros((16, OBS_CHUNK), BF16)
+    for chunk in range(obs.shape[0] // per_chunk):
         fields = [obs[chunk * per_chunk + i] for i in range(per_chunk)]
         fields = jnp.concatenate(fields, axis=1)
         value = fields[0:1] + fields[1:2]
         weight = fields[2:3] + fields[3:4]
         offset = fields[4:5] + fields[5:6]
         row = fields[6:7] + float(ROW_SHIFT)
-        place = place_ids - fields[7:8]
-        chosen = jnp.where(row_ids == row, 1.0, 0.0).astype(BF16)
-        picked = dot(forecast_t[...], chosen)
+        row_group = jnp.floor(row * (1.0 / 16.0))
+        first = jnp.where(low_ids == row - 16.0 * row_group, 1.0, 0.0).astype(BF16)
+        row_group = jnp.broadcast_to(row_group, (16, OBS_CHUNK)).astype(BF16)
+        chosen = jnp.concatenate(
+            [
+                jnp.where(row_group == jnp.array(float(g), BF16), first, none)
+                for g in range(BLOCKS * ROWS // 16)
+            ],
+            axis=0,
+        )
+        columns = slice(chunk * OBS_CHUNK, (chunk + 1) * OBS_CHUNK)
+        chosen_all[:, columns] = chosen
+        picked = dot(forecast, chosen)
+        group = jnp.floor(fields[7:8] * (1.0 / 16.0))
+        place = near_ids - (fields[7:8] - 16.0 * group)
+        group8 = jnp.broadcast_to(group, (8, OBS_CHUNK))
+        window = [jnp.zeros((8, OBS_CHUNK), F32)] * 4
+        for g in range(WIDTH // 16 - 1):
+            mask = group8 == float(g)
+            for i in range(4):
+                rows = slice(16 * g + 8 * i, 16 * g + 8 * i + 8)
+                window[i] = jnp.where(mask, picked[rows] + picked[WIDTH:][rows], window[i])
+        window = jnp.concatenate(window, axis=0)
         w_left, w_here, w_right, w_far = lagrange_rows(offset)
         stencil = jnp.where(
             place == 0.0,
@@ -329,38 +354,46 @@
                 jnp.where(place == 2.0, w_right, jnp.where(place == 3.0, w_far, 0.0)),
             ),
         )
-        reading = jnp.sum(stencil * (picked[0:WIDTH] + picked[WIDTH:]), axis=0, keepdims=True)
-        spread = stencil * (weight * (reading - value))
-        high, low = split(spread)
-        forcing[...] += dot(chosen, jnp.concatenate([high, low], axis=0), NT)
-        return carry
-
-    lax.fori_loop(0, obs.shape[0] // per_chunk, observe, 0)
-
-    lanes = lane_ids((ROWS, WIDTH))
-    halos = []
-    source = []
+        reading = jnp.sum(stencil * window, axis=0, keepdims=True)
+        parts = split(stencil * (weight * (reading - value)))
+        group = jnp.broadcast_to(group, (16, OBS_CHUNK)).astype(BF16)
+        masks = [group == jnp.array(float(g), BF16) for g in range(WIDTH // 16 - 1)]
+        for i, part in enumerate(parts):
+            pieces = []
+            for g in range(WIDTH // 16):
+                piece = none
+                if g > 0:
+                    piece = jnp.where(masks[g - 1], part[16:32], piece)
+                if g < WIDTH // 16 - 1:
+                    piece = jnp.where(masks[g], part[0:16], piece)
+                pieces.append(piece)
+            spread_all[i * WIDTH : (i + 1) * WIDTH, columns] = jnp.concatenate(pieces, axis=0)
+    forcing = dot(chosen_all[...], spread_all[...], NT)
+    forcing = forcing[:, 0:WIDTH] + forcing[:, WIDTH:]
+
+    lanes = lane_ids((BLOCKS * ROWS, WIDTH))
+    halo = pltpu.roll(forcing, WIDTH - STRIDE, 1)
+    halo = jnp.concatenate([halo[(BLOCKS - 1) * ROWS :], halo[: (BLOCKS - 1) * ROWS]], axis=0)
+    forcing = jnp.where(lanes < STRIDE, forcing, 0.0) + jnp.where(lanes < 3, halo, 0.0)
+    costate = []
     for a in range(BLOCKS):
-        rows = slice(a * ROWS, (a + 1) * ROWS)
-        both = forcing[rows, 0:WIDTH] + forcing[rows, WIDTH : 2 * WIDTH]
-        halos.append(pltpu.roll(both, WIDTH - STRIDE, 1))
-        source.append(both)
-    grad_cos = jnp.zeros((ROWS, orders), F32)
-    grad_sin = jnp.zeros((ROWS, orders), F32)
-    for a in range(BLOCKS):
-        force = jnp.where(lanes < STRIDE, source[a], 0.0)
-        force = force + jnp.where(lanes < 3, halos[a - 1], 0.0)
+        force = forcing[a * ROWS : (a + 1) * ROWS]
         grad_hidden = dot(out_columns[:, 0:ROWS], force.astype(BF16))
         grad_pre = (grad_hidden * slopes[a]).astype(BF16)
         grad_unit = dot(in_rows[...], grad_pre)[0:ROWS]
-        field = state[a]
+        field = state[a * ROWS : (a + 1) * ROWS, :]
         mean_sq = jnp.sum(field * field, axis=0, keepdims=True) * (1.0 / channels)
         inverse = lax.rsqrt(mean_sq + EPSILON)
         scaled = grad_unit * gains[...]
         along = jnp.sum(scaled * field, axis=0, keepdims=True) * (1.0 / channels)
-        costate = force + scaled * inverse - field * (along * inverse * inverse * inverse)
-        block = dot3(split(costate), table, NT)
+        costate.append(force + scaled * inverse - field * (along * inverse * inverse * inverse))
+    costate = split(jnp.concatenate(costate, axis=0))
+    blocks = dot3(costate, (wide_high[...], wide_low[...]))
+    grad_cos = jnp.zeros((ROWS, orders), F32)
+    grad_sin = jnp.zeros((ROWS, orders), F32)
+    for a in range(BLOCKS):
         turn_cos, turn_sin = turns[a : a + 1, :], turns[8 + a : 9 + a, :]
+        block = blocks[a * ROWS : (a + 1) * ROWS]
         block_cos, block_sin = block[:, 0:orders], block[:, orders:]
         grad_cos = grad_cos + turn_cos * block_cos - turn_sin * block_sin
         grad_sin = grad_sin + turn_sin * block_cos + turn_cos * block_sin
@@ -382,14 +415,14 @@
         lambda *refs: cycle_kernel(channels, *refs),
         out_shape=jax.ShapeDtypeStruct((2 * orders, LANES), BF16),
         scratch_shapes=[
-            pltpu.VMEM((BLOCKS, ROWS, WIDTH), F32),
-            pltpu.VMEM((2 * WIDTH, BLOCKS * ROWS), BF16),
+            pltpu.VMEM((BLOCKS * ROWS, WIDTH), F32),
             pltpu.VMEM((BLOCKS, hidden, WIDTH), F32),
             pltpu.VMEM((BANDS // 2, FIELDS, LANES), F32),
-            pltpu.VMEM((BLOCKS * ROWS, 2 * WIDTH), F32),
+            pltpu.VMEM((BLOCKS * ROWS, BANDS * SLOTS), BF16),
+            pltpu.VMEM((2 * WIDTH, BANDS * SLOTS), BF16),
             pltpu.VMEM((2 * orders, LANES), F32),
         ],
-        compiler_params=pltpu.CompilerParams(vmem_limit_bytes=40 * 1024 * 1024),
+        compiler_params=pltpu.CompilerParams(vmem_limit_bytes=36 * MIB),
         cost_estimate=pl.CostEstimate(
             flops=8_000_000_000, bytes_accessed=4_000_000, transcendentals=1_200_000
         ),
@@ -398,7 +431,7 @@
 
 
 def analysis_kernel(parity, arrived, control, sigma, table_high, table_low, out, rows):
-    channels = sigma.shape[0] // 3
+    channels = sigma.shape[0]
     orders = arrived.shape[0] // 2
     rows[...] = arrived[...].astype(F32)
     lanes = lane_ids((orders, LANES))
@@ -409,11 +442,7 @@
         grad = grad + jnp.where(lanes < LANES - channels, low, 0.0)
         grad_t = split(grad.T[0:ROWS])
         projected = dot3(grad_t, (table_high[0], table_low[0]))
-        for block in range(3):
-            deviation = sigma[pl.ds(block, channels, stride=3), :]
-            place = pl.ds(3 * r + block, channels, stride=6)
-            step = projected[0:channels, block * LANES : (block + 1) * LANES]
-            out[place, :] = control[place, :] + deviation * step
+        out[:, r, 0, :] = control[:, r, 0, :] + sigma[:, 0, :] * projected[0:channels]
 
 
 def analysis(parity, arrived, control, sigma, table):
@@ -438,6 +467,7 @@
             scratch_shapes=[pltpu.VMEM(arrived.shape, F32)],
         ),
         cost_estimate=pl.CostEstimate(flops=400_000_000, bytes_accessed=2_000_000, transcendentals=0),
+        compiler_params=pltpu.CompilerParams(vmem_limit_bytes=12 * MIB),
         name="analysis",
     )(parity, arrived, control, sigma, *table)
 
@@ -462,10 +492,8 @@
     zonal = zonal_np(lat_count, lon_count)
     turns = turn_np(lat_count, lon_count)
     parity = (lax.axis_index("tp") % 2).astype(jnp.int32).reshape(1)
-    control_rows = control.reshape(-1, LANES)
-    sigma_rows = spec_sigma.reshape(-1, LANES)
-
-    send = synthesis(parity, control_rows, sigma_rows, w_in, w_out.T, legendre)
+
+    send = synthesis(parity, control, spec_sigma, w_in, w_out.T, legendre)
     got = lax.all_to_all(send, "tp", split_axis=0, concat_axis=0, tiled=True)
     obs = pack_obs(
         *(
@@ -490,10 +518,8 @@
         concat_axis=0,
         tiled=True,
     )
-    result = analysis(
-        parity, modes.reshape(2 * lat_count, LANES), control_rows, sigma_rows, legendre
-    )
-    return result.reshape(control.shape)
+    modes = modes.reshape(2 * lat_count, LANES)
+    return analysis(parity, modes, control, spec_sigma, legendre)
 
 
 def solution(mesh):

time: 115 us -> 102 us (0.89)
  Pallas kernels: 32.3 us -> 19.1 us
  other arithmetic: 1.91 us -> 0.09 us
    pallas_call x1, Pallas kernels: 20.2 us -> 13.8 us  [run_cycle(): pl.pallas_call(lambda *refs: cycle_kernel(channels, *refs), out_shape=jax...]
    unnamed x28 -> x52, local copies, waits for them, and re-layouts: 5.43 us -> 9.12 us
    reshape x3 -> x0, local copies, waits for them, and re-layouts: 3.32 us -> none  [the longest x1 1.82 us: shards(): return result.reshape(control.shape)]
    unnamed x2 -> x0, other arithmetic: 1.82 us -> none
    pallas_call x1, Pallas kernels: 2.09 us -> 0.36 us  [gather_weights(): pl.pallas_call(weights_kernel, out_shape=(jax.ShapeDtypeStruct((80, hidde...]
    pallas_call x1, Pallas kernels: 2.56 us -> 1.09 us  [pack_obs(): pl.pallas_call(pack_kernel, out_shape=jax.ShapeDtypeStruct((BANDS, FIELDS...]
    pallas_call x1, Pallas kernels: 2.73 us -> 1.42 us  [analysis(): pl.pallas_call(analysis_kernel, out_shape=jax.ShapeDtypeStruct(control.sh...]
    pallas_call x1, Pallas kernels: 2.72 us -> 1.48 us  [synthesis(): pl.pallas_call(synthesis_kernel, out_shape=jax.ShapeDtypeStruct((TPS, SEN...]
  transfers between devices with their start and end apart: 2 -> 2, of which waited for: 2 -> 2; matrix products, arithmetic and copies ran while one was open for 0% -> 1% of each run, Pallas kernels for 4% -> 1%
where the time goes in v1:
time: 102 us; the launch traced here: 101 us
  blocking collectives  26.4 us (26%)
  waiting for transfers between devices  23.5 us (23%)
  starting transfers between devices  21.7 us (21%)
  Pallas kernels  19.1 us (19%)
  local copies, waits for them, and re-layouts  10 us (10%)
    all_to_all x1, blocking collectives, shards(): lax.all_to_all(modes.reshape(lat_count, 2, LANES), ('band', 'tp'), split_...  26.4 us
    pallas_call x1, Pallas kernels, run_cycle(): pl.pallas_call(lambda *refs: cycle_kernel(channels, *refs), out_shape=jax...  13.8 us
    all_to_all x1, waiting for transfers between devices, shards(): got = lax.all_to_all(send, 'tp', split_axis=0, concat_axis=0, tiled=True)  13.1 us
    all_to_all x1, starting transfers between devices, shards(): got = lax.all_to_all(send, 'tp', split_axis=0, concat_axis=0, tiled=True)  11 us
    all_to_all x1, starting transfers between devices, shards(): lax.all_to_all(send, 'band', split_axis=0, concat_axis=0, tiled=True)  10.7 us
    all_to_all x1, waiting for transfers between devices, shards(): lax.all_to_all(send, 'band', split_axis=0, concat_axis=0, tiled=True)  10.4 us
    unnamed x52, local copies, waits for them, and re-layouts  9.12 us
  transfers between devices with their start and end apart: 2, of which 2 were waited for; matrix products, arithmetic and copies ran while one was open for 1% of the time, Pallas kernels for 1%

profile of v1, /device:TPU:1, one launch (start us, length us, event | category | flops | bytes accessed | tf_op | source)
XLA Modules:
  0.0 101.0 jit_solution(15514821117017633406)
XLA Ops:
  0.0 0.0 copy-start.8
  0.0 0.7 copy-done.8
  0.7 0.0 copy-start
  0.7 1.1 %copy-done = bf16[2,512,384]{2,1,0:T(8,128)(2,1)S(1)} copy-done((bf16[2,512,384]{2,1,0:T(8,128)(2,1)S(1)}, bf16[2,512,384]{2,1,0:T(8,128)(2,1)}, u32[]{:S(2)}) %copy-start) | copy-done | bytes 786456
  1.9 0.0 copy-start.2
  1.9 1.1 %copy-done.2 = bf16[2,512,384]{2,1,0:T(8,128)(2,1)S(1)} copy-done((bf16[2,512,384]{2,1,0:T(8,128)(2,1)S(1)}, bf16[2,512,384]{2,1,0:T(8,128)(2,1)}, u32[]{:S(2)}) %copy-start.2) | copy-done | bytes 786456
  3.0 0.0 copy-start.4
  3.0 0.9 copy-done.4
  3.9 0.0 copy-start.6
  3.9 0.9 copy-done.6
  4.8 0.0 copy-start.9
  4.8 0.7 copy-done.9
  5.5 1.5 %synthesis.1 = bf16[8,224,128]{2,1,0:T(8,128)(2,1)} custom-call(s32[1]{0:T(128)} %bitcast.parity, f32[69,2,1,384]{3,2,1,0:T(1,128)S(1)} %copy-done.4, f32[69,1,384]{2,1,0:T(1,128)S(1)} %copy-done.6, bf16[69,96]{1,0:T(8,128)(2,1)S(1)} %copy-done.8, bf16[69,96]{1,0:T(8,128)(2,1)S(1)} %bitcast.29, bf16[2,512,384]{2,1,0:T(8,128)(2,1)S(1)} %copy-done.2, ...), custom_call_target="tpu_custom_call" | custom-call | flops 400000000 | bytes 2000000 | tf_op jit(solution)/shard_map/synthesis/pallas_call | solution.py:121
  7.0 0.0 copy-start.21
  7.0 11.0 %all-to-all-start = ((bf16[8,224,128]{2,1,0:T(8,128)(2,1)}), bf16[8,224,128]{2,1,0:T(8,128)(2,1)S(1)}, u32[]{:S(2)}, u32[]{:S(2)}) async-start(bf16[8,224,128]{2,1,0:T(8,128)(2,1)} %synthesis.1), calls=%async_computation | async-start | bytes 917504 | tf_op jit(solution)/shard_map/all_to_all | solution.py:497
  18.0 0.0 copy-done.21
  18.0 0.0 copy-start.22
  18.1 0.6 copy-done.22
  18.7 0.0 copy-start.12
  18.7 0.0 copy-start.13
  18.7 0.0 copy-start.14
  18.7 0.8 pad.8
  19.5 0.0 copy-start.11
  19.5 0.0 copy-start.10
  19.5 0.0 copy-done.12
  19.5 0.0 copy-done.13
  19.5 0.0 copy-done.14
  19.5 0.7 copy-done.11
  20.2 0.0 copy-done.10
  20.2 1.1 %pack_obs.1.obs = f32[64,1024]{1,0:T(8,128)S(1)} custom-call(s32[8,128]{1,0:T(8,128)S(1)} %bitcast.30, s32[8,128]{1,0:T(8,128)S(1)} %bitcast.31, f32[8,128]{1,0:T(8,128)S(1)} %bitcast.32, f32[8,128]{1,0:T(8,128)S(1)} %bitcast.33, f32[8,128]{1,0:T(8,128)S(1)} %bitcast.34), custom_call_target="tpu_custom_call" | custom-call | flops 200000000 | bytes 300000 | tf_op jit(solution)/shard_map/pack_obs/pallas_call | solution.py:180
  21.3 0.1 bitcast_dynamic-update-slice_fusion.3
  21.4 13.1 %all-to-all-done.arrived = bf16[8,224,128]{2,1,0:T(8,128)(2,1)S(1)} async-done(((bf16[8,224,128]{2,1,0:T(8,128)(2,1)}), bf16[8,224,128]{2,1,0:T(8,128)(2,1)S(1)}, u32[]{:S(2)}, u32[]{:S(2)}) %all-to-all-start) | async-done | bytes 458784 | tf_op jit(solution)/shard_map/all_to_all | solution.py:497
  34.5 0.9 regroup.1
  35.4 10.7 %all-to-all-start.1 = ((bf16[64,16,128]{2,1,0:T(8,128)(2,1)}), bf16[64,16,128]{2,1,0:T(8,128)(2,1)S(1)}, u32[]{:S(2)}, u32[]{:S(2)}) async-start(bf16[64,16,128]{2,1,0:T(8,128)(2,1)} %bitcast.7), calls=%async_computation.1 | async-start | bytes 524288 | tf_op jit(solution)/shard_map/all_to_all | solution.py:505
  46.2 0.1 bitcast_dynamic-update-slice_fusion.2
  46.2 0.0 copy-start.20
  46.2 0.1 bitcast_dynamic-update-slice_fusion.1
  46.3 0.0 copy-start.17
  46.3 0.1 bitcast_dynamic-update-slice_fusion
  46.4 0.8 copy-done.20
  47.3 0.0 copy-start.15
  47.3 0.0 copy-start.16
  47.3 0.1 fusion.1.refs_1_
  47.4 0.4 weights.1
  47.7 0.0 copy-start.19
  47.7 10.4 %all-to-all-done.1.refs_0_ = bf16[64,16,128]{2,1,0:T(8,128)(2,1)S(1)} async-done(((bf16[64,16,128]{2,1,0:T(8,128)(2,1)}), bf16[64,16,128]{2,1,0:T(8,128)(2,1)S(1)}, u32[]{:S(2)}, u32[]{:S(2)}) %all-to-all-start.1) | async-done | bytes 262176 | tf_op jit(solution)/shard_map/all_to_all | solution.py:505
  58.1 0.1 broadcast_in_dim.2.refs_2_
  58.2 0.0 copy-done.17
  58.2 0.0 copy-done.15
  58.2 0.0 copy-done.16
  58.2 0.0 copy-done.19
  58.2 0.0 copy-start.18
  58.3 1.0 %copy-done.18 = bf16[1024,256]{1,0:T(8,128)(2,1)S(1)} copy-done((bf16[1024,256]{1,0:T(8,128)(2,1)S(1)}, bf16[1024,256]{1,0:T(8,128)(2,1)}, u32[]{:S(2)}) %copy-start.18) | copy-done | bytes 524312
  59.3 0.0 copy-start.1
  59.3 0.0 copy-start.3
  59.3 13.8 %cycle.1 = bf16[1024,128]{1,0:T(8,128)(2,1)S(1)} custom-call(bf16[64,16,128]{2,1,0:T(8,128)(2,1)S(1)} %all-to-all-done.1.refs_0_, f32[6,72,256]{2,1,0:T(8,128)S(1)} %fusion.1.refs_1_, f32[72,256]{1,0:T(8,128)S(1)} %broadcast_in_dim.2.refs_2_, bf16[80,768]{1,0:T(8,128)(2,1)S(1)} %get-tuple-element.9.refs_3_, bf16[768,128]{1,0:T(8,128)(2,1)S(1)} %get-tuple-element.10.refs_4_, ...), custom_call_target="tpu_custom_call" | custom-call | flops 8000000000 | bytes 4000000 | tf_op jit(solution)/shard_map/cycle/pallas_call | solution.py:414
  73.1 0.0 copy-start.5
  73.1 0.0 copy-start.7
  73.1 26.4 %all_to_all.15 = bf16[512,2,128]{2,1,0:T(2,128)(2,1)S(1)} all-to-all(bf16[512,2,128]{2,1,0:T(2,128)(2,1)S(1)} %bitcast.28), channel_id=1, replica_groups=mesh['band'=64,'tp'=8] {'band','tp'}, dimensions={0} | all-to-all | bytes 524288 | tf_op jit(solution)/shard_map/all_to_all | solution.py:514
  99.5 0.0 copy-done.1
  99.5 0.0 copy-done.3
  99.5 0.0 copy-done.5
  99.5 0.0 copy-done.7
  99.5 1.4 %analysis.1 = f32[69,2,1,384]{3,2,1,0:T(1,128)} custom-call(s32[1]{0:T(128)} %bitcast.parity, bf16[1024,128]{1,0:T(8,128)(2,1)S(1)} %bitcast.27, f32[69,2,1,384]{3,2,1,0:T(1,128)S(1)} %copy-done.5, f32[69,1,384]{2,1,0:T(1,128)S(1)} %copy-done.7, bf16[2,512,384]{2,1,0:T(8,128)(2,1)S(1)} %copy-done.3, bf16[2,512,384]{2,1,0:T(8,128)(2,1)S(1)} %copy-done.1), custom_call_target="tpu_custom_call" | custom-call | flops 400000000 | bytes 2000000 | tf_op jit(solution)/shard_map/analysis/pallas_call | solution.py:453
  (4 shorter events, 0.1 us)
Async XLA Ops:
  0.0 0.7 copy-start.8
  0.7 1.1 %copy-start = (bf16[2,512,384]{2,1,0:T(8,128)(2,1)S(1)}, bf16[2,512,384]{2,1,0:T(8,128)(2,1)}, u32[]{:S(2)}) copy-start(bf16[2,512,384]{2,1,0:T(8,128)(2,1)} %constant.35.clone.table_low) | copy-start | bytes 2359300
  1.9 1.1 %copy-start.2 = (bf16[2,512,384]{2,1,0:T(8,128)(2,1)S(1)}, bf16[2,512,384]{2,1,0:T(8,128)(2,1)}, u32[]{:S(2)}) copy-start(bf16[2,512,384]{2,1,0:T(8,128)(2,1)} %constant.34.clone.table_high) | copy-start | bytes 2359300
  3.0 0.9 copy-start.4
  3.9 0.9 copy-start.6
  4.8 0.7 copy-start.9
  7.0 11.0 %copy-start.21 = (f32[69,1,1440]{2,1,0:T(1,128)S(1)}, f32[69,1,1440]{2,1,0:T(1,128)}, u32[]{:S(2)}) copy-start(f32[69,1,1440]{2,1,0:T(1,128)} %param.20) | copy-start | bytes 1192324
  7.0 27.5 %all-to-all-start = ((bf16[8,224,128]{2,1,0:T(8,128)(2,1)}), bf16[8,224,128]{2,1,0:T(8,128)(2,1)S(1)}, u32[]{:S(2)}, u32[]{:S(2)}) async-start(bf16[8,224,128]{2,1,0:T(8,128)(2,1)} %synthesis.1), calls=%async_computation | async-start | bytes 917504 | tf_op jit(solution)/shard_map/all_to_all | solution.py:497
  18.0 0.7 copy-start.22
  18.7 0.8 copy-start.12
  18.7 0.8 copy-start.13
  18.7 0.8 copy-start.14
  19.5 0.7 copy-start.11
  19.5 0.7 copy-start.10
  35.4 22.7 %all-to-all-start.1 = ((bf16[64,16,128]{2,1,0:T(8,128)(2,1)}), bf16[64,16,128]{2,1,0:T(8,128)(2,1)S(1)}, u32[]{:S(2)}, u32[]{:S(2)}) async-start(bf16[64,16,128]{2,1,0:T(8,128)(2,1)} %bitcast.7), calls=%async_computation.1 | async-start | bytes 524288 | tf_op jit(solution)/shard_map/all_to_all | solution.py:505
  46.2 1.0 %copy-start.20 = (f32[72,1440]{1,0:T(8,128)S(1)}, f32[72,1440]{1,0:T(8,128)}, u32[]{:S(2)}) copy-start(f32[72,1440]{1,0:T(8,128)} %pad.8) | copy-start | bytes 1244164
  46.3 11.9 %copy-start.17 = (bf16[1024,256]{1,0:T(8,128)(2,1)S(1)}, bf16[1024,256]{1,0:T(8,128)(2,1)}, u32[]{:S(2)}) copy-start(bf16[1024,256]{1,0:T(8,128)(2,1)} %constant.37.clone.refs_8_) | copy-start | bytes 1572868
  47.3 11.0 %copy-start.15 = (bf16[256,1024]{1,0:T(8,128)(2,1)S(1)}, bf16[256,1024]{1,0:T(8,128)(2,1)}, u32[]{:S(2)}) copy-start(bf16[256,1024]{1,0:T(8,128)(2,1)} %constant.39.clone.refs_10_) | copy-start | bytes 1572868
  47.3 11.0 %copy-start.16 = (bf16[256,1024]{1,0:T(8,128)(2,1)S(1)}, bf16[256,1024]{1,0:T(8,128)(2,1)}, u32[]{:S(2)}) copy-start(bf16[256,1024]{1,0:T(8,128)(2,1)} %constant.38.clone.refs_9_) | copy-start | bytes 1572868
  47.7 10.5 %copy-start.19 = (f32[16,512]{1,0:T(8,128)S(1)}, f32[16,512]{1,0:T(8,128)}, u32[]{:S(2)}) copy-start(f32[16,512]{1,0:T(8,128)} %constant.40.clone.refs_11_) | copy-start | bytes 98308
  58.2 1.0 %copy-start.18 = (bf16[1024,256]{1,0:T(8,128)(2,1)S(1)}, bf16[1024,256]{1,0:T(8,128)(2,1)}, u32[]{:S(2)}) copy-start(bf16[1024,256]{1,0:T(8,128)(2,1)} %constant.36.clone.refs_7_) | copy-start | bytes 1572868
  59.3 40.2 %copy-start.1 = (bf16[2,512,384]{2,1,0:T(8,128)(2,1)S(1)}, bf16[2,512,384]{2,1,0:T(8,128)(2,1)}, u32[]{:S(2)}) copy-start(bf16[2,512,384]{2,1,0:T(8,128)(2,1)} %constant.35.clone.table_low) | copy-start | bytes 2359300
  59.3 40.2 %copy-start.3 = (bf16[2,512,384]{2,1,0:T(8,128)(2,1)S(1)}, bf16[2,512,384]{2,1,0:T(8,128)(2,1)}, u32[]{:S(2)}) copy-start(bf16[2,512,384]{2,1,0:T(8,128)(2,1)} %constant.34.clone.table_high) | copy-start | bytes 2359300
  73.1 26.4 %copy-start.5 = (f32[69,2,1,384]{3,2,1,0:T(1,128)S(1)}, f32[69,2,1,384]{3,2,1,0:T(1,128)}, u32[]{:S(2)}) copy-start(f32[69,2,1,384]{3,2,1,0:T(1,128)} %control.3) | copy-start | bytes 635908
  73.1 26.4 %copy-start.7 = (f32[69,1,384]{2,1,0:T(1,128)S(1)}, f32[69,1,384]{2,1,0:T(1,128)}, u32[]{:S(2)}) copy-start(f32[69,1,384]{2,1,0:T(1,128)} %sigma.3) | copy-start | bytes 317956

commit v2 on v1

--- a/solution.py
+++ b/solution.py
@@ -83,13 +83,43 @@
     return lax.broadcasted_iota(jnp.int32, shape, len(shape) - 1)
 
 
-SEND_ROWS = 224
+SEND_ROWS = 144
 REST_LANE = 96
 
 
-def synthesis_kernel(parity, control, sigma, w_in, w_out, table_high, table_low, out, coef, modes):
-    channels = w_in.shape[0]
+def synthesis_kernel(
+    control_hbm,
+    sigma_hbm,
+    high_hbm,
+    low_hbm,
+    shard,
+    out,
+    control,
+    sigma,
+    table_high,
+    table_low,
+    coef,
+    modes,
+    arrivals,
+):
+    parity = lax.rem(lax.axis_index("tp"), 2)
+    copies = [
+        pltpu.make_async_copy(source, target, arrivals.at[i])
+        for i, (source, target) in enumerate(
+            (
+                (control_hbm, control),
+                (sigma_hbm, sigma),
+                (high_hbm.at[parity], table_high),
+                (low_hbm.at[parity], table_low),
+            )
+        )
+    ]
+    for copy in copies:
+        copy.start()
+    channels = sigma.shape[0]
     coef[...] = jnp.zeros_like(coef)
+    copies[0].wait()
+    copies[1].wait()
     deviation = sigma[:, 0, :]
     first = deviation * control[:, 0, 0, :]
     second = deviation * control[:, 1, 0, :]
@@ -98,50 +128,43 @@
     tail = channels - (LANES - ROWS)
     coef[LANES + REST_LANE : LANES + REST_LANE + tail, :] = second[LANES - ROWS :]
     parts = split(coef[...])
-    whole = dot3((table_high[0], table_low[0]), parts, NT)
+    copies[2].wait()
+    copies[3].wait()
+    whole = dot3((table_high[...], table_low[...]), parts, NT)
     modes[0] = whole[:, 0:LANES]
     modes[1] = whole[:, LANES:]
-    in_rows = jnp.pad(w_in[...].astype(F32), ((0, 80 - channels), (0, LANES - w_in.shape[1])))
-    out_rows = jnp.pad(w_out[...].astype(F32), ((0, 80 - channels), (0, LANES - w_in.shape[1])))
-    out_rows = out_rows.astype(BF16)
+    rows = shard[...].astype(F32)
     for dest in range(TPS):
-        whole = modes[0, pl.ds(dest, BANDS, stride=TPS), :]
+        out[dest, 0:BANDS, :] = modes[0, pl.ds(dest, BANDS, stride=TPS), :].astype(BF16)
         rest = modes[1, pl.ds(dest, BANDS, stride=TPS), :]
-        out[dest, 0:BANDS, :] = whole.astype(BF16)
-        out[dest, BANDS : 2 * BANDS, :] = (rest + in_rows[0:BANDS]).astype(BF16)
-        out[dest, 2 * BANDS : 144, :] = in_rows[BANDS:].astype(BF16)
-        out[dest, 144:SEND_ROWS, :] = out_rows
-
-
-def synthesis(parity, control, sigma, w_in, w_out_t, table):
-    wave_count = table[0].shape[2]
-    lat_count = table[0].shape[1]
-    whole = lambda shape: pl.BlockSpec(shape, lambda i, p: (0,) * len(shape))
-    chosen = pl.BlockSpec((1, lat_count, wave_count), lambda i, p: (p[0], 0, 0))
+        out[dest, BANDS : 2 * BANDS, :] = (rest + rows[0:BANDS]).astype(BF16)
+        out[dest, 2 * BANDS : SEND_ROWS, :] = rows[BANDS:].astype(BF16)
+
+
+IN_VMEM = pl.BlockSpec(memory_space=pltpu.VMEM)
+IN_HBM = pl.BlockSpec(memory_space=pltpu.HBM)
+
+
+def synthesis(control, sigma, shard, table):
+    lat_count, wave_count = table[0].shape[1:]
     return pl.pallas_call(
         synthesis_kernel,
         out_shape=jax.ShapeDtypeStruct((TPS, SEND_ROWS, LANES), BF16),
-        grid_spec=pltpu.PrefetchScalarGridSpec(
-            num_scalar_prefetch=1,
-            grid=(1,),
-            in_specs=[
-                whole(control.shape),
-                whole(sigma.shape),
-                whole(w_in.shape),
-                whole(w_out_t.shape),
-                chosen,
-                chosen,
-            ],
-            out_specs=whole((TPS, SEND_ROWS, LANES)),
-            scratch_shapes=[
-                pltpu.VMEM((2 * LANES, wave_count), F32),
-                pltpu.VMEM((2, lat_count, LANES), F32),
-            ],
-        ),
+        in_specs=[IN_HBM] * 4 + [IN_VMEM],
+        out_specs=IN_VMEM,
+        scratch_shapes=[
+            pltpu.VMEM(control.shape, F32),
+            pltpu.VMEM(sigma.shape, F32),
+            pltpu.VMEM((lat_count, wave_count), BF16),
+            pltpu.VMEM((lat_count, wave_count), BF16),
+            pltpu.VMEM((2 * LANES, wave_count), F32),
+            pltpu.VMEM((2, lat_count, LANES), F32),
+            pltpu.SemaphoreType.DMA((4,)),
+        ],
         cost_estimate=pl.CostEstimate(flops=400_000_000, bytes_accessed=2_000_000, transcendentals=0),
         compiler_params=pltpu.CompilerParams(vmem_limit_bytes=12 * MIB),
         name="synthesis",
-    )(parity, control, sigma, w_in, w_out_t, *table)
+    )(control, sigma, *table, shard)
 
 
 def pack_kernel(band, cell, value, weight, offset, out):
@@ -207,11 +230,14 @@
     )(arrived, obs)
 
 
-def weights_kernel(arrived, in_rows, in_columns, out_rows, out_columns):
-    for columns, rows, start in ((in_columns, in_rows, BANDS), (out_columns, out_rows, 144)):
+def weights_kernel(own, other, in_rows, in_columns, out_rows, out_columns):
+    even = lax.rem(lax.axis_index("band"), 2) == 0
+    for columns, rows, first in ((in_columns, in_rows, True), (out_columns, out_rows, False)):
         pieces = []
         for t in range(TPS):
-            piece = arrived[t, start : start + 80, :].astype(F32)
+            mine = own[t, BANDS:SEND_ROWS, :].astype(F32)
+            theirs = other[t, BANDS:SEND_ROWS, :].astype(F32)
+            piece = jnp.where(even == first, mine, theirs)
             piece = jnp.concatenate([piece, jnp.zeros((LANES - 80, LANES), F32)], axis=0)
             pieces.append(piece.T[0:96])
         upright = jnp.concatenate(pieces, axis=0)
@@ -219,7 +245,7 @@
         rows[...] = upright.T[0:80].astype(BF16)
 
 
-def gather_weights(arrived):
+def gather_weights(own, other):
     hidden = TPS * 96
     return pl.pallas_call(
         weights_kernel,
@@ -232,7 +258,7 @@
         cost_estimate=pl.CostEstimate(flops=1_000_000, bytes_accessed=1_500_000, transcendentals=0),
         compiler_params=pltpu.CompilerParams(vmem_limit_bytes=8 * MIB),
         name="weights",
-    )(arrived)
+    )(own, other)
 
 
 GELU_SCALE = math.sqrt(2.0 / math.pi)
@@ -257,12 +283,17 @@
     in_columns,
     out_rows,
     out_columns,
+    turns,
+    table_high_hbm,
+    table_low_hbm,
+    wide_high_hbm,
+    wide_low_hbm,
+    out,
     table_high,
     table_low,
     wide_high,
     wide_low,
-    turns,
-    out,
+    arrivals,
     state,
     slopes,
     obs,
@@ -271,6 +302,19 @@
     paired,
 ):
     orders = turns.shape[1]
+    copies = [
+        pltpu.make_async_copy(source, target, arrivals.at[i])
+        for i, (source, target) in enumerate(
+            (
+                (table_high_hbm, table_high),
+                (table_low_hbm, table_low),
+                (wide_high_hbm, wide_high),
+                (wide_low_hbm, wide_low),
+            )
+        )
+    ]
+    for copy in copies:
+        copy.start()
     slices = arrived[...].astype(F32)
     rest = slices[:, 8:16, :]
     cos_sin = slices[:, 0:8, :].reshape(orders, LANES).T
@@ -289,6 +333,8 @@
         turned_sin = sin_part * turn_cos - cos_part * turn_sin
         turned.append(jnp.concatenate([turned_cos, turned_sin], axis=1))
     turned = split(jnp.concatenate(turned, axis=0))
+    copies[0].wait()
+    copies[1].wait()
     state[...] = prior[...].reshape(BLOCKS * ROWS, WIDTH) + dot3(
         turned, (table_high[...], table_low[...])
     )
@@ -368,8 +414,8 @@
                     piece = jnp.where(masks[g], part[0:16], piece)
                 pieces.append(piece)
             spread_all[i * WIDTH : (i + 1) * WIDTH, columns] = jnp.concatenate(pieces, axis=0)
-    forcing = dot(chosen_all[...], spread_all[...], NT)
-    forcing = forcing[:, 0:WIDTH] + forcing[:, WIDTH:]
+    forcing = dot(spread_all[...], chosen_all[...], NT)
+    forcing = (forcing[0:WIDTH] + forcing[WIDTH:]).T
 
     lanes = lane_ids((BLOCKS * ROWS, WIDTH))
     halo = pltpu.roll(forcing, WIDTH - STRIDE, 1)
@@ -388,6 +434,8 @@
         along = jnp.sum(scaled * field, axis=0, keepdims=True) * (1.0 / channels)
         costate.append(force + scaled * inverse - field * (along * inverse * inverse * inverse))
     costate = split(jnp.concatenate(costate, axis=0))
+    copies[2].wait()
+    copies[3].wait()
     blocks = dot3(costate, (wide_high[...], wide_low[...]))
     grad_cos = jnp.zeros((ROWS, orders), F32)
     grad_sin = jnp.zeros((ROWS, orders), F32)
@@ -414,7 +462,11 @@
     return pl.pallas_call(
         lambda *refs: cycle_kernel(channels, *refs),
         out_shape=jax.ShapeDtypeStruct((2 * orders, LANES), BF16),
+        in_specs=[IN_VMEM] * 8 + [IN_HBM] * 4,
+        out_specs=IN_VMEM,
         scratch_shapes=[
+            *(pltpu.VMEM(part.shape, BF16) for part in table),
+            pltpu.SemaphoreType.DMA((4,)),
             pltpu.VMEM((BLOCKS * ROWS, WIDTH), F32),
             pltpu.VMEM((BLOCKS, hidden, WIDTH), F32),
             pltpu.VMEM((BANDS // 2, FIELDS, LANES), F32),
@@ -427,7 +479,7 @@
             flops=8_000_000_000, bytes_accessed=4_000_000, transcendentals=1_200_000
         ),
         name="cycle",
-    )(arrived, prior, gains, *weights, *table, turns)
+    )(arrived, prior, gains, *weights, turns, *table)
 
 
 def analysis_kernel(parity, arrived, control, sigma, table_high, table_low, out, rows):
@@ -492,8 +544,10 @@
     zonal = zonal_np(lat_count, lon_count)
     turns = turn_np(lat_count, lon_count)
     parity = (lax.axis_index("tp") % 2).astype(jnp.int32).reshape(1)
-
-    send = synthesis(parity, control, spec_sigma, w_in, w_out.T, legendre)
+    even = lax.axis_index("band") % 2 == 0
+    pads = ((0, 80 - channels), (0, LANES - w_in.shape[1]))
+    shard = jnp.pad(jnp.where(even, w_in, w_out.T), pads)
+    send = synthesis(control, spec_sigma, shard, legendre)
     got = lax.all_to_all(send, "tp", split_axis=0, concat_axis=0, tiled=True)
     obs = pack_obs(
         *(
@@ -503,7 +557,8 @@
     )
     send = regroup(got, obs).reshape(BANDS, 16, LANES)
     arrived = lax.all_to_all(send, "band", split_axis=0, concat_axis=0, tiled=True)
-    weights = gather_weights(got)
+    other = lax.ppermute(got, "band", [(i, i ^ 1) for i in range(BANDS)])
+    weights = gather_weights(got, other)
     prior = jnp.pad(prior_mean_field[:, 0, :], ((0, ROWS - channels), (0, 0)))
     prior = jnp.concatenate([prior, prior[:, : WIDTH - STRIDE]], axis=1)
     prior = jnp.stack([prior[:, a * STRIDE : a * STRIDE + WIDTH] for a in range(BLOCKS)])

time: 102 us -> 101 us (level)
  blocking collectives: 26.4 us -> 0 us
  starting transfers between devices: 21.7 us -> 35.1 us
  waiting for transfers between devices: 23.5 us -> 34.3 us
    all_to_all x1 -> x0, blocking collectives: 26.4 us -> none  [shards(): lax.all_to_all(modes.reshape(lat_count, 2, LANES), ('band', 'tp'), split_...]
    all_to_all x0 -> x1, waiting for transfers between devices: none -> 17 us  [shards(): lax.all_to_all(modes.reshape(lat_count, 2, LANES), ('band', 'tp'), split_...]
    all_to_all x0 -> x1, starting transfers between devices: none -> 9.03 us  [shards(): lax.all_to_all(modes.reshape(lat_count, 2, LANES), ('band', 'tp'), split_...]
    all_to_all x1, waiting for transfers between devices: 13.1 us -> 8.56 us  [shards(): got = lax.all_to_all(send, 'tp', split_axis=0, concat_axis=0, tiled=True)]
    ppermute x0 -> x1, starting transfers between devices: none -> 2.55 us  [shards(): other = lax.ppermute(got, 'band', [(i, i ^ 1) for i in range(BANDS)])]
    all_to_all x1, waiting for transfers between devices: 10.4 us -> 7.92 us  [shards(): lax.all_to_all(send, 'band', split_axis=0, concat_axis=0, tiled=True)]
    all_to_all x1, starting transfers between devices: 10.7 us -> 12.5 us  [shards(): lax.all_to_all(send, 'band', split_axis=0, concat_axis=0, tiled=True)]
    unnamed x52 -> x46, local copies, waits for them, and re-layouts: 9.12 us -> 9.75 us
  transfers between devices with their start and end apart: 2 -> 4, of which waited for: 2 -> 4; matrix products, arithmetic and copies ran while one was open for 1% -> 1% of each run, Pallas kernels for 1% -> 1%
where the time goes in v2:
time: 101 us; the launch traced here: 99.9 us
  starting transfers between devices  35.1 us (35%)
  waiting for transfers between devices  34.3 us (34%)
  Pallas kernels  19.6 us (19%)
  local copies, waits for them, and re-layouts  9.88 us (10%)
    all_to_all x1, waiting for transfers between devices, shards(): lax.all_to_all(modes.reshape(lat_count, 2, LANES), ('band', 'tp'), split_...  17 us
    pallas_call x1, Pallas kernels, run_cycle(): pl.pallas_call(lambda *refs: cycle_kernel(channels, *refs), out_shape=jax...  13.6 us
    all_to_all x1, starting transfers between devices, shards(): lax.all_to_all(send, 'band', split_axis=0, concat_axis=0, tiled=True)  12.5 us
    all_to_all x1, starting transfers between devices, shards(): got = lax.all_to_all(send, 'tp', split_axis=0, concat_axis=0, tiled=True)  11 us
    unnamed x46, local copies, waits for them, and re-layouts  9.75 us
    all_to_all x1, starting transfers between devices, shards(): lax.all_to_all(modes.reshape(lat_count, 2, LANES), ('band', 'tp'), split_...  9.03 us
    all_to_all x1, waiting for transfers between devices, shards(): got = lax.all_to_all(send, 'tp', split_axis=0, concat_axis=0, tiled=True)  8.56 us
    all_to_all x1, waiting for transfers between devices, shards(): lax.all_to_all(send, 'band', split_axis=0, concat_axis=0, tiled=True)  7.92 us
  transfers between devices with their start and end apart: 4, of which 4 were waited for; matrix products, arithmetic and copies ran while one was open for 1% of the time, Pallas kernels for 1%

profile of v2, /device:TPU:1, one launch (start us, length us, event | category | flops | bytes accessed | tf_op | source)
XLA Modules:
  0.0 99.9 jit_solution(6360837900865129647)
XLA Ops:
  0.0 0.0 copy-start.18
  0.0 0.0 copy-start.6
  0.0 0.7 copy-done.18
  0.7 0.7 bitcast_select_fusion
  1.5 0.0 copy-done.6
  1.5 0.0 copy-start
  1.5 1.1 %copy-done = bf16[2,512,384]{2,1,0:T(8,128)(2,1)S(1)} copy-done((bf16[2,512,384]{2,1,0:T(8,128)(2,1)S(1)}, bf16[2,512,384]{2,1,0:T(8,128)(2,1)}, u32[]{:S(2)}) %copy-start) | copy-done | bytes 786456
  2.6 0.0 copy-start.2
  2.6 1.1 %copy-done.2 = bf16[2,512,384]{2,1,0:T(8,128)(2,1)S(1)} copy-done((bf16[2,512,384]{2,1,0:T(8,128)(2,1)S(1)}, bf16[2,512,384]{2,1,0:T(8,128)(2,1)}, u32[]{:S(2)}) %copy-start.2) | copy-done | bytes 786456
  3.7 0.0 copy-start.4
  3.7 0.9 copy-done.4
  4.7 2.3 %synthesis.1 = bf16[8,144,128]{2,1,0:T(8,128)(2,1)} custom-call(f32[69,2,1,384]{3,2,1,0:T(1,128)S(1)} %copy-done.4, f32[69,1,384]{2,1,0:T(1,128)S(1)} %copy-done.6, bf16[2,512,384]{2,1,0:T(8,128)(2,1)S(1)} %copy-done, bf16[2,512,384]{2,1,0:T(8,128)(2,1)S(1)} %copy-done.2, bf16[80,128]{1,0:T(8,128)(2,1)S(1)} %pad.12.shard), custom_call_target="tpu_custom_call" | custom-call | flops 400000000 | bytes 2000000 | tf_op jit(solution)/shard_map/synthesis/pallas_call | solution.py:150
  7.0 0.0 copy-start.17
  7.0 11.0 %all-to-all-start = ((bf16[8,144,128]{2,1,0:T(8,128)(2,1)}), bf16[8,144,128]{2,1,0:T(8,128)(2,1)S(1)}, u32[]{:S(2)}, u32[]{:S(2)}) async-start(bf16[8,144,128]{2,1,0:T(8,128)(2,1)} %synthesis.1), calls=%async_computation | async-start | bytes 589824 | tf_op jit(solution)/shard_map/all_to_all | solution.py:551
  18.0 0.0 copy-done.17
  18.0 0.0 copy-start.19
  18.1 0.0 copy-start.9
  18.1 0.0 copy-start.10
  18.1 0.0 copy-start.11
  18.1 0.6 copy-done.19
  18.7 0.0 copy-start.8
  18.7 0.0 copy-start.7
  18.7 0.0 copy-done.9
  18.7 0.0 copy-done.10
  18.8 0.0 copy-done.11
  18.8 0.6 copy-done.8
  19.4 0.0 copy-done.7
  19.4 1.1 %pack_obs.1.obs = f32[64,1024]{1,0:T(8,128)S(1)} custom-call(s32[8,128]{1,0:T(8,128)S(1)} %bitcast.29, s32[8,128]{1,0:T(8,128)S(1)} %bitcast.30, f32[8,128]{1,0:T(8,128)S(1)} %bitcast.31, f32[8,128]{1,0:T(8,128)S(1)} %bitcast.32, f32[8,128]{1,0:T(8,128)S(1)} %bitcast.33), custom_call_target="tpu_custom_call" | custom-call | flops 200000000 | bytes 300000 | tf_op jit(solution)/shard_map/pack_obs/pallas_call | solution.py:203
  20.5 0.1 bitcast_dynamic-update-slice_fusion.3
  20.6 8.6 %all-to-all-done.arrived.own = bf16[8,144,128]{2,1,0:T(8,128)(2,1)S(1)} async-done(((bf16[8,144,128]{2,1,0:T(8,128)(2,1)}), bf16[8,144,128]{2,1,0:T(8,128)(2,1)S(1)}, u32[]{:S(2)}, u32[]{:S(2)}) %all-to-all-start) | async-done | bytes 294944 | tf_op jit(solution)/shard_map/all_to_all | solution.py:551
  29.2 0.9 regroup.1
  30.1 12.5 %all-to-all-start.1 = ((bf16[64,16,128]{2,1,0:T(8,128)(2,1)}), bf16[64,16,128]{2,1,0:T(8,128)(2,1)S(1)}, u32[]{:S(2)}, u32[]{:S(2)}) async-start(bf16[64,16,128]{2,1,0:T(8,128)(2,1)} %bitcast.7), calls=%async_computation.1 | async-start | bytes 524288 | tf_op jit(solution)/shard_map/all_to_all | solution.py:559
  42.6 0.1 bitcast_dynamic-update-slice_fusion.2
  42.7 0.1 bitcast_dynamic-update-slice_fusion.1
  42.8 2.5 %collective-permute-start = (bf16[8,144,128]{2,1,0:T(8,128)(2,1)S(1)}, bf16[8,144,128]{2,1,0:T(8,128)(2,1)S(1)}, u32[]{:S(2)}, u32[]{:S(2)}) collective-permute-start(bf16[8,144,128]{2,1,0:T(8,128)(2,1)S(1)} %all-to-all-done.arrived.own), channel_id=1, source_target_pairs={{0,8},{8,0},{16,24},{24,16},{32,40},{40,32},{48,56},{56,48},{64,72... | collective-permute-start | bytes 884744 | tf_op jit(solution)/shard_map/ppermute | solution.py:560
  45.3 0.1 bitcast_dynamic-update-slice_fusion
  45.4 0.1 fusion.1.refs_1_
  45.5 0.8 collective-permute-done.other
  46.3 0.3 weights.1
  46.7 0.0 copy-start.16
  46.7 7.9 %all-to-all-done.1.refs_0_ = bf16[64,16,128]{2,1,0:T(8,128)(2,1)S(1)} async-done(((bf16[64,16,128]{2,1,0:T(8,128)(2,1)}), bf16[64,16,128]{2,1,0:T(8,128)(2,1)S(1)}, u32[]{:S(2)}, u32[]{:S(2)}) %all-to-all-start.1) | async-done | bytes 262176 | tf_op jit(solution)/shard_map/all_to_all | solution.py:559
  54.6 0.1 broadcast_in_dim.2.refs_2_
  54.7 0.0 copy-done.16
  54.7 0.0 copy-start.12
  54.7 1.0 %copy-done.12 = bf16[1024,256]{1,0:T(8,128)(2,1)S(1)} copy-done((bf16[1024,256]{1,0:T(8,128)(2,1)S(1)}, bf16[1024,256]{1,0:T(8,128)(2,1)}, u32[]{:S(2)}) %copy-start.12) | copy-done | bytes 524312
  55.7 0.0 copy-start.13
  55.7 1.0 %copy-done.13 = bf16[1024,256]{1,0:T(8,128)(2,1)S(1)} copy-done((bf16[1024,256]{1,0:T(8,128)(2,1)S(1)}, bf16[1024,256]{1,0:T(8,128)(2,1)}, u32[]{:S(2)}) %copy-start.13) | copy-done | bytes 524312
  56.8 0.0 copy-start.14
  56.8 1.0 %copy-done.14 = bf16[256,1024]{1,0:T(8,128)(2,1)S(1)} copy-done((bf16[256,1024]{1,0:T(8,128)(2,1)S(1)}, bf16[256,1024]{1,0:T(8,128)(2,1)}, u32[]{:S(2)}) %copy-start.14) | copy-done | bytes 524312
  57.8 0.0 copy-start.15
  57.8 1.0 %copy-done.15 = bf16[256,1024]{1,0:T(8,128)(2,1)S(1)} copy-done((bf16[256,1024]{1,0:T(8,128)(2,1)S(1)}, bf16[256,1024]{1,0:T(8,128)(2,1)}, u32[]{:S(2)}) %copy-start.15) | copy-done | bytes 524312
  58.8 0.0 copy-start.1
  58.8 0.0 copy-start.3
  58.8 13.6 %cycle.1 = bf16[1024,128]{1,0:T(8,128)(2,1)} custom-call(bf16[64,16,128]{2,1,0:T(8,128)(2,1)S(1)} %all-to-all-done.1.refs_0_, f32[6,72,256]{2,1,0:T(8,128)S(1)} %fusion.1.refs_1_, f32[72,256]{1,0:T(8,128)S(1)} %broadcast_in_dim.2.refs_2_, bf16[80,768]{1,0:T(8,128)(2,1)S(1)} %get-tuple-element.9.refs_3_, bf16[768,128]{1,0:T(8,128)(2,1)S(1)} %get-tuple-element.10.refs_4_, ...), custom_call_target="tpu_custom_call" | custom-call | flops 8000000000 | bytes 4000000 | tf_op jit(solution)/shard_map/cycle/pallas_call | solution.py:462
  72.4 0.0 copy-start.5
  72.5 9.0 %all-to-all-start.2 = ((bf16[512,2,128]{2,1,0:T(2,128)(2,1)}), bf16[512,2,128]{2,1,0:T(2,128)(2,1)S(1)}, u32[]{:S(2)}, u32[]{:S(2)}) async-start(bf16[512,2,128]{2,1,0:T(2,128)(2,1)} %bitcast.14), calls=%async_computation.2 | async-start | bytes 524288 | tf_op jit(solution)/shard_map/all_to_all | solution.py:569
  81.5 17.0 %all-to-all-done.2 = bf16[512,2,128]{2,1,0:T(2,128)(2,1)S(1)} async-done(((bf16[512,2,128]{2,1,0:T(2,128)(2,1)}), bf16[512,2,128]{2,1,0:T(2,128)(2,1)S(1)}, u32[]{:S(2)}, u32[]{:S(2)}) %all-to-all-start.2) | async-done | bytes 262176 | tf_op jit(solution)/shard_map/all_to_all | solution.py:569
  98.5 0.0 copy-done.1
  98.5 0.0 copy-done.3
  98.5 0.0 copy-done.5
  98.5 1.4 %analysis.1 = f32[69,2,1,384]{3,2,1,0:T(1,128)} custom-call(s32[1]{0:T(128)} %bitcast.parity, bf16[1024,128]{1,0:T(8,128)(2,1)S(1)} %bitcast.28, f32[69,2,1,384]{3,2,1,0:T(1,128)S(1)} %copy-done.5, f32[69,1,384]{2,1,0:T(1,128)S(1)} %copy-done.6, bf16[2,512,384]{2,1,0:T(8,128)(2,1)S(1)} %copy-done.1, bf16[2,512,384]{2,1,0:T(8,128)(2,1)S(1)} %copy-done.3), custom_call_target="tpu_custom_call" | custom-call | flops 400000000 | bytes 2000000 | tf_op jit(solution)/shard_map/analysis/pallas_call | solution.py:505
  (6 shorter events, 0.1 us)
Async XLA Ops:
  0.0 0.7 copy-start.18
  0.0 1.5 %copy-start.6 = (f32[69,1,384]{2,1,0:T(1,128)S(1)}, f32[69,1,384]{2,1,0:T(1,128)}, u32[]{:S(2)}) copy-start(f32[69,1,384]{2,1,0:T(1,128)} %sigma.1) | copy-start | bytes 317956
  1.5 1.1 %copy-start = (bf16[2,512,384]{2,1,0:T(8,128)(2,1)S(1)}, bf16[2,512,384]{2,1,0:T(8,128)(2,1)}, u32[]{:S(2)}) copy-start(bf16[2,512,384]{2,1,0:T(8,128)(2,1)} %constant.45.clone.high_hbm.table_high) | copy-start | bytes 2359300
  2.6 1.1 %copy-start.2 = (bf16[2,512,384]{2,1,0:T(8,128)(2,1)S(1)}, bf16[2,512,384]{2,1,0:T(8,128)(2,1)}, u32[]{:S(2)}) copy-start(bf16[2,512,384]{2,1,0:T(8,128)(2,1)} %constant.46.clone.low_hbm.table_low) | copy-start | bytes 2359300
  3.7 0.9 copy-start.4
  7.0 11.0 %copy-start.17 = (f32[69,1,1440]{2,1,0:T(1,128)S(1)}, f32[69,1,1440]{2,1,0:T(1,128)}, u32[]{:S(2)}) copy-start(f32[69,1,1440]{2,1,0:T(1,128)} %param.20) | copy-start | bytes 1192324
  7.0 22.2 %all-to-all-start = ((bf16[8,144,128]{2,1,0:T(8,128)(2,1)}), bf16[8,144,128]{2,1,0:T(8,128)(2,1)S(1)}, u32[]{:S(2)}, u32[]{:S(2)}) async-start(bf16[8,144,128]{2,1,0:T(8,128)(2,1)} %synthesis.1), calls=%async_computation | async-start | bytes 589824 | tf_op jit(solution)/shard_map/all_to_all | solution.py:551
  18.0 0.7 copy-start.19
  18.1 0.7 copy-start.9
  18.1 0.7 copy-start.10
  18.1 0.7 copy-start.11
  18.7 0.7 copy-start.8
  18.7 0.7 copy-start.7
  30.1 24.5 %all-to-all-start.1 = ((bf16[64,16,128]{2,1,0:T(8,128)(2,1)}), bf16[64,16,128]{2,1,0:T(8,128)(2,1)S(1)}, u32[]{:S(2)}, u32[]{:S(2)}) async-start(bf16[64,16,128]{2,1,0:T(8,128)(2,1)} %bitcast.7), calls=%async_computation.1 | async-start | bytes 524288 | tf_op jit(solution)/shard_map/all_to_all | solution.py:559
  42.8 3.6 %collective-permute-start = (bf16[8,144,128]{2,1,0:T(8,128)(2,1)S(1)}, bf16[8,144,128]{2,1,0:T(8,128)(2,1)S(1)}, u32[]{:S(2)}, u32[]{:S(2)}) collective-permute-start(bf16[8,144,128]{2,1,0:T(8,128)(2,1)S(1)} %all-to-all-done.arrived.own), channel_id=1, source_target_pairs={{0,8},{8,0},{16,24},{24,16},{32,40},{40,32},{48,56},{56,48},{64,72... | collective-permute-start | bytes 884744 | tf_op jit(solution)/shard_map/ppermute | solution.py:560
  46.7 8.0 %copy-start.16 = (f32[16,512]{1,0:T(8,128)S(1)}, f32[16,512]{1,0:T(8,128)}, u32[]{:S(2)}) copy-start(f32[16,512]{1,0:T(8,128)} %constant.47.clone.refs_7_) | copy-start | bytes 98308
  54.7 1.0 %copy-start.12 = (bf16[1024,256]{1,0:T(8,128)(2,1)S(1)}, bf16[1024,256]{1,0:T(8,128)(2,1)}, u32[]{:S(2)}) copy-start(bf16[1024,256]{1,0:T(8,128)(2,1)} %constant.48.clone.refs_8_) | copy-start | bytes 1572868
  55.7 1.0 %copy-start.13 = (bf16[1024,256]{1,0:T(8,128)(2,1)S(1)}, bf16[1024,256]{1,0:T(8,128)(2,1)}, u32[]{:S(2)}) copy-start(bf16[1024,256]{1,0:T(8,128)(2,1)} %constant.49.clone.refs_9_) | copy-start | bytes 1572868
  56.8 1.0 %copy-start.14 = (bf16[256,1024]{1,0:T(8,128)(2,1)S(1)}, bf16[256,1024]{1,0:T(8,128)(2,1)}, u32[]{:S(2)}) copy-start(bf16[256,1024]{1,0:T(8,128)(2,1)} %constant.50.clone.refs_10_) | copy-start | bytes 1572868
  57.8 1.0 %copy-start.15 = (bf16[256,1024]{1,0:T(8,128)(2,1)S(1)}, bf16[256,1024]{1,0:T(8,128)(2,1)}, u32[]{:S(2)}) copy-start(bf16[256,1024]{1,0:T(8,128)(2,1)} %constant.51.clone.refs_11_) | copy-start | bytes 1572868
  58.8 39.6 %copy-start.1 = (bf16[2,512,384]{2,1,0:T(8,128)(2,1)S(1)}, bf16[2,512,384]{2,1,0:T(8,128)(2,1)}, u32[]{:S(2)}) copy-start(bf16[2,512,384]{2,1,0:T(8,128)(2,1)} %constant.45.clone.high_hbm.table_high) | copy-start | bytes 2359300
  58.8 39.6 %copy-start.3 = (bf16[2,512,384]{2,1,0:T(8,128)(2,1)S(1)}, bf16[2,512,384]{2,1,0:T(8,128)(2,1)}, u32[]{:S(2)}) copy-start(bf16[2,512,384]{2,1,0:T(8,128)(2,1)} %constant.46.clone.low_hbm.table_low) | copy-start | bytes 2359300
  72.4 26.1 %copy-start.5 = (f32[69,2,1,384]{3,2,1,0:T(1,128)S(1)}, f32[69,2,1,384]{3,2,1,0:T(1,128)}, u32[]{:S(2)}) copy-start(f32[69,2,1,384]{3,2,1,0:T(1,128)} %control.1) | copy-start | bytes 635908
  72.5 26.0 %all-to-all-start.2 = ((bf16[512,2,128]{2,1,0:T(2,128)(2,1)}), bf16[512,2,128]{2,1,0:T(2,128)(2,1)S(1)}, u32[]{:S(2)}, u32[]{:S(2)}) async-start(bf16[512,2,128]{2,1,0:T(2,128)(2,1)} %bitcast.14), calls=%async_computation.2 | async-start | bytes 524288 | tf_op jit(solution)/shard_map/all_to_all | solution.py:569

commit v3 on v2

--- a/solution.py
+++ b/solution.py
@@ -92,12 +92,15 @@
     sigma_hbm,
     high_hbm,
     low_hbm,
-    shard,
+    w_in_hbm,
+    w_out_hbm,
     out,
     control,
     sigma,
     table_high,
     table_low,
+    w_in,
+    w_out,
     coef,
     modes,
     arrivals,
@@ -111,6 +114,8 @@
                 (sigma_hbm, sigma),
                 (high_hbm.at[parity], table_high),
                 (low_hbm.at[parity], table_low),
+                (w_in_hbm, w_in),
+                (w_out_hbm, w_out),
             )
         )
     ]
@@ -128,12 +133,14 @@
     tail = channels - (LANES - ROWS)
     coef[LANES + REST_LANE : LANES + REST_LANE + tail, :] = second[LANES - ROWS :]
     parts = split(coef[...])
-    copies[2].wait()
-    copies[3].wait()
+    for copy in copies[2:]:
+        copy.wait()
     whole = dot3((table_high[...], table_low[...]), parts, NT)
     modes[0] = whole[:, 0:LANES]
     modes[1] = whole[:, LANES:]
-    rows = shard[...].astype(F32)
+    even = lax.rem(lax.axis_index("band"), 2) == 0
+    rows = jnp.where(even, w_in[...].astype(F32), w_out[...].astype(F32))
+    rows = jnp.pad(rows, ((0, 80 - channels), (0, LANES - rows.shape[1])))
     for dest in range(TPS):
         out[dest, 0:BANDS, :] = modes[0, pl.ds(dest, BANDS, stride=TPS), :].astype(BF16)
         rest = modes[1, pl.ds(dest, BANDS, stride=TPS), :]
@@ -141,30 +148,36 @@
         out[dest, 2 * BANDS : SEND_ROWS, :] = rows[BANDS:].astype(BF16)
 
 
+def in_hbm(*arrays):
+    return tuple(pltpu.with_memory_space_constraint(jnp.asarray(a), pltpu.HBM) for a in arrays)
+
+
 IN_VMEM = pl.BlockSpec(memory_space=pltpu.VMEM)
 IN_HBM = pl.BlockSpec(memory_space=pltpu.HBM)
 
 
-def synthesis(control, sigma, shard, table):
+def synthesis(control, sigma, w_in, w_out_t, table):
     lat_count, wave_count = table[0].shape[1:]
     return pl.pallas_call(
         synthesis_kernel,
         out_shape=jax.ShapeDtypeStruct((TPS, SEND_ROWS, LANES), BF16),
-        in_specs=[IN_HBM] * 4 + [IN_VMEM],
+        in_specs=[IN_HBM] * 6,
         out_specs=IN_VMEM,
         scratch_shapes=[
             pltpu.VMEM(control.shape, F32),
             pltpu.VMEM(sigma.shape, F32),
             pltpu.VMEM((lat_count, wave_count), BF16),
             pltpu.VMEM((lat_count, wave_count), BF16),
+            pltpu.VMEM(w_in.shape, BF16),
+            pltpu.VMEM(w_in.shape, BF16),
             pltpu.VMEM((2 * LANES, wave_count), F32),
             pltpu.VMEM((2, lat_count, LANES), F32),
-            pltpu.SemaphoreType.DMA((4,)),
+            pltpu.SemaphoreType.DMA((6,)),
         ],
         cost_estimate=pl.CostEstimate(flops=400_000_000, bytes_accessed=2_000_000, transcendentals=0),
         compiler_params=pltpu.CompilerParams(vmem_limit_bytes=12 * MIB),
         name="synthesis",
-    )(control, sigma, *table, shard)
+    )(*in_hbm(control, sigma, *table, w_in, w_out_t))
 
 
 def pack_kernel(band, cell, value, weight, offset, out):
@@ -230,7 +243,18 @@
     )(arrived, obs)
 
 
-def weights_kernel(own, other, in_rows, in_columns, out_rows, out_columns):
+def prepare_kernel(own, other, *refs):
+    sources, (in_rows, in_columns, out_rows, out_columns, *targets), (arrivals,) = (
+        refs[:1],
+        refs[1:6],
+        refs[6:],
+    )
+    copies = [
+        pltpu.make_async_copy(source, target, arrivals.at[i])
+        for i, (source, target) in enumerate(zip(sources, targets))
+    ]
+    for copy in copies:
+        copy.start()
     even = lax.rem(lax.axis_index("band"), 2) == 0
     for columns, rows, first in ((in_columns, in_rows, True), (out_columns, out_rows, False)):
         pieces = []
@@ -243,22 +267,28 @@
         upright = jnp.concatenate(pieces, axis=0)
         columns[...] = upright.astype(BF16)
         rows[...] = upright.T[0:80].astype(BF16)
-
-
-def gather_weights(own, other):
+    for copy in copies:
+        copy.wait()
+
+
+def prepare(own, other, tables):
     hidden = TPS * 96
     return pl.pallas_call(
-        weights_kernel,
+        prepare_kernel,
         out_shape=(
             jax.ShapeDtypeStruct((80, hidden), BF16),
             jax.ShapeDtypeStruct((hidden, LANES), BF16),
             jax.ShapeDtypeStruct((80, hidden), BF16),
             jax.ShapeDtypeStruct((hidden, LANES), BF16),
+            *(jax.ShapeDtypeStruct(table.shape, table.dtype) for table in tables),
         ),
-        cost_estimate=pl.CostEstimate(flops=1_000_000, bytes_accessed=1_500_000, transcendentals=0),
+        in_specs=[IN_VMEM] * 2 + [IN_HBM],
+        out_specs=[IN_VMEM] * 5,
+        scratch_shapes=[pltpu.SemaphoreType.DMA((1,))],
+        cost_estimate=pl.CostEstimate(flops=1_000_000, bytes_accessed=5_000_000, transcendentals=0),
         compiler_params=pltpu.CompilerParams(vmem_limit_bytes=8 * MIB),
-        name="weights",
-    )(own, other)
+        name="prepare",
+    )(own, other, *in_hbm(*tables))
 
 
 GELU_SCALE = math.sqrt(2.0 / math.pi)
@@ -303,15 +333,10 @@
 ):
     orders = turns.shape[1]
     copies = [
-        pltpu.make_async_copy(source, target, arrivals.at[i])
-        for i, (source, target) in enumerate(
-            (
-                (table_high_hbm, table_high),
-                (table_low_hbm, table_low),
-                (wide_high_hbm, wide_high),
-                (wide_low_hbm, wide_low),
-            )
-        )
+        pltpu.make_async_copy(table_high_hbm, table_high, arrivals.at[0]),
+        pltpu.make_async_copy(table_low_hbm, table_low, arrivals.at[1]),
+        pltpu.make_async_copy(wide_high_hbm, wide_high, arrivals.at[2]),
+        pltpu.make_async_copy(wide_low_hbm, wide_low, arrivals.at[3]),
     ]
     for copy in copies:
         copy.start()
@@ -333,8 +358,8 @@
         turned_sin = sin_part * turn_cos - cos_part * turn_sin
         turned.append(jnp.concatenate([turned_cos, turned_sin], axis=1))
     turned = split(jnp.concatenate(turned, axis=0))
-    copies[0].wait()
-    copies[1].wait()
+    for copy in copies[:2]:
+        copy.wait()
     state[...] = prior[...].reshape(BLOCKS * ROWS, WIDTH) + dot3(
         turned, (table_high[...], table_low[...])
     )
@@ -434,8 +459,8 @@
         along = jnp.sum(scaled * field, axis=0, keepdims=True) * (1.0 / channels)
         costate.append(force + scaled * inverse - field * (along * inverse * inverse * inverse))
     costate = split(jnp.concatenate(costate, axis=0))
-    copies[2].wait()
-    copies[3].wait()
+    for copy in copies[2:]:
+        copy.wait()
     blocks = dot3(costate, (wide_high[...], wide_low[...]))
     grad_cos = jnp.zeros((ROWS, orders), F32)
     grad_sin = jnp.zeros((ROWS, orders), F32)
@@ -456,9 +481,9 @@
     out[...] = paired[...].astype(BF16)
 
 
-def run_cycle(channels, arrived, prior, gains, weights, table, turns):
-    orders = turns.shape[1]
-    hidden = weights[1].shape[0]
+def run_cycle(channels, arrived, prior, gains, prepared, table):
+    orders = prepared[4].shape[1]
+    hidden = prepared[1].shape[0]
     return pl.pallas_call(
         lambda *refs: cycle_kernel(channels, *refs),
         out_shape=jax.ShapeDtypeStruct((2 * orders, LANES), BF16),
@@ -479,7 +504,7 @@
             flops=8_000_000_000, bytes_accessed=4_000_000, transcendentals=1_200_000
         ),
         name="cycle",
-    )(arrived, prior, gains, *weights, turns, *table)
+    )(arrived, prior, gains, *prepared, *in_hbm(*table))
 
 
 def analysis_kernel(parity, arrived, control, sigma, table_high, table_low, out, rows):
@@ -544,10 +569,7 @@
     zonal = zonal_np(lat_count, lon_count)
     turns = turn_np(lat_count, lon_count)
     parity = (lax.axis_index("tp") % 2).astype(jnp.int32).reshape(1)
-    even = lax.axis_index("band") % 2 == 0
-    pads = ((0, 80 - channels), (0, LANES - w_in.shape[1]))
-    shard = jnp.pad(jnp.where(even, w_in, w_out.T), pads)
-    send = synthesis(control, spec_sigma, shard, legendre)
+    send = synthesis(control, spec_sigma, w_in, w_out.T, legendre)
     got = lax.all_to_all(send, "tp", split_axis=0, concat_axis=0, tiled=True)
     obs = pack_obs(
         *(
@@ -558,14 +580,14 @@
     send = regroup(got, obs).reshape(BANDS, 16, LANES)
     arrived = lax.all_to_all(send, "band", split_axis=0, concat_axis=0, tiled=True)
     other = lax.ppermute(got, "band", [(i, i ^ 1) for i in range(BANDS)])
-    weights = gather_weights(got, other)
+    prepared = prepare(got, other, (turns,))
     prior = jnp.pad(prior_mean_field[:, 0, :], ((0, ROWS - channels), (0, 0)))
     prior = jnp.concatenate([prior, prior[:, : WIDTH - STRIDE]], axis=1)
     prior = jnp.stack([prior[:, a * STRIDE : a * STRIDE + WIDTH] for a in range(BLOCKS)])
     gains = jnp.broadcast_to(
         jnp.pad(magnitude_factor, (0, ROWS - channels))[:, None], (ROWS, WIDTH)
     )
-    modes = run_cycle(channels, arrived, prior, gains, weights, zonal, turns)
+    modes = run_cycle(channels, arrived, prior, gains, prepared, zonal)
     modes = lax.all_to_all(
         modes.reshape(lat_count, 2, LANES),
         ("band", "tp"),

time: 101 us -> 92.4 us (0.915)
  local copies, waits for them, and re-layouts: 9.88 us -> 1.79 us
  Pallas kernels: 19.6 us -> 21.1 us
    unnamed x46 -> x28, local copies, waits for them, and re-layouts: 9.75 us -> 1.68 us
  transfers between devices with their start and end apart: 4 -> 4, of which waited for: 4 -> 4; matrix products, arithmetic and copies ran while one was open for 1% -> 1% of each run, Pallas kernels for 1% -> 2%
where the time goes in v3:
time: 92.4 us; the launch traced here: 91.9 us
  starting transfers between devices  34.9 us (38%)
  waiting for transfers between devices  33.9 us (37%)
  Pallas kernels  21.1 us (23%)
  local copies, waits for them, and re-layouts  1.79 us (2%)
    all_to_all x1, waiting for transfers between devices, shards(): lax.all_to_all(modes.reshape(lat_count, 2, LANES), ('band', 'tp'), split_...  17 us
    pallas_call x1, Pallas kernels, run_cycle(): pl.pallas_call(lambda *refs: cycle_kernel(channels, *refs), out_shape=jax...  14.2 us
    all_to_all x1, starting transfers between devices, shards(): lax.all_to_all(send, 'band', split_axis=0, concat_axis=0, tiled=True)  12.5 us
    all_to_all x1, starting transfers between devices, shards(): got = lax.all_to_all(send, 'tp', split_axis=0, concat_axis=0, tiled=True)  11 us
    all_to_all x1, starting transfers between devices, shards(): lax.all_to_all(modes.reshape(lat_count, 2, LANES), ('band', 'tp'), split_...  8.82 us
    all_to_all x1, waiting for transfers between devices, shards(): got = lax.all_to_all(send, 'tp', split_axis=0, concat_axis=0, tiled=True)  8.55 us
    all_to_all x1, waiting for transfers between devices, shards(): lax.all_to_all(send, 'band', split_axis=0, concat_axis=0, tiled=True)  7.5 us
    pallas_call x1, Pallas kernels, synthesis(): pl.pallas_call(synthesis_kernel, out_shape=jax.ShapeDtypeStruct((TPS, SEN...  2.67 us
  transfers between devices with their start and end apart: 4, of which 4 were waited for; matrix products, arithmetic and copies ran while one was open for 1% of the time, Pallas kernels for 2%

profile of v3, /device:TPU:1, one launch (start us, length us, event | category | flops | bytes accessed | tf_op | source)
XLA Modules:
  0.0 91.9 jit_solution(8080666874440433962)
XLA Ops:
  0.0 2.7 %synthesis.1 = bf16[8,144,128]{2,1,0:T(8,128)(2,1)} custom-call(f32[69,2,1,384]{3,2,1,0:T(1,128)} %control.1, f32[69,1,384]{2,1,0:T(1,128)} %sigma.1, bf16[2,512,384]{2,1,0:T(8,128)(2,1)} %constant.34.clone.high_hbm.table_high, bf16[2,512,384]{2,1,0:T(8,128)(2,1)} %constant.35.clone.low_hbm.table_low, bf16[69,96]{1,0:T(8,128)(2,1)} %w_in_hbm.1, ...), custom_call_target="tpu_custom_call" | custom-call | flops 400000000 | bytes 2000000 | tf_op jit(solution)/shard_map/synthesis/pallas_call | solution.py:161
  2.7 0.0 copy-start.9
  2.7 11.0 %all-to-all-start = ((bf16[8,144,128]{2,1,0:T(8,128)(2,1)}), bf16[8,144,128]{2,1,0:T(8,128)(2,1)S(1)}, u32[]{:S(2)}, u32[]{:S(2)}) async-start(bf16[8,144,128]{2,1,0:T(8,128)(2,1)} %synthesis.1), calls=%async_computation | async-start | bytes 589824 | tf_op jit(solution)/shard_map/all_to_all | solution.py:573
  13.7 0.0 copy-done.9
  13.7 0.0 copy-start.10
  13.8 0.0 copy-start.6
  13.8 0.0 copy-start.7
  13.8 0.0 copy-start.8
  13.8 0.6 copy-done.10
  14.4 0.0 copy-start.5
  14.4 0.0 copy-start.4
  14.4 0.0 copy-done.6
  14.4 0.0 copy-done.7
  14.5 0.0 copy-done.8
  14.5 0.6 copy-done.5
  15.1 0.0 copy-done.4
  15.1 1.1 %pack_obs.1.obs = f32[64,1024]{1,0:T(8,128)S(1)} custom-call(s32[8,128]{1,0:T(8,128)S(1)} %bitcast.28, s32[8,128]{1,0:T(8,128)S(1)} %bitcast.29, f32[8,128]{1,0:T(8,128)S(1)} %bitcast.30, f32[8,128]{1,0:T(8,128)S(1)} %bitcast.31, f32[8,128]{1,0:T(8,128)S(1)} %bitcast.32), custom_call_target="tpu_custom_call" | custom-call | flops 200000000 | bytes 300000 | tf_op jit(solution)/shard_map/pack_obs/pallas_call | solution.py:216
  16.2 0.1 bitcast_dynamic-update-slice_fusion.3
  16.3 8.6 %all-to-all-done.arrived.own = bf16[8,144,128]{2,1,0:T(8,128)(2,1)S(1)} async-done(((bf16[8,144,128]{2,1,0:T(8,128)(2,1)}), bf16[8,144,128]{2,1,0:T(8,128)(2,1)S(1)}, u32[]{:S(2)}, u32[]{:S(2)}) %all-to-all-start) | async-done | bytes 294944 | tf_op jit(solution)/shard_map/all_to_all | solution.py:573
  24.9 1.0 %regroup.1 = bf16[1024,128]{1,0:T(8,128)(2,1)} custom-call(bf16[8,144,128]{2,1,0:T(8,128)(2,1)S(1)} %all-to-all-done.arrived.own, f32[64,1024]{1,0:T(8,128)S(1)} %pack_obs.1.obs), custom_call_target="tpu_custom_call" | custom-call | flops 300000 | bytes 800000 | tf_op jit(solution)/shard_map/regroup/pallas_call | solution.py:236
  25.8 12.5 %all-to-all-start.1 = ((bf16[64,16,128]{2,1,0:T(8,128)(2,1)}), bf16[64,16,128]{2,1,0:T(8,128)(2,1)S(1)}, u32[]{:S(2)}, u32[]{:S(2)}) async-start(bf16[64,16,128]{2,1,0:T(8,128)(2,1)} %bitcast.7), calls=%async_computation.1 | async-start | bytes 524288 | tf_op jit(solution)/shard_map/all_to_all | solution.py:581
  38.3 0.1 bitcast_dynamic-update-slice_fusion.2
  38.4 0.1 bitcast_dynamic-update-slice_fusion.1
  38.5 2.5 %collective-permute-start = (bf16[8,144,128]{2,1,0:T(8,128)(2,1)S(1)}, bf16[8,144,128]{2,1,0:T(8,128)(2,1)S(1)}, u32[]{:S(2)}, u32[]{:S(2)}) collective-permute-start(bf16[8,144,128]{2,1,0:T(8,128)(2,1)S(1)} %all-to-all-done.arrived.own), channel_id=1, source_target_pairs={{0,8},{8,0},{16,24},{24,16},{32,40},{40,32},{48,56},{56,48},{64,72... | collective-permute-start | bytes 884744 | tf_op jit(solution)/shard_map/ppermute | solution.py:582
  41.0 0.1 bitcast_dynamic-update-slice_fusion
  41.1 0.1 fusion.1.refs_1_
  41.2 0.8 collective-permute-done.other
  42.0 0.8 prepare.1
  42.8 7.5 %all-to-all-done.1.refs_0_ = bf16[64,16,128]{2,1,0:T(8,128)(2,1)S(1)} async-done(((bf16[64,16,128]{2,1,0:T(8,128)(2,1)}), bf16[64,16,128]{2,1,0:T(8,128)(2,1)S(1)}, u32[]{:S(2)}, u32[]{:S(2)}) %all-to-all-start.1) | async-done | bytes 262176 | tf_op jit(solution)/shard_map/all_to_all | solution.py:581
  50.3 0.1 broadcast_in_dim.2.refs_2_
  50.4 0.0 copy-start
  50.4 0.0 copy-start.1
  50.4 14.2 %cycle.1 = bf16[1024,128]{1,0:T(8,128)(2,1)} custom-call(bf16[64,16,128]{2,1,0:T(8,128)(2,1)S(1)} %all-to-all-done.1.refs_0_, f32[6,72,256]{2,1,0:T(8,128)S(1)} %fusion.1.refs_1_, f32[72,256]{1,0:T(8,128)S(1)} %broadcast_in_dim.2.refs_2_, bf16[80,768]{1,0:T(8,128)(2,1)S(1)} %get-tuple-element.10.refs_3_, bf16[768,128]{1,0:T(8,128)(2,1)S(1)} %get-tuple-element.11.refs_4_, ...), custom_call_target="tpu_custom_call" | custom-call | flops 8000000000 | bytes 4000000 | tf_op jit(solution)/shard_map/cycle/pallas_call | solution.py:487
  64.6 0.0 copy-start.2
  64.6 0.0 copy-start.3
  64.6 8.8 %all-to-all-start.2 = ((bf16[512,2,128]{2,1,0:T(2,128)(2,1)}), bf16[512,2,128]{2,1,0:T(2,128)(2,1)S(1)}, u32[]{:S(2)}, u32[]{:S(2)}) async-start(bf16[512,2,128]{2,1,0:T(2,128)(2,1)} %bitcast.14), calls=%async_computation.2 | async-start | bytes 524288 | tf_op jit(solution)/shard_map/all_to_all | solution.py:591
  73.4 17.0 %all-to-all-done.2 = bf16[512,2,128]{2,1,0:T(2,128)(2,1)S(1)} async-done(((bf16[512,2,128]{2,1,0:T(2,128)(2,1)}), bf16[512,2,128]{2,1,0:T(2,128)(2,1)S(1)}, u32[]{:S(2)}, u32[]{:S(2)}) %all-to-all-start.2) | async-done | bytes 262176 | tf_op jit(solution)/shard_map/all_to_all | solution.py:591
  90.5 0.0 copy-done
  90.5 0.0 copy-done.1
  90.5 0.0 copy-done.2
  90.5 0.0 copy-done.3
  90.5 1.4 %analysis.1 = f32[69,2,1,384]{3,2,1,0:T(1,128)} custom-call(s32[1]{0:T(128)} %bitcast.parity, bf16[1024,128]{1,0:T(8,128)(2,1)S(1)} %bitcast.27, f32[69,2,1,384]{3,2,1,0:T(1,128)S(1)} %copy-done.2, f32[69,1,384]{2,1,0:T(1,128)S(1)} %copy-done.3, bf16[2,512,384]{2,1,0:T(8,128)(2,1)S(1)} %copy-done, bf16[2,512,384]{2,1,0:T(8,128)(2,1)S(1)} %copy-done.1), custom_call_target="tpu_custom_call" | custom-call | flops 400000000 | bytes 2000000 | tf_op jit(solution)/shard_map/analysis/pallas_call | solution.py:530
  (5 shorter events, 0.1 us)
Async XLA Ops:
  2.7 11.0 %copy-start.9 = (f32[69,1,1440]{2,1,0:T(1,128)S(1)}, f32[69,1,1440]{2,1,0:T(1,128)}, u32[]{:S(2)}) copy-start(f32[69,1,1440]{2,1,0:T(1,128)} %param.20) | copy-start | bytes 1192324
  2.7 22.2 %all-to-all-start = ((bf16[8,144,128]{2,1,0:T(8,128)(2,1)}), bf16[8,144,128]{2,1,0:T(8,128)(2,1)S(1)}, u32[]{:S(2)}, u32[]{:S(2)}) async-start(bf16[8,144,128]{2,1,0:T(8,128)(2,1)} %synthesis.1), calls=%async_computation | async-start | bytes 589824 | tf_op jit(solution)/shard_map/all_to_all | solution.py:573
  13.7 0.7 copy-start.10
  13.8 0.7 copy-start.6
  13.8 0.7 copy-start.7
  13.8 0.7 copy-start.8
  14.4 0.7 copy-start.5
  14.4 0.7 copy-start.4
  25.8 24.5 %all-to-all-start.1 = ((bf16[64,16,128]{2,1,0:T(8,128)(2,1)}), bf16[64,16,128]{2,1,0:T(8,128)(2,1)S(1)}, u32[]{:S(2)}, u32[]{:S(2)}) async-start(bf16[64,16,128]{2,1,0:T(8,128)(2,1)} %bitcast.7), calls=%async_computation.1 | async-start | bytes 524288 | tf_op jit(solution)/shard_map/all_to_all | solution.py:581
  38.5 3.6 %collective-permute-start = (bf16[8,144,128]{2,1,0:T(8,128)(2,1)S(1)}, bf16[8,144,128]{2,1,0:T(8,128)(2,1)S(1)}, u32[]{:S(2)}, u32[]{:S(2)}) collective-permute-start(bf16[8,144,128]{2,1,0:T(8,128)(2,1)S(1)} %all-to-all-done.arrived.own), channel_id=1, source_target_pairs={{0,8},{8,0},{16,24},{24,16},{32,40},{40,32},{48,56},{56,48},{64,72... | collective-permute-start | bytes 884744 | tf_op jit(solution)/shard_map/ppermute | solution.py:582
  50.4 40.1 %copy-start = (bf16[2,512,384]{2,1,0:T(8,128)(2,1)S(1)}, bf16[2,512,384]{2,1,0:T(8,128)(2,1)}, u32[]{:S(2)}) copy-start(bf16[2,512,384]{2,1,0:T(8,128)(2,1)} %constant.34.clone.high_hbm.table_high) | copy-start | bytes 2359300
  50.4 40.1 %copy-start.1 = (bf16[2,512,384]{2,1,0:T(8,128)(2,1)S(1)}, bf16[2,512,384]{2,1,0:T(8,128)(2,1)}, u32[]{:S(2)}) copy-start(bf16[2,512,384]{2,1,0:T(8,128)(2,1)} %constant.35.clone.low_hbm.table_low) | copy-start | bytes 2359300
  64.6 25.9 %copy-start.2 = (f32[69,2,1,384]{3,2,1,0:T(1,128)S(1)}, f32[69,2,1,384]{3,2,1,0:T(1,128)}, u32[]{:S(2)}) copy-start(f32[69,2,1,384]{3,2,1,0:T(1,128)} %control.1) | copy-start | bytes 635908
  64.6 25.9 %copy-start.3 = (f32[69,1,384]{2,1,0:T(1,128)S(1)}, f32[69,1,384]{2,1,0:T(1,128)}, u32[]{:S(2)}) copy-start(f32[69,1,384]{2,1,0:T(1,128)} %sigma.1) | copy-start | bytes 317956
  64.6 25.8 %all-to-all-start.2 = ((bf16[512,2,128]{2,1,0:T(2,128)(2,1)}), bf16[512,2,128]{2,1,0:T(2,128)(2,1)S(1)}, u32[]{:S(2)}, u32[]{:S(2)}) async-start(bf16[512,2,128]{2,1,0:T(2,128)(2,1)} %bitcast.14), calls=%async_computation.2 | async-start | bytes 524288 | tf_op jit(solution)/shard_map/all_to_all | solution.py:591

commit v4 on v3

--- a/solution.py
+++ b/solution.py
@@ -14,6 +14,7 @@
 F32 = jnp.float32
 
 BLOCKS = 6
+PAIRS = BLOCKS // 2
 STRIDE = 240
 WIDTH = 256
 ROWS = 72
@@ -45,17 +46,23 @@
     return split_np(np.stack(tables))
 
 
+def even_odd_np(orders):
+    return np.concatenate([np.arange(0, orders, 2), np.arange(1, orders, 2)])
+
+
 def zonal_np(orders, lon_count):
-    phases = np.arange(orders)[:, None] * np.arange(WIDTH)[None, :] % lon_count
+    phases = even_odd_np(orders)[:, None] * np.arange(WIDTH)[None, :] % lon_count
     angles = phases * (2.0 * math.pi / lon_count)
-    high, low = split_np(np.concatenate([np.cos(angles), np.sin(angles)], axis=0))
+    halves = angles.reshape(2, 1, orders // 2, WIDTH)
+    parts = np.concatenate([np.cos(halves), np.sin(halves)], axis=1)
+    high, low = split_np(parts.reshape(2 * orders, WIDTH))
     return high, low, np.ascontiguousarray(high.T), np.ascontiguousarray(low.T)
 
 
 def turn_np(orders, lon_count):
-    phases = np.arange(BLOCKS)[:, None] * STRIDE * np.arange(orders)[None, :] % lon_count
+    phases = np.arange(PAIRS)[:, None] * STRIDE * even_odd_np(orders)[None, :] % lon_count
     angles = phases * (2.0 * math.pi / lon_count)
-    pad = np.zeros((8 - BLOCKS, orders))
+    pad = np.zeros((4 - PAIRS, orders))
     return np.concatenate([np.cos(angles), pad, np.sin(angles), pad]).astype(np.float32)
 
 
@@ -83,8 +90,9 @@
     return lax.broadcasted_iota(jnp.int32, shape, len(shape) - 1)
 
 
-SEND_ROWS = 144
+SEND_ROWS = 128
 REST_LANE = 96
+PIECE_LANE = 112
 
 
 def synthesis_kernel(
@@ -140,12 +148,21 @@
     modes[1] = whole[:, LANES:]
     even = lax.rem(lax.axis_index("band"), 2) == 0
     rows = jnp.where(even, w_in[...].astype(F32), w_out[...].astype(F32))
-    rows = jnp.pad(rows, ((0, 80 - channels), (0, LANES - rows.shape[1])))
+    rows = jnp.pad(rows, ((0, ROWS - channels), (0, LANES - rows.shape[1])))
+    lanes = lane_ids((8, LANES))
+    pieces = [
+        jnp.where(
+            lanes >= PIECE_LANE,
+            pltpu.roll(rows[BANDS:ROWS], PIECE_LANE - start, 1),
+            rows[start // 2 : start // 2 + 8],
+        )
+        for start in range(0, REST_LANE, 16)
+    ]
+    rows = jnp.concatenate([*pieces, rows[REST_LANE // 2 : BANDS]], axis=0)
     for dest in range(TPS):
         out[dest, 0:BANDS, :] = modes[0, pl.ds(dest, BANDS, stride=TPS), :].astype(BF16)
         rest = modes[1, pl.ds(dest, BANDS, stride=TPS), :]
-        out[dest, BANDS : 2 * BANDS, :] = (rest + rows[0:BANDS]).astype(BF16)
-        out[dest, 2 * BANDS : SEND_ROWS, :] = rows[BANDS:].astype(BF16)
+        out[dest, BANDS:SEND_ROWS, :] = (rest + rows).astype(BF16)
 
 
 def in_hbm(*arrays):
@@ -256,14 +273,21 @@
     for copy in copies:
         copy.start()
     even = lax.rem(lax.axis_index("band"), 2) == 0
+    lanes = lane_ids((8, LANES))
+    filler = jnp.zeros((LANES - ROWS, LANES), F32)
     for columns, rows, first in ((in_columns, in_rows, True), (out_columns, out_rows, False)):
         pieces = []
         for t in range(TPS):
             mine = own[t, BANDS:SEND_ROWS, :].astype(F32)
             theirs = other[t, BANDS:SEND_ROWS, :].astype(F32)
             piece = jnp.where(even == first, mine, theirs)
-            piece = jnp.concatenate([piece, jnp.zeros((LANES - 80, LANES), F32)], axis=0)
-            pieces.append(piece.T[0:96])
+            last = jnp.zeros((8, LANES), F32)
+            for start in range(0, REST_LANE, 16):
+                part = piece[start // 2 : start // 2 + 8]
+                part = pltpu.roll(part, LANES - PIECE_LANE + start, 1)
+                last = jnp.where((lanes >= start) & (lanes < start + 16), part, last)
+            piece = jnp.concatenate([piece, last, filler], axis=0)
+            pieces.append(piece.T[0:REST_LANE])
         upright = jnp.concatenate(pieces, axis=0)
         columns[...] = upright.astype(BF16)
         rows[...] = upright.T[0:80].astype(BF16)
@@ -342,8 +366,13 @@
         copy.start()
     slices = arrived[...].astype(F32)
     rest = slices[:, 8:16, :]
-    cos_sin = slices[:, 0:8, :].reshape(orders, LANES).T
-    tail = rest.reshape(orders, LANES).T
+    half = orders // 2
+    paired[0:orders, :] = slices[:, 0:8, :].reshape(orders, LANES)
+    paired[orders:, :] = rest.reshape(orders, LANES)
+    cos_sin = [paired[pl.ds(p, half, stride=2), :] for p in range(2)]
+    cos_sin = jnp.concatenate(cos_sin, axis=0).T
+    tail = [paired[pl.ds(orders + p, half, stride=2), :] for p in range(2)]
+    tail = jnp.concatenate(tail, axis=0).T
     cos_part = cos_sin[0:ROWS]
     sin_part = jnp.concatenate([cos_sin[ROWS:LANES], tail[0:16]], axis=0)
     pairs = rest.reshape(BANDS // 2, 2, FIELDS, LANES)
@@ -352,17 +381,26 @@
     obs[...] = jnp.where(lane_ids(near.shape) < SLOTS, near, pairs[:, 1])
 
     turned = []
-    for a in range(BLOCKS):
-        turn_cos, turn_sin = turns[a : a + 1, :], turns[8 + a : 9 + a, :]
+    for a in range(PAIRS):
+        turn_cos, turn_sin = turns[a : a + 1, :], turns[4 + a : 5 + a, :]
         turned_cos = cos_part * turn_cos + sin_part * turn_sin
         turned_sin = sin_part * turn_cos - cos_part * turn_sin
-        turned.append(jnp.concatenate([turned_cos, turned_sin], axis=1))
+        turned.append(
+            jnp.concatenate(
+                [turned_cos[:, :half], turned_sin[:, :half], turned_cos[:, half:], turned_sin[:, half:]],
+                axis=1,
+            )
+        )
     turned = split(jnp.concatenate(turned, axis=0))
     for copy in copies[:2]:
         copy.wait()
-    state[...] = prior[...].reshape(BLOCKS * ROWS, WIDTH) + dot3(
-        turned, (table_high[...], table_low[...])
-    )
+    sums = []
+    for p in range(2):
+        span = slice(p * orders, (p + 1) * orders)
+        part = (turned[0][:, span], turned[1][:, span])
+        sums.append(dot3(part, (table_high[span, :], table_low[span, :])))
+    field = jnp.concatenate([sums[0] + sums[1], sums[0] - sums[1]], axis=0)
+    state[...] = prior[...].reshape(BLOCKS * ROWS, WIDTH) + field
 
     forecast = []
     for a in range(BLOCKS):
@@ -372,9 +410,9 @@
         pre = dot(in_columns[:, 0:ROWS], unit)
         square = pre * pre
         inner = pre * (GELU_SCALE + (GELU_SCALE * GELU_CUBE) * square)
-        half = 0.5 + 0.5 * jnp.tanh(inner)
-        hidden = pre * half
-        slopes[a] = half + hidden * (1.0 - half) * (
+        gate = 0.5 + 0.5 * jnp.tanh(inner)
+        hidden = pre * gate
+        slopes[a] = gate + hidden * (1.0 - gate) * (
             2.0 * GELU_SCALE + (6.0 * GELU_SCALE * GELU_CUBE) * square
         )
         forecast.append(field + dot(out_rows[...], hidden.astype(BF16))[0:ROWS])
@@ -382,16 +420,17 @@
     forecast = jnp.concatenate(forecast, axis=0)
 
     per_chunk = OBS_CHUNK // LANES
+    chunks = obs.shape[0] // per_chunk
     low_ids = lax.broadcasted_iota(jnp.int32, (16, OBS_CHUNK), 0).astype(F32)
     near_ids = lax.broadcasted_iota(jnp.int32, (32, OBS_CHUNK), 0).astype(F32)
     none = jnp.zeros((16, OBS_CHUNK), BF16)
-    for chunk in range(obs.shape[0] // per_chunk):
+
+    def fields_of(chunk):
         fields = [obs[chunk * per_chunk + i] for i in range(per_chunk)]
-        fields = jnp.concatenate(fields, axis=1)
-        value = fields[0:1] + fields[1:2]
-        weight = fields[2:3] + fields[3:4]
-        offset = fields[4:5] + fields[5:6]
-        row = fields[6:7] + float(ROW_SHIFT)
+        return jnp.concatenate(fields, axis=1)
+
+    def choose(chunk):
+        row = fields_of(chunk)[6:7] + float(ROW_SHIFT)
         row_group = jnp.floor(row * (1.0 / 16.0))
         first = jnp.where(low_ids == row - 16.0 * row_group, 1.0, 0.0).astype(BF16)
         row_group = jnp.broadcast_to(row_group, (16, OBS_CHUNK)).astype(BF16)
@@ -402,9 +441,15 @@
             ],
             axis=0,
         )
+        chosen_all[:, chunk * OBS_CHUNK : (chunk + 1) * OBS_CHUNK] = chosen
+        return chosen
+
+    def observe(chunk, picked):
+        fields = fields_of(chunk)
         columns = slice(chunk * OBS_CHUNK, (chunk + 1) * OBS_CHUNK)
-        chosen_all[:, columns] = chosen
-        picked = dot(forecast, chosen)
+        value = fields[0:1] + fields[1:2]
+        weight = fields[2:3] + fields[3:4]
+        offset = fields[4:5] + fields[5:6]
         group = jnp.floor(fields[7:8] * (1.0 / 16.0))
         place = near_ids - (fields[7:8] - 16.0 * group)
         group8 = jnp.broadcast_to(group, (8, OBS_CHUNK))
@@ -439,6 +484,17 @@
                     piece = jnp.where(masks[g], part[0:16], piece)
                 pieces.append(piece)
             spread_all[i * WIDTH : (i + 1) * WIDTH, columns] = jnp.concatenate(pieces, axis=0)
+
+    chosen = choose(0)
+    picked = None
+    for chunk in range(chunks):
+        latest = dot(forecast, chosen)
+        if chunk + 1 < chunks:
+            chosen = choose(chunk + 1)
+        if chunk > 0:
+            observe(chunk - 1, picked)
+        picked = latest
+    observe(chunks - 1, picked)
     forcing = dot(spread_all[...], chosen_all[...], NT)
     forcing = (forcing[0:WIDTH] + forcing[WIDTH:]).T
 
@@ -458,26 +514,29 @@
         scaled = grad_unit * gains[...]
         along = jnp.sum(scaled * field, axis=0, keepdims=True) * (1.0 / channels)
         costate.append(force + scaled * inverse - field * (along * inverse * inverse * inverse))
-    costate = split(jnp.concatenate(costate, axis=0))
+    near = jnp.concatenate(costate[:PAIRS], axis=0)
+    far = jnp.concatenate(costate[PAIRS:], axis=0)
     for copy in copies[2:]:
         copy.wait()
-    blocks = dot3(costate, (wide_high[...], wide_low[...]))
-    grad_cos = jnp.zeros((ROWS, orders), F32)
-    grad_sin = jnp.zeros((ROWS, orders), F32)
-    for a in range(BLOCKS):
-        turn_cos, turn_sin = turns[a : a + 1, :], turns[8 + a : 9 + a, :]
-        block = blocks[a * ROWS : (a + 1) * ROWS]
-        block_cos, block_sin = block[:, 0:orders], block[:, orders:]
-        grad_cos = grad_cos + turn_cos * block_cos - turn_sin * block_sin
-        grad_sin = grad_sin + turn_sin * block_cos + turn_cos * block_sin
-
-    lanes = lane_ids((orders, LANES))
-    pad = jnp.zeros((LANES - ROWS, orders), F32)
-    for r, grad in ((0, grad_cos), (1, grad_sin)):
-        upright = jnp.concatenate([grad, pad], axis=0).T
-        high = upright.astype(BF16).astype(F32)
-        low = pltpu.roll(upright - high, channels, 1)
-        paired[pl.ds(r, orders, stride=2), :] = jnp.where(lanes < channels, high, low)
+    pad = jnp.zeros((LANES - ROWS, half), F32)
+    lanes = lane_ids((half, LANES))
+    for p, both in enumerate((near + far, near - far)):
+        span = slice(p * orders, (p + 1) * orders)
+        blocks = dot3(split(both), (wide_high[:, span], wide_low[:, span]))
+        grads = [jnp.zeros((ROWS, half), F32)] * 2
+        for a in range(PAIRS):
+            turn_cos = turns[a : a + 1, p * half : (p + 1) * half]
+            turn_sin = turns[4 + a : 5 + a, p * half : (p + 1) * half]
+            block = blocks[a * ROWS : (a + 1) * ROWS]
+            block_cos, block_sin = block[:, :half], block[:, half:]
+            grads[0] = grads[0] + turn_cos * block_cos - turn_sin * block_sin
+            grads[1] = grads[1] + turn_sin * block_cos + turn_cos * block_sin
+        for r in range(2):
+            upright = jnp.concatenate([grads[r], pad], axis=0).T
+            high = upright.astype(BF16).astype(F32)
+            low = pltpu.roll(upright - high, channels, 1)
+            place = pl.ds(2 * p + r, half, stride=4)
+            paired[place, :] = jnp.where(lanes < channels, high, low)
     out[...] = paired[...].astype(BF16)
 
 

time: 92.4 us -> 90.5 us (0.979)
  Pallas kernels: 21.1 us -> 19.7 us
    pallas_call x1, Pallas kernels: 14.2 us -> 12.8 us  [run_cycle(): pl.pallas_call(lambda *refs: cycle_kernel(channels, *refs), out_shape=jax...]
where the time goes in v4:
time: 90.5 us; the launch traced here: 90 us
  starting transfers between devices  35 us (39%)
  waiting for transfers between devices  33.2 us (37%)
  Pallas kernels  19.7 us (22%)
  local copies, waits for them, and re-layouts  1.81 us (2%)
    all_to_all x1, waiting for transfers between devices, shards(): lax.all_to_all(modes.reshape(lat_count, 2, LANES), ('band', 'tp'), split_...  17 us
    pallas_call x1, Pallas kernels, run_cycle(): pl.pallas_call(lambda *refs: cycle_kernel(channels, *refs), out_shape=jax...  12.8 us
    all_to_all x1, starting transfers between devices, shards(): lax.all_to_all(send, 'band', split_axis=0, concat_axis=0, tiled=True)  12.6 us
    all_to_all x1, starting transfers between devices, shards(): got = lax.all_to_all(send, 'tp', split_axis=0, concat_axis=0, tiled=True)  11 us
    all_to_all x1, starting transfers between devices, shards(): lax.all_to_all(modes.reshape(lat_count, 2, LANES), ('band', 'tp'), split_...  9 us
    all_to_all x1, waiting for transfers between devices, shards(): got = lax.all_to_all(send, 'tp', split_axis=0, concat_axis=0, tiled=True)  8.36 us
    all_to_all x1, waiting for transfers between devices, shards(): lax.all_to_all(send, 'band', split_axis=0, concat_axis=0, tiled=True)  7.58 us
    pallas_call x1, Pallas kernels, synthesis(): pl.pallas_call(synthesis_kernel, out_shape=jax.ShapeDtypeStruct((TPS, SEN...  2.67 us
  transfers between devices with their start and end apart: 4, of which 4 were waited for; matrix products, arithmetic and copies ran while one was open for 1% of the time, Pallas kernels for 2%

profile of v4, /device:TPU:1, one launch (start us, length us, event | category | flops | bytes accessed | tf_op | source)
XLA Modules:
  0.0 90.0 jit_solution(9464072833661139480)
XLA Ops:
  0.0 2.7 %synthesis.1 = bf16[8,128,128]{2,1,0:T(8,128)(2,1)} custom-call(f32[69,2,1,384]{3,2,1,0:T(1,128)} %control.1, f32[69,1,384]{2,1,0:T(1,128)} %sigma.1, bf16[2,512,384]{2,1,0:T(8,128)(2,1)} %constant.34.clone.high_hbm.table_high, bf16[2,512,384]{2,1,0:T(8,128)(2,1)} %constant.35.clone.low_hbm.table_low, bf16[69,96]{1,0:T(8,128)(2,1)} %w_in_hbm.1, ...), custom_call_target="tpu_custom_call" | custom-call | flops 400000000 | bytes 2000000 | tf_op jit(solution)/shard_map/synthesis/pallas_call | solution.py:178
  2.7 0.0 copy-start.9
  2.7 11.0 %all-to-all-start = ((bf16[8,128,128]{2,1,0:T(8,128)(2,1)}), bf16[8,128,128]{2,1,0:T(8,128)(2,1)S(1)}, u32[]{:S(2)}, u32[]{:S(2)}) async-start(bf16[8,128,128]{2,1,0:T(8,128)(2,1)} %synthesis.1), calls=%async_computation | async-start | bytes 524288 | tf_op jit(solution)/shard_map/all_to_all | solution.py:632
  13.7 0.0 copy-done.9
  13.7 0.0 copy-start.6
  13.7 0.0 copy-start.7
  13.7 0.0 copy-start.8
  13.8 0.0 copy-start.5
  13.8 0.0 copy-start.4
  13.8 0.6 copy-done.6
  14.4 0.0 copy-done.7
  14.4 0.0 copy-done.8
  14.4 0.0 copy-done.5
  14.5 0.0 copy-done.4
  14.5 1.1 %pack_obs.1.obs = f32[64,1024]{1,0:T(8,128)S(1)} custom-call(s32[8,128]{1,0:T(8,128)S(1)} %bitcast.28, s32[8,128]{1,0:T(8,128)S(1)} %bitcast.29, f32[8,128]{1,0:T(8,128)S(1)} %bitcast.30, f32[8,128]{1,0:T(8,128)S(1)} %bitcast.31, f32[8,128]{1,0:T(8,128)S(1)} %bitcast.32), custom_call_target="tpu_custom_call" | custom-call | flops 200000000 | bytes 300000 | tf_op jit(solution)/shard_map/pack_obs/pallas_call | solution.py:233
  15.6 0.1 bitcast_dynamic-update-slice_fusion.3
  15.7 8.4 %all-to-all-done.arrived.own = bf16[8,128,128]{2,1,0:T(8,128)(2,1)S(1)} async-done(((bf16[8,128,128]{2,1,0:T(8,128)(2,1)}), bf16[8,128,128]{2,1,0:T(8,128)(2,1)S(1)}, u32[]{:S(2)}, u32[]{:S(2)}) %all-to-all-start) | async-done | bytes 262176 | tf_op jit(solution)/shard_map/all_to_all | solution.py:632
  24.0 1.0 %regroup.1 = bf16[1024,128]{1,0:T(8,128)(2,1)} custom-call(bf16[8,128,128]{2,1,0:T(8,128)(2,1)S(1)} %all-to-all-done.arrived.own, f32[64,1024]{1,0:T(8,128)S(1)} %pack_obs.1.obs), custom_call_target="tpu_custom_call" | custom-call | flops 300000 | bytes 800000 | tf_op jit(solution)/shard_map/regroup/pallas_call | solution.py:253
  25.0 12.6 %all-to-all-start.1 = ((bf16[64,16,128]{2,1,0:T(8,128)(2,1)}), bf16[64,16,128]{2,1,0:T(8,128)(2,1)S(1)}, u32[]{:S(2)}, u32[]{:S(2)}) async-start(bf16[64,16,128]{2,1,0:T(8,128)(2,1)} %bitcast.7), calls=%async_computation.1 | async-start | bytes 524288 | tf_op jit(solution)/shard_map/all_to_all | solution.py:640
  37.6 0.1 bitcast_dynamic-update-slice_fusion.2
  37.7 0.1 bitcast_dynamic-update-slice_fusion.1
  37.8 2.4 %collective-permute-start = (bf16[8,128,128]{2,1,0:T(8,128)(2,1)S(1)}, bf16[8,128,128]{2,1,0:T(8,128)(2,1)S(1)}, u32[]{:S(2)}, u32[]{:S(2)}) collective-permute-start(bf16[8,128,128]{2,1,0:T(8,128)(2,1)S(1)} %all-to-all-done.arrived.own), channel_id=1, source_target_pairs={{0,8},{8,0},{16,24},{24,16},{32,40},{40,32},{48,56},{56,48},{64,72... | collective-permute-start | bytes 786440 | tf_op jit(solution)/shard_map/ppermute | solution.py:641
  40.2 0.0 copy-start.10
  40.2 0.6 copy-done.10
  40.8 0.1 bitcast_dynamic-update-slice_fusion
  40.9 0.1 fusion.1.refs_1_
  41.0 0.3 collective-permute-done.other
  41.3 0.7 prepare.1
  42.0 7.6 %all-to-all-done.1.refs_0_ = bf16[64,16,128]{2,1,0:T(8,128)(2,1)S(1)} async-done(((bf16[64,16,128]{2,1,0:T(8,128)(2,1)}), bf16[64,16,128]{2,1,0:T(8,128)(2,1)S(1)}, u32[]{:S(2)}, u32[]{:S(2)}) %all-to-all-start.1) | async-done | bytes 262176 | tf_op jit(solution)/shard_map/all_to_all | solution.py:640
  49.6 0.1 broadcast_in_dim.2.refs_2_
  49.7 0.0 copy-start
  49.7 0.0 copy-start.1
  49.7 12.8 %cycle.1 = bf16[1024,128]{1,0:T(8,128)(2,1)} custom-call(bf16[64,16,128]{2,1,0:T(8,128)(2,1)S(1)} %all-to-all-done.1.refs_0_, f32[6,72,256]{2,1,0:T(8,128)S(1)} %fusion.1.refs_1_, f32[72,256]{1,0:T(8,128)S(1)} %broadcast_in_dim.2.refs_2_, bf16[80,768]{1,0:T(8,128)(2,1)S(1)} %get-tuple-element.10.refs_3_, bf16[768,128]{1,0:T(8,128)(2,1)S(1)} %get-tuple-element.11.refs_4_, ...), custom_call_target="tpu_custom_call" | custom-call | flops 8000000000 | bytes 4000000 | tf_op jit(solution)/shard_map/cycle/pallas_call | solution.py:546
  62.5 0.0 copy-start.2
  62.5 0.0 copy-start.3
  62.6 9.0 %all-to-all-start.2 = ((bf16[512,2,128]{2,1,0:T(2,128)(2,1)}), bf16[512,2,128]{2,1,0:T(2,128)(2,1)S(1)}, u32[]{:S(2)}, u32[]{:S(2)}) async-start(bf16[512,2,128]{2,1,0:T(2,128)(2,1)} %bitcast.14), calls=%async_computation.2 | async-start | bytes 524288 | tf_op jit(solution)/shard_map/all_to_all | solution.py:650
  71.6 17.0 %all-to-all-done.2 = bf16[512,2,128]{2,1,0:T(2,128)(2,1)S(1)} async-done(((bf16[512,2,128]{2,1,0:T(2,128)(2,1)}), bf16[512,2,128]{2,1,0:T(2,128)(2,1)S(1)}, u32[]{:S(2)}, u32[]{:S(2)}) %all-to-all-start.2) | async-done | bytes 262176 | tf_op jit(solution)/shard_map/all_to_all | solution.py:650
  88.6 0.0 copy-done
  88.6 0.0 copy-done.1
  88.6 0.0 copy-done.2
  88.6 0.0 copy-done.3
  88.6 1.4 %analysis.1 = f32[69,2,1,384]{3,2,1,0:T(1,128)} custom-call(s32[1]{0:T(128)} %bitcast.parity, bf16[1024,128]{1,0:T(8,128)(2,1)S(1)} %bitcast.27, f32[69,2,1,384]{3,2,1,0:T(1,128)S(1)} %copy-done.2, f32[69,1,384]{2,1,0:T(1,128)S(1)} %copy-done.3, bf16[2,512,384]{2,1,0:T(8,128)(2,1)S(1)} %copy-done, bf16[2,512,384]{2,1,0:T(8,128)(2,1)S(1)} %copy-done.1), custom_call_target="tpu_custom_call" | custom-call | flops 400000000 | bytes 2000000 | tf_op jit(solution)/shard_map/analysis/pallas_call | solution.py:589
  (5 shorter events, 0.1 us)
Async XLA Ops:
  2.7 11.0 %copy-start.9 = (f32[69,1,1440]{2,1,0:T(1,128)S(1)}, f32[69,1,1440]{2,1,0:T(1,128)}, u32[]{:S(2)}) copy-start(f32[69,1,1440]{2,1,0:T(1,128)} %param.20) | copy-start | bytes 1192324
  2.7 21.4 %all-to-all-start = ((bf16[8,128,128]{2,1,0:T(8,128)(2,1)}), bf16[8,128,128]{2,1,0:T(8,128)(2,1)S(1)}, u32[]{:S(2)}, u32[]{:S(2)}) async-start(bf16[8,128,128]{2,1,0:T(8,128)(2,1)} %synthesis.1), calls=%async_computation | async-start | bytes 524288 | tf_op jit(solution)/shard_map/all_to_all | solution.py:632
  13.7 0.7 copy-start.6
  13.7 0.7 copy-start.7
  13.7 0.7 copy-start.8
  13.8 0.7 copy-start.5
  13.8 0.7 copy-start.4
  25.0 24.6 %all-to-all-start.1 = ((bf16[64,16,128]{2,1,0:T(8,128)(2,1)}), bf16[64,16,128]{2,1,0:T(8,128)(2,1)S(1)}, u32[]{:S(2)}, u32[]{:S(2)}) async-start(bf16[64,16,128]{2,1,0:T(8,128)(2,1)} %bitcast.7), calls=%async_computation.1 | async-start | bytes 524288 | tf_op jit(solution)/shard_map/all_to_all | solution.py:640
  37.8 3.5 %collective-permute-start = (bf16[8,128,128]{2,1,0:T(8,128)(2,1)S(1)}, bf16[8,128,128]{2,1,0:T(8,128)(2,1)S(1)}, u32[]{:S(2)}, u32[]{:S(2)}) collective-permute-start(bf16[8,128,128]{2,1,0:T(8,128)(2,1)S(1)} %all-to-all-done.arrived.own), channel_id=1, source_target_pairs={{0,8},{8,0},{16,24},{24,16},{32,40},{40,32},{48,56},{56,48},{64,72... | collective-permute-start | bytes 786440 | tf_op jit(solution)/shard_map/ppermute | solution.py:641
  40.2 0.7 copy-start.10
  49.7 38.9 %copy-start = (bf16[2,512,384]{2,1,0:T(8,128)(2,1)S(1)}, bf16[2,512,384]{2,1,0:T(8,128)(2,1)}, u32[]{:S(2)}) copy-start(bf16[2,512,384]{2,1,0:T(8,128)(2,1)} %constant.34.clone.high_hbm.table_high) | copy-start | bytes 2359300
  49.7 38.9 %copy-start.1 = (bf16[2,512,384]{2,1,0:T(8,128)(2,1)S(1)}, bf16[2,512,384]{2,1,0:T(8,128)(2,1)}, u32[]{:S(2)}) copy-start(bf16[2,512,384]{2,1,0:T(8,128)(2,1)} %constant.35.clone.low_hbm.table_low) | copy-start | bytes 2359300
  62.5 26.1 %copy-start.2 = (f32[69,2,1,384]{3,2,1,0:T(1,128)S(1)}, f32[69,2,1,384]{3,2,1,0:T(1,128)}, u32[]{:S(2)}) copy-start(f32[69,2,1,384]{3,2,1,0:T(1,128)} %control.1) | copy-start | bytes 635908
  62.5 26.1 %copy-start.3 = (f32[69,1,384]{2,1,0:T(1,128)S(1)}, f32[69,1,384]{2,1,0:T(1,128)}, u32[]{:S(2)}) copy-start(f32[69,1,384]{2,1,0:T(1,128)} %sigma.1) | copy-start | bytes 317956
  62.6 26.0 %all-to-all-start.2 = ((bf16[512,2,128]{2,1,0:T(2,128)(2,1)}), bf16[512,2,128]{2,1,0:T(2,128)(2,1)S(1)}, u32[]{:S(2)}, u32[]{:S(2)}) async-start(bf16[512,2,128]{2,1,0:T(2,128)(2,1)} %bitcast.14), calls=%async_computation.2 | async-start | bytes 524288 | tf_op jit(solution)/shard_map/all_to_all | solution.py:650

commit v5 on v4

--- a/solution.py
+++ b/solution.py
@@ -90,9 +90,10 @@
     return lax.broadcasted_iota(jnp.int32, shape, len(shape) - 1)
 
 
-SEND_ROWS = 128
+SEND_ROWS = 112
 REST_LANE = 96
-PIECE_LANE = 112
+MORE_LANE = 112
+QUARTER = 40
 
 
 def synthesis_kernel(
@@ -146,22 +147,17 @@
     whole = dot3((table_high[...], table_low[...]), parts, NT)
     modes[0] = whole[:, 0:LANES]
     modes[1] = whole[:, LANES:]
-    even = lax.rem(lax.axis_index("band"), 2) == 0
-    rows = jnp.where(even, w_in[...].astype(F32), w_out[...].astype(F32))
-    rows = jnp.pad(rows, ((0, ROWS - channels), (0, LANES - rows.shape[1])))
-    lanes = lane_ids((8, LANES))
-    pieces = [
-        jnp.where(
-            lanes >= PIECE_LANE,
-            pltpu.roll(rows[BANDS:ROWS], PIECE_LANE - start, 1),
-            rows[start // 2 : start // 2 + 8],
-        )
-        for start in range(0, REST_LANE, 16)
-    ]
-    rows = jnp.concatenate([*pieces, rows[REST_LANE // 2 : BANDS]], axis=0)
+    code = lax.rem(lax.axis_index("band"), 4)
+    rows = jnp.where(lax.rem(code, 2) == 0, w_in[...].astype(F32), w_out[...].astype(F32))
+    rows = jnp.pad(rows, ((0, 2 * QUARTER - channels), (0, LANES - rows.shape[1])))
+    rows = jnp.where(code < 2, rows[0:QUARTER], rows[QUARTER:])
+    rows = jnp.concatenate([rows, jnp.zeros((48 - QUARTER, LANES), F32)], axis=0)
+    filler = jnp.zeros((32, LANES), F32)
     for dest in range(TPS):
         out[dest, 0:BANDS, :] = modes[0, pl.ds(dest, BANDS, stride=TPS), :].astype(BF16)
         rest = modes[1, pl.ds(dest, BANDS, stride=TPS), :]
+        more = pltpu.roll(rest[48:BANDS], MORE_LANE - REST_LANE, 1)
+        rest = rest[0:48] + jnp.concatenate([more, filler], axis=0)
         out[dest, BANDS:SEND_ROWS, :] = (rest + rows).astype(BF16)
 
 
@@ -243,7 +239,14 @@
     lanes = lane_ids((BANDS, LANES))
     for t in range(TPS):
         rows[pl.ds(t, BANDS, stride=16), :] = arrived[t, 0:BANDS, :].astype(F32)
-        rest = pltpu.roll(arrived[t, BANDS : 2 * BANDS, :].astype(F32), LANES - REST_LANE, 1)
+        rest = arrived[t, BANDS:SEND_ROWS, :].astype(F32)
+        rest = jnp.concatenate(
+            [
+                pltpu.roll(rest, LANES - REST_LANE, 1),
+                pltpu.roll(rest[0 : 2 * BANDS - SEND_ROWS], LANES - MORE_LANE, 1),
+            ],
+            axis=0,
+        )
         rest = jnp.where(lanes < 16, rest, obs[:, t * LANES : (t + 1) * LANES])
         rows[pl.ds(8 + t, BANDS, stride=16), :] = rest
     out[...] = rows[...].astype(BF16)
@@ -260,42 +263,40 @@
     )(arrived, obs)
 
 
-def prepare_kernel(own, other, *refs):
-    sources, (in_rows, in_columns, out_rows, out_columns, *targets), (arrivals,) = (
-        refs[:1],
-        refs[1:6],
-        refs[6:],
-    )
-    copies = [
-        pltpu.make_async_copy(source, target, arrivals.at[i])
-        for i, (source, target) in enumerate(zip(sources, targets))
-    ]
-    for copy in copies:
-        copy.start()
-    even = lax.rem(lax.axis_index("band"), 2) == 0
-    lanes = lane_ids((8, LANES))
-    filler = jnp.zeros((LANES - ROWS, LANES), F32)
-    for columns, rows, first in ((in_columns, in_rows, True), (out_columns, out_rows, False)):
+def prepare_kernel(*refs):
+    arrived, (source,), (in_rows, in_columns, out_rows, out_columns, target), (arrival,) = (
+        refs[:4],
+        refs[4:5],
+        refs[5:10],
+        refs[10:],
+    )
+    copy = pltpu.make_async_copy(source, target, arrival)
+    copy.start()
+    code = lax.rem(lax.axis_index("band"), 4)
+    filler = jnp.zeros((LANES - 2 * QUARTER, LANES), F32)
+    for columns, rows, weight in ((in_columns, in_rows, 0), (out_columns, out_rows, 1)):
         pieces = []
         for t in range(TPS):
-            mine = own[t, BANDS:SEND_ROWS, :].astype(F32)
-            theirs = other[t, BANDS:SEND_ROWS, :].astype(F32)
-            piece = jnp.where(even == first, mine, theirs)
-            last = jnp.zeros((8, LANES), F32)
-            for start in range(0, REST_LANE, 16):
-                part = piece[start // 2 : start // 2 + 8]
-                part = pltpu.roll(part, LANES - PIECE_LANE + start, 1)
-                last = jnp.where((lanes >= start) & (lanes < start + 16), part, last)
-            piece = jnp.concatenate([piece, last, filler], axis=0)
+            quarters = []
+            for wanted in (weight, weight + 2):
+                choices = [arrived[wanted ^ own][t, BANDS:SEND_ROWS, :] for own in range(4)]
+                choices = [choice.astype(F32)[0:QUARTER] for choice in choices]
+                quarters.append(
+                    jnp.where(
+                        code < 2,
+                        jnp.where(code == 0, choices[0], choices[1]),
+                        jnp.where(code == 2, choices[2], choices[3]),
+                    )
+                )
+            piece = jnp.concatenate([*quarters, filler], axis=0)
             pieces.append(piece.T[0:REST_LANE])
         upright = jnp.concatenate(pieces, axis=0)
         columns[...] = upright.astype(BF16)
         rows[...] = upright.T[0:80].astype(BF16)
-    for copy in copies:
-        copy.wait()
-
-
-def prepare(own, other, tables):
+    copy.wait()
+
+
+def prepare(arrived, turns):
     hidden = TPS * 96
     return pl.pallas_call(
         prepare_kernel,
@@ -304,15 +305,15 @@
             jax.ShapeDtypeStruct((hidden, LANES), BF16),
             jax.ShapeDtypeStruct((80, hidden), BF16),
             jax.ShapeDtypeStruct((hidden, LANES), BF16),
-            *(jax.ShapeDtypeStruct(table.shape, table.dtype) for table in tables),
+            jax.ShapeDtypeStruct(turns.shape, turns.dtype),
         ),
-        in_specs=[IN_VMEM] * 2 + [IN_HBM],
+        in_specs=[IN_VMEM] * 4 + [IN_HBM],
         out_specs=[IN_VMEM] * 5,
-        scratch_shapes=[pltpu.SemaphoreType.DMA((1,))],
+        scratch_shapes=[pltpu.SemaphoreType.DMA],
         cost_estimate=pl.CostEstimate(flops=1_000_000, bytes_accessed=5_000_000, transcendentals=0),
         compiler_params=pltpu.CompilerParams(vmem_limit_bytes=8 * MIB),
         name="prepare",
-    )(own, other, *in_hbm(*tables))
+    )(*arrived, *in_hbm(turns))
 
 
 GELU_SCALE = math.sqrt(2.0 / math.pi)
@@ -638,8 +639,10 @@
     )
     send = regroup(got, obs).reshape(BANDS, 16, LANES)
     arrived = lax.all_to_all(send, "band", split_axis=0, concat_axis=0, tiled=True)
-    other = lax.ppermute(got, "band", [(i, i ^ 1) for i in range(BANDS)])
-    prepared = prepare(got, other, (turns,))
+    others = [
+        lax.ppermute(got, "band", [(i, i ^ flip) for i in range(BANDS)]) for flip in (1, 2, 3)
+    ]
+    prepared = prepare([got, *others], turns)
     prior = jnp.pad(prior_mean_field[:, 0, :], ((0, ROWS - channels), (0, 0)))
     prior = jnp.concatenate([prior, prior[:, : WIDTH - STRIDE]], axis=1)
     prior = jnp.stack([prior[:, a * STRIDE : a * STRIDE + WIDTH] for a in range(BLOCKS)])

time: 90.5 us -> 98.4 us (1.087)
  starting transfers between devices: 35 us -> 42.7 us
    ppermute x1 -> x3, waiting for transfers between devices: 0.28 us -> 8.69 us  [shards(): lax.ppermute(got, 'band', [(i, i ^ flip) for i in range(BANDS)])]
    all_to_all x1, waiting for transfers between devices: 7.58 us -> 0.01 us  [shards(): lax.all_to_all(send, 'band', split_axis=0, concat_axis=0, tiled=True)]
    ppermute x1 -> x3, starting transfers between devices: 2.36 us -> 7.87 us  [shards(): lax.ppermute(got, 'band', [(i, i ^ flip) for i in range(BANDS)])]
    all_to_all x1, starting transfers between devices: 9 us -> 11.4 us  [shards(): lax.all_to_all(modes.reshape(lat_count, 2, LANES), ('band', 'tp'), split_...]
  transfers between devices with their start and end apart: 4 -> 6, of which waited for: 4 -> 4; matrix products, arithmetic and copies ran while one was open for 1% -> 1% of each run, Pallas kernels for 2% -> 2%
where the time goes in v5:
time: 98.4 us; the launch traced here: 97.9 us
  starting transfers between devices  42.7 us (43%)
  waiting for transfers between devices  33.3 us (34%)
  Pallas kernels  19.7 us (20%)
  local copies, waits for them, and re-layouts  1.82 us (2%)
    all_to_all x1, waiting for transfers between devices, shards(): lax.all_to_all(modes.reshape(lat_count, 2, LANES), ('band', 'tp'), split_...  16.8 us
    pallas_call x1, Pallas kernels, run_cycle(): pl.pallas_call(lambda *refs: cycle_kernel(channels, *refs), out_shape=jax...  12.8 us
    all_to_all x1, starting transfers between devices, shards(): lax.all_to_all(send, 'band', split_axis=0, concat_axis=0, tiled=True)  12.5 us
    all_to_all x1, starting transfers between devices, shards(): lax.all_to_all(modes.reshape(lat_count, 2, LANES), ('band', 'tp'), split_...  11.4 us
    all_to_all x1, starting transfers between devices, shards(): got = lax.all_to_all(send, 'tp', split_axis=0, concat_axis=0, tiled=True)  11 us
    ppermute x3, waiting for transfers between devices, shards(): lax.ppermute(got, 'band', [(i, i ^ flip) for i in range(BANDS)])  8.69 us
    ppermute x3, starting transfers between devices, shards(): lax.ppermute(got, 'band', [(i, i ^ flip) for i in range(BANDS)])  7.87 us
    all_to_all x1, waiting for transfers between devices, shards(): got = lax.all_to_all(send, 'tp', split_axis=0, concat_axis=0, tiled=True)  7.75 us
  transfers between devices with their start and end apart: 6, of which 4 were waited for; matrix products, arithmetic and copies ran while one was open for 1% of the time, Pallas kernels for 2%

profile of v5, /device:TPU:1, one launch (start us, length us, event | category | flops | bytes accessed | tf_op | source)
XLA Modules:
  0.0 97.9 jit_solution(4776177229075445192)
XLA Ops:
  0.0 2.7 %synthesis.1 = bf16[8,112,128]{2,1,0:T(8,128)(2,1)} custom-call(f32[69,2,1,384]{3,2,1,0:T(1,128)} %control.1, f32[69,1,384]{2,1,0:T(1,128)} %sigma.1, bf16[2,512,384]{2,1,0:T(8,128)(2,1)} %constant.34.clone.high_hbm.table_high, bf16[2,512,384]{2,1,0:T(8,128)(2,1)} %constant.35.clone.low_hbm.table_low, bf16[69,96]{1,0:T(8,128)(2,1)} %w_in_hbm.1, ...), custom_call_target="tpu_custom_call" | custom-call | flops 400000000 | bytes 2000000 | tf_op jit(solution)/shard_map/synthesis/pallas_call | solution.py:174
  2.7 0.0 copy-start.9
  2.7 11.0 %all-to-all-start = ((bf16[8,112,128]{2,1,0:T(8,128)(2,1)}), bf16[8,112,128]{2,1,0:T(8,128)(2,1)S(1)}, u32[]{:S(2)}, u32[]{:S(2)}) async-start(bf16[8,112,128]{2,1,0:T(8,128)(2,1)} %synthesis.1), calls=%async_computation | async-start | bytes 458752 | tf_op jit(solution)/shard_map/all_to_all | solution.py:633
  13.7 0.0 copy-done.9
  13.7 0.0 copy-start.6
  13.7 0.0 copy-start.7
  13.8 0.0 copy-start.8
  13.8 0.0 copy-start.5
  13.8 0.0 copy-start.4
  13.8 0.6 copy-done.6
  14.4 0.0 copy-done.7
  14.4 0.0 copy-done.8
  14.5 0.0 copy-done.5
  14.5 0.0 copy-done.4
  14.5 1.1 %pack_obs.1.obs = f32[64,1024]{1,0:T(8,128)S(1)} custom-call(s32[8,128]{1,0:T(8,128)S(1)} %bitcast.28, s32[8,128]{1,0:T(8,128)S(1)} %bitcast.29, f32[8,128]{1,0:T(8,128)S(1)} %bitcast.30, f32[8,128]{1,0:T(8,128)S(1)} %bitcast.31, f32[8,128]{1,0:T(8,128)S(1)} %bitcast.32), custom_call_target="tpu_custom_call" | custom-call | flops 200000000 | bytes 300000 | tf_op jit(solution)/shard_map/pack_obs/pallas_call | solution.py:229
  15.6 0.1 bitcast_dynamic-update-slice_fusion.3
  15.7 7.8 %all-to-all-done.arrived.refs_0_ = bf16[8,112,128]{2,1,0:T(8,128)(2,1)S(1)} async-done(((bf16[8,112,128]{2,1,0:T(8,128)(2,1)}), bf16[8,112,128]{2,1,0:T(8,128)(2,1)S(1)}, u32[]{:S(2)}, u32[]{:S(2)}) %all-to-all-start) | async-done | bytes 229408 | tf_op jit(solution)/shard_map/all_to_all | solution.py:633
  23.5 0.9 regroup.1
  24.4 12.5 %all-to-all-start.1 = ((bf16[64,16,128]{2,1,0:T(8,128)(2,1)}), bf16[64,16,128]{2,1,0:T(8,128)(2,1)S(1)}, u32[]{:S(2)}, u32[]{:S(2)}) async-start(bf16[64,16,128]{2,1,0:T(8,128)(2,1)} %bitcast.7), calls=%async_computation.1 | async-start | bytes 524288 | tf_op jit(solution)/shard_map/all_to_all | solution.py:641
  36.9 0.1 bitcast_dynamic-update-slice_fusion.2
  37.0 0.1 bitcast_dynamic-update-slice_fusion.1
  37.1 2.4 %collective-permute-start = (bf16[8,112,128]{2,1,0:T(8,128)(2,1)S(1)}, bf16[8,112,128]{2,1,0:T(8,128)(2,1)S(1)}, u32[]{:S(2)}, u32[]{:S(2)}) collective-permute-start(bf16[8,112,128]{2,1,0:T(8,128)(2,1)S(1)} %all-to-all-done.arrived.refs_0_), channel_id=1, source_target_pairs={{0,8},{8,0},{16,24},{24,16},{32,40},{40,32},{48,56},{56,48},{64,72... | collective-permute-start | bytes 688136 | tf_op jit(solution)/shard_map/ppermute | solution.py:643
  39.5 3.2 %collective-permute-start.1 = (bf16[8,112,128]{2,1,0:T(8,128)(2,1)S(1)}, bf16[8,112,128]{2,1,0:T(8,128)(2,1)S(1)}, u32[]{:S(2)}, u32[]{:S(2)}) collective-permute-start(bf16[8,112,128]{2,1,0:T(8,128)(2,1)S(1)} %all-to-all-done.arrived.refs_0_), channel_id=1, source_target_pairs={{0,16},{8,24},{16,0},{24,8},{32,48},{40,56},{48,32},{56,40},{64,80... | collective-permute-start | bytes 688136 | tf_op jit(solution)/shard_map/ppermute | solution.py:643
  42.7 2.3 %collective-permute-start.2 = (bf16[8,112,128]{2,1,0:T(8,128)(2,1)S(1)}, bf16[8,112,128]{2,1,0:T(8,128)(2,1)S(1)}, u32[]{:S(2)}, u32[]{:S(2)}) collective-permute-start(bf16[8,112,128]{2,1,0:T(8,128)(2,1)S(1)} %all-to-all-done.arrived.refs_0_), channel_id=1, source_target_pairs={{0,24},{8,16},{16,8},{24,0},{32,56},{40,48},{48,40},{56,32},{64,88... | collective-permute-start | bytes 688136 | tf_op jit(solution)/shard_map/ppermute | solution.py:643
  45.0 0.0 copy-start.10
  45.1 0.6 copy-done.10
  45.7 0.1 bitcast_dynamic-update-slice_fusion
  45.7 0.1 fusion.1.refs_1_
  45.9 0.0 collective-permute-done.refs_1_
  45.9 3.6 %collective-permute-done.1.refs_2_ = bf16[8,112,128]{2,1,0:T(8,128)(2,1)S(1)} collective-permute-done((bf16[8,112,128]{2,1,0:T(8,128)(2,1)S(1)}, bf16[8,112,128]{2,1,0:T(8,128)(2,1)S(1)}, u32[]{:S(2)}, u32[]{:S(2)}) %collective-permute-start.1) | collective-permute-done | bytes 229408 | tf_op jit(solution)/shard_map/ppermute | solution.py:643
  49.5 5.1 %collective-permute-done.2.refs_3_ = bf16[8,112,128]{2,1,0:T(8,128)(2,1)S(1)} collective-permute-done((bf16[8,112,128]{2,1,0:T(8,128)(2,1)S(1)}, bf16[8,112,128]{2,1,0:T(8,128)(2,1)S(1)}, u32[]{:S(2)}, u32[]{:S(2)}) %collective-permute-start.2) | collective-permute-done | bytes 229408 | tf_op jit(solution)/shard_map/ppermute | solution.py:643
  54.6 0.7 prepare.1
  55.3 0.0 all-to-all-done.1.refs_0_
  55.3 0.1 broadcast_in_dim.2.refs_2_
  55.4 0.0 copy-start
  55.4 0.0 copy-start.1
  55.4 12.8 %cycle.1 = bf16[1024,128]{1,0:T(8,128)(2,1)} custom-call(bf16[64,16,128]{2,1,0:T(8,128)(2,1)S(1)} %all-to-all-done.1.refs_0_, f32[6,72,256]{2,1,0:T(8,128)S(1)} %fusion.1.refs_1_, f32[72,256]{1,0:T(8,128)S(1)} %broadcast_in_dim.2.refs_2_, bf16[80,768]{1,0:T(8,128)(2,1)S(1)} %get-tuple-element.10.refs_3_, bf16[768,128]{1,0:T(8,128)(2,1)S(1)} %get-tuple-element.11.refs_4_, ...), custom_call_target="tpu_custom_call" | custom-call | flops 8000000000 | bytes 4000000 | tf_op jit(solution)/shard_map/cycle/pallas_call | solution.py:547
  68.2 0.0 copy-start.2
  68.2 0.0 copy-start.3
  68.3 11.4 %all-to-all-start.2 = ((bf16[512,2,128]{2,1,0:T(2,128)(2,1)}), bf16[512,2,128]{2,1,0:T(2,128)(2,1)S(1)}, u32[]{:S(2)}, u32[]{:S(2)}) async-start(bf16[512,2,128]{2,1,0:T(2,128)(2,1)} %bitcast.14), calls=%async_computation.2 | async-start | bytes 524288 | tf_op jit(solution)/shard_map/all_to_all | solution.py:653
  79.6 16.8 %all-to-all-done.2 = bf16[512,2,128]{2,1,0:T(2,128)(2,1)S(1)} async-done(((bf16[512,2,128]{2,1,0:T(2,128)(2,1)}), bf16[512,2,128]{2,1,0:T(2,128)(2,1)S(1)}, u32[]{:S(2)}, u32[]{:S(2)}) %all-to-all-start.2) | async-done | bytes 262176 | tf_op jit(solution)/shard_map/all_to_all | solution.py:653
  96.5 0.0 copy-done
  96.5 0.0 copy-done.1
  96.5 0.0 copy-done.2
  96.5 0.0 copy-done.3
  96.5 1.4 %analysis.1 = f32[69,2,1,384]{3,2,1,0:T(1,128)} custom-call(s32[1]{0:T(128)} %bitcast.parity, bf16[1024,128]{1,0:T(8,128)(2,1)S(1)} %bitcast.27, f32[69,2,1,384]{3,2,1,0:T(1,128)S(1)} %copy-done.2, f32[69,1,384]{2,1,0:T(1,128)S(1)} %copy-done.3, bf16[2,512,384]{2,1,0:T(8,128)(2,1)S(1)} %copy-done, bf16[2,512,384]{2,1,0:T(8,128)(2,1)S(1)} %copy-done.1), custom_call_target="tpu_custom_call" | custom-call | flops 400000000 | bytes 2000000 | tf_op jit(solution)/shard_map/analysis/pallas_call | solution.py:590
  (5 shorter events, 0.1 us)
Async XLA Ops:
  2.7 11.0 %copy-start.9 = (f32[69,1,1440]{2,1,0:T(1,128)S(1)}, f32[69,1,1440]{2,1,0:T(1,128)}, u32[]{:S(2)}) copy-start(f32[69,1,1440]{2,1,0:T(1,128)} %param.20) | copy-start | bytes 1192324
  2.7 20.7 %all-to-all-start = ((bf16[8,112,128]{2,1,0:T(8,128)(2,1)}), bf16[8,112,128]{2,1,0:T(8,128)(2,1)S(1)}, u32[]{:S(2)}, u32[]{:S(2)}) async-start(bf16[8,112,128]{2,1,0:T(8,128)(2,1)} %synthesis.1), calls=%async_computation | async-start | bytes 458752 | tf_op jit(solution)/shard_map/all_to_all | solution.py:633
  13.7 0.7 copy-start.6
  13.7 0.7 copy-start.7
  13.8 0.7 copy-start.8
  13.8 0.7 copy-start.5
  13.8 0.7 copy-start.4
  24.4 30.9 %all-to-all-start.1 = ((bf16[64,16,128]{2,1,0:T(8,128)(2,1)}), bf16[64,16,128]{2,1,0:T(8,128)(2,1)S(1)}, u32[]{:S(2)}, u32[]{:S(2)}) async-start(bf16[64,16,128]{2,1,0:T(8,128)(2,1)} %bitcast.7), calls=%async_computation.1 | async-start | bytes 524288 | tf_op jit(solution)/shard_map/all_to_all | solution.py:641
  37.1 8.8 %collective-permute-start = (bf16[8,112,128]{2,1,0:T(8,128)(2,1)S(1)}, bf16[8,112,128]{2,1,0:T(8,128)(2,1)S(1)}, u32[]{:S(2)}, u32[]{:S(2)}) collective-permute-start(bf16[8,112,128]{2,1,0:T(8,128)(2,1)S(1)} %all-to-all-done.arrived.refs_0_), channel_id=1, source_target_pairs={{0,8},{8,0},{16,24},{24,16},{32,40},{40,32},{48,56},{56,48},{64,72... | collective-permute-start | bytes 688136 | tf_op jit(solution)/shard_map/ppermute | solution.py:643
  39.5 10.0 %collective-permute-start.1 = (bf16[8,112,128]{2,1,0:T(8,128)(2,1)S(1)}, bf16[8,112,128]{2,1,0:T(8,128)(2,1)S(1)}, u32[]{:S(2)}, u32[]{:S(2)}) collective-permute-start(bf16[8,112,128]{2,1,0:T(8,128)(2,1)S(1)} %all-to-all-done.arrived.refs_0_), channel_id=1, source_target_pairs={{0,16},{8,24},{16,0},{24,8},{32,48},{40,56},{48,32},{56,40},{64,80... | collective-permute-start | bytes 688136 | tf_op jit(solution)/shard_map/ppermute | solution.py:643
  42.7 11.9 %collective-permute-start.2 = (bf16[8,112,128]{2,1,0:T(8,128)(2,1)S(1)}, bf16[8,112,128]{2,1,0:T(8,128)(2,1)S(1)}, u32[]{:S(2)}, u32[]{:S(2)}) collective-permute-start(bf16[8,112,128]{2,1,0:T(8,128)(2,1)S(1)} %all-to-all-done.arrived.refs_0_), channel_id=1, source_target_pairs={{0,24},{8,16},{16,8},{24,0},{32,56},{40,48},{48,40},{56,32},{64,88... | collective-permute-start | bytes 688136 | tf_op jit(solution)/shard_map/ppermute | solution.py:643
  45.0 0.7 copy-start.10
  55.4 41.1 %copy-start = (bf16[2,512,384]{2,1,0:T(8,128)(2,1)S(1)}, bf16[2,512,384]{2,1,0:T(8,128)(2,1)}, u32[]{:S(2)}) copy-start(bf16[2,512,384]{2,1,0:T(8,128)(2,1)} %constant.34.clone.high_hbm.table_high) | copy-start | bytes 2359300
  55.4 41.1 %copy-start.1 = (bf16[2,512,384]{2,1,0:T(8,128)(2,1)S(1)}, bf16[2,512,384]{2,1,0:T(8,128)(2,1)}, u32[]{:S(2)}) copy-start(bf16[2,512,384]{2,1,0:T(8,128)(2,1)} %constant.35.clone.low_hbm.table_low) | copy-start | bytes 2359300
  68.2 28.3 %copy-start.2 = (f32[69,2,1,384]{3,2,1,0:T(1,128)S(1)}, f32[69,2,1,384]{3,2,1,0:T(1,128)}, u32[]{:S(2)}) copy-start(f32[69,2,1,384]{3,2,1,0:T(1,128)} %control.1) | copy-start | bytes 635908
  68.2 28.3 %copy-start.3 = (f32[69,1,384]{2,1,0:T(1,128)S(1)}, f32[69,1,384]{2,1,0:T(1,128)}, u32[]{:S(2)}) copy-start(f32[69,1,384]{2,1,0:T(1,128)} %sigma.1) | copy-start | bytes 317956
  68.3 28.2 %all-to-all-start.2 = ((bf16[512,2,128]{2,1,0:T(2,128)(2,1)}), bf16[512,2,128]{2,1,0:T(2,128)(2,1)S(1)}, u32[]{:S(2)}, u32[]{:S(2)}) async-start(bf16[512,2,128]{2,1,0:T(2,128)(2,1)} %bitcast.14), calls=%async_computation.2 | async-start | bytes 524288 | tf_op jit(solution)/shard_map/all_to_all | solution.py:653

commit v6 on v4

--- a/solution.py
+++ b/solution.py
@@ -262,9 +262,9 @@
 
 def prepare_kernel(own, other, *refs):
     sources, (in_rows, in_columns, out_rows, out_columns, *targets), (arrivals,) = (
-        refs[:1],
-        refs[1:6],
-        refs[6:],
+        refs[:3],
+        refs[3:10],
+        refs[10:],
     )
     copies = [
         pltpu.make_async_copy(source, target, arrivals.at[i])
@@ -306,9 +306,9 @@
             jax.ShapeDtypeStruct((hidden, LANES), BF16),
             *(jax.ShapeDtypeStruct(table.shape, table.dtype) for table in tables),
         ),
-        in_specs=[IN_VMEM] * 2 + [IN_HBM],
-        out_specs=[IN_VMEM] * 5,
-        scratch_shapes=[pltpu.SemaphoreType.DMA((1,))],
+        in_specs=[IN_VMEM] * 2 + [IN_HBM] * 3,
+        out_specs=[IN_VMEM] * 7,
+        scratch_shapes=[pltpu.SemaphoreType.DMA((3,))],
         cost_estimate=pl.CostEstimate(flops=1_000_000, bytes_accessed=5_000_000, transcendentals=0),
         compiler_params=pltpu.CompilerParams(vmem_limit_bytes=8 * MIB),
         name="prepare",
@@ -331,20 +331,19 @@
 def cycle_kernel(
     channels,
     arrived,
-    prior,
     gains,
     in_rows,
     in_columns,
     out_rows,
     out_columns,
     turns,
-    table_high_hbm,
-    table_low_hbm,
+    table_high,
+    table_low,
+    prior_hbm,
     wide_high_hbm,
     wide_low_hbm,
     out,
-    table_high,
-    table_low,
+    prior,
     wide_high,
     wide_low,
     arrivals,
@@ -357,10 +356,9 @@
 ):
     orders = turns.shape[1]
     copies = [
-        pltpu.make_async_copy(table_high_hbm, table_high, arrivals.at[0]),
-        pltpu.make_async_copy(table_low_hbm, table_low, arrivals.at[1]),
-        pltpu.make_async_copy(wide_high_hbm, wide_high, arrivals.at[2]),
-        pltpu.make_async_copy(wide_low_hbm, wide_low, arrivals.at[3]),
+        pltpu.make_async_copy(prior_hbm, prior, arrivals.at[0]),
+        pltpu.make_async_copy(wide_high_hbm, wide_high, arrivals.at[1]),
+        pltpu.make_async_copy(wide_low_hbm, wide_low, arrivals.at[2]),
     ]
     for copy in copies:
         copy.start()
@@ -392,14 +390,13 @@
             )
         )
     turned = split(jnp.concatenate(turned, axis=0))
-    for copy in copies[:2]:
-        copy.wait()
     sums = []
     for p in range(2):
         span = slice(p * orders, (p + 1) * orders)
         part = (turned[0][:, span], turned[1][:, span])
         sums.append(dot3(part, (table_high[span, :], table_low[span, :])))
     field = jnp.concatenate([sums[0] + sums[1], sums[0] - sums[1]], axis=0)
+    copies[0].wait()
     state[...] = prior[...].reshape(BLOCKS * ROWS, WIDTH) + field
 
     forecast = []
@@ -516,7 +513,7 @@
         costate.append(force + scaled * inverse - field * (along * inverse * inverse * inverse))
     near = jnp.concatenate(costate[:PAIRS], axis=0)
     far = jnp.concatenate(costate[PAIRS:], axis=0)
-    for copy in copies[2:]:
+    for copy in copies[1:]:
         copy.wait()
     pad = jnp.zeros((LANES - ROWS, half), F32)
     lanes = lane_ids((half, LANES))
@@ -540,17 +537,18 @@
     out[...] = paired[...].astype(BF16)
 
 
-def run_cycle(channels, arrived, prior, gains, prepared, table):
+def run_cycle(channels, arrived, prior, gains, prepared, wide):
     orders = prepared[4].shape[1]
     hidden = prepared[1].shape[0]
     return pl.pallas_call(
         lambda *refs: cycle_kernel(channels, *refs),
         out_shape=jax.ShapeDtypeStruct((2 * orders, LANES), BF16),
-        in_specs=[IN_VMEM] * 8 + [IN_HBM] * 4,
+        in_specs=[IN_VMEM] * 9 + [IN_HBM] * 3,
         out_specs=IN_VMEM,
         scratch_shapes=[
-            *(pltpu.VMEM(part.shape, BF16) for part in table),
-            pltpu.SemaphoreType.DMA((4,)),
+            pltpu.VMEM(prior.shape, F32),
+            *(pltpu.VMEM(part.shape, BF16) for part in wide),
+            pltpu.SemaphoreType.DMA((3,)),
             pltpu.VMEM((BLOCKS * ROWS, WIDTH), F32),
             pltpu.VMEM((BLOCKS, hidden, WIDTH), F32),
             pltpu.VMEM((BANDS // 2, FIELDS, LANES), F32),
@@ -563,10 +561,11 @@
             flops=8_000_000_000, bytes_accessed=4_000_000, transcendentals=1_200_000
         ),
         name="cycle",
-    )(arrived, prior, gains, *prepared, *in_hbm(*table))
-
-
-def analysis_kernel(parity, arrived, control, sigma, table_high, table_low, out, rows):
+    )(arrived, gains, *prepared, *in_hbm(prior, *wide))
+
+
+def analysis_kernel(arrived, control, sigma, table_high, table_low, out, rows):
+    parity = lax.rem(lax.axis_index("tp"), 2)
     channels = sigma.shape[0]
     orders = arrived.shape[0] // 2
     rows[...] = arrived[...].astype(F32)
@@ -577,35 +576,19 @@
         grad = jnp.where(lanes < channels, both, 0.0)
         grad = grad + jnp.where(lanes < LANES - channels, low, 0.0)
         grad_t = split(grad.T[0:ROWS])
-        projected = dot3(grad_t, (table_high[0], table_low[0]))
+        projected = dot3(grad_t, (table_high[parity], table_low[parity]))
         out[:, r, 0, :] = control[:, r, 0, :] + sigma[:, 0, :] * projected[0:channels]
 
 
-def analysis(parity, arrived, control, sigma, table):
-    wave_count = table[0].shape[2]
-    lat_count = table[0].shape[1]
-    whole = lambda shape: pl.BlockSpec(shape, lambda i, p: (0,) * len(shape))
-    chosen = pl.BlockSpec((1, lat_count, wave_count), lambda i, p: (p[0], 0, 0))
+def analysis(arrived, control, sigma, table):
     return pl.pallas_call(
         analysis_kernel,
         out_shape=jax.ShapeDtypeStruct(control.shape, F32),
-        grid_spec=pltpu.PrefetchScalarGridSpec(
-            num_scalar_prefetch=1,
-            grid=(1,),
-            in_specs=[
-                whole(arrived.shape),
-                whole(control.shape),
-                whole(sigma.shape),
-                chosen,
-                chosen,
-            ],
-            out_specs=whole(control.shape),
-            scratch_shapes=[pltpu.VMEM(arrived.shape, F32)],
-        ),
+        scratch_shapes=[pltpu.VMEM(arrived.shape, F32)],
         cost_estimate=pl.CostEstimate(flops=400_000_000, bytes_accessed=2_000_000, transcendentals=0),
         compiler_params=pltpu.CompilerParams(vmem_limit_bytes=12 * MIB),
         name="analysis",
-    )(parity, arrived, control, sigma, *table)
+    )(arrived, control, sigma, *table)
 
 
 def shards(
@@ -627,7 +610,6 @@
     legendre = legendre_np(wave_count, lat_count)
     zonal = zonal_np(lat_count, lon_count)
     turns = turn_np(lat_count, lon_count)
-    parity = (lax.axis_index("tp") % 2).astype(jnp.int32).reshape(1)
     send = synthesis(control, spec_sigma, w_in, w_out.T, legendre)
     got = lax.all_to_all(send, "tp", split_axis=0, concat_axis=0, tiled=True)
     obs = pack_obs(
@@ -639,14 +621,14 @@
     send = regroup(got, obs).reshape(BANDS, 16, LANES)
     arrived = lax.all_to_all(send, "band", split_axis=0, concat_axis=0, tiled=True)
     other = lax.ppermute(got, "band", [(i, i ^ 1) for i in range(BANDS)])
-    prepared = prepare(got, other, (turns,))
+    prepared = prepare(got, other, (turns, *zonal[:2]))
     prior = jnp.pad(prior_mean_field[:, 0, :], ((0, ROWS - channels), (0, 0)))
     prior = jnp.concatenate([prior, prior[:, : WIDTH - STRIDE]], axis=1)
     prior = jnp.stack([prior[:, a * STRIDE : a * STRIDE + WIDTH] for a in range(BLOCKS)])
     gains = jnp.broadcast_to(
         jnp.pad(magnitude_factor, (0, ROWS - channels))[:, None], (ROWS, WIDTH)
     )
-    modes = run_cycle(channels, arrived, prior, gains, prepared, zonal)
+    modes = run_cycle(channels, arrived, prior, gains, prepared, zonal[2:])
     modes = lax.all_to_all(
         modes.reshape(lat_count, 2, LANES),
         ("band", "tp"),
@@ -655,7 +637,7 @@
         tiled=True,
     )
     modes = modes.reshape(2 * lat_count, LANES)
-    return analysis(parity, modes, control, spec_sigma, legendre)
+    return analysis(modes, control, spec_sigma, legendre)
 
 
 def solution(mesh):

time: 90.5 us -> 89.4 us (0.988)
  blocking collectives: 0 us -> 26.3 us
  waiting for transfers between devices: 33.2 us -> 15.5 us
  starting transfers between devices: 35 us -> 26 us
    all_to_all x0 -> x1, blocking collectives: none -> 26.3 us  [shards(): lax.all_to_all(modes.reshape(lat_count, 2, LANES), ('band', 'tp'), split_...]
    all_to_all x1 -> x0, waiting for transfers between devices: 17 us -> none  [shards(): lax.all_to_all(modes.reshape(lat_count, 2, LANES), ('band', 'tp'), split_...]
    all_to_all x1 -> x0, starting transfers between devices: 9 us -> none  [shards(): lax.all_to_all(modes.reshape(lat_count, 2, LANES), ('band', 'tp'), split_...]
    pallas_call x1, Pallas kernels: 12.8 us -> 11.5 us  [run_cycle(): pl.pallas_call(lambda *refs: cycle_kernel(channels, *refs), out_shape=jax...]
  transfers between devices with their start and end apart: 4 -> 3, of which waited for: 4 -> 3; matrix products, arithmetic and copies ran while one was open for 1% -> 1% of each run, Pallas kernels for 2% -> 3%
where the time goes in v6:
time: 89.4 us; the launch traced here: 89 us
  blocking collectives  26.3 us (29%)
  starting transfers between devices  26 us (29%)
  Pallas kernels  19 us (21%)
  waiting for transfers between devices  15.5 us (17%)
  local copies, waits for them, and re-layouts  1.82 us (2%)
    all_to_all x1, blocking collectives, shards(): lax.all_to_all(modes.reshape(lat_count, 2, LANES), ('band', 'tp'), split_...  26.3 us
    all_to_all x1, starting transfers between devices, shards(): lax.all_to_all(send, 'band', split_axis=0, concat_axis=0, tiled=True)  12.6 us
    pallas_call x1, Pallas kernels, run_cycle(): pl.pallas_call(lambda *refs: cycle_kernel(channels, *refs), out_shape=jax...  11.5 us
    all_to_all x1, starting transfers between devices, shards(): got = lax.all_to_all(send, 'tp', split_axis=0, concat_axis=0, tiled=True)  11 us
    all_to_all x1, waiting for transfers between devices, shards(): got = lax.all_to_all(send, 'tp', split_axis=0, concat_axis=0, tiled=True)  8.36 us
    all_to_all x1, waiting for transfers between devices, shards(): lax.all_to_all(send, 'band', split_axis=0, concat_axis=0, tiled=True)  6.89 us
    pallas_call x1, Pallas kernels, synthesis(): pl.pallas_call(synthesis_kernel, out_shape=jax.ShapeDtypeStruct((TPS, SEN...  2.65 us
    ppermute x1, starting transfers between devices, shards(): other = lax.ppermute(got, 'band', [(i, i ^ 1) for i in range(BANDS)])  2.36 us
  transfers between devices with their start and end apart: 3, of which 3 were waited for; matrix products, arithmetic and copies ran while one was open for 1% of the time, Pallas kernels for 3%

profile of v6, /device:TPU:1, one launch (start us, length us, event | category | flops | bytes accessed | tf_op | source)
XLA Modules:
  0.0 89.0 jit_solution(6455932367991882471)
XLA Ops:
  0.0 2.6 %synthesis.1 = bf16[8,128,128]{2,1,0:T(8,128)(2,1)} custom-call(f32[69,2,1,384]{3,2,1,0:T(1,128)} %control.1, f32[69,1,384]{2,1,0:T(1,128)} %sigma.1, bf16[2,512,384]{2,1,0:T(8,128)(2,1)} %constant.17.clone.high_hbm.table_high, bf16[2,512,384]{2,1,0:T(8,128)(2,1)} %constant.18.clone.low_hbm.table_low, bf16[69,96]{1,0:T(8,128)(2,1)} %w_in_hbm.1, ...), custom_call_target="tpu_custom_call" | custom-call | flops 400000000 | bytes 2000000 | tf_op jit(solution)/shard_map/synthesis/pallas_call | solution.py:178
  2.7 0.0 copy-start.9
  2.7 11.0 %all-to-all-start = ((bf16[8,128,128]{2,1,0:T(8,128)(2,1)}), bf16[8,128,128]{2,1,0:T(8,128)(2,1)S(1)}, u32[]{:S(2)}, u32[]{:S(2)}) async-start(bf16[8,128,128]{2,1,0:T(8,128)(2,1)} %synthesis.1), calls=%async_computation | async-start | bytes 524288 | tf_op jit(solution)/shard_map/all_to_all | solution.py:614
  13.7 0.0 copy-done.9
  13.7 0.0 copy-start.6
  13.7 0.0 copy-start.7
  13.7 0.0 copy-start.8
  13.8 0.0 copy-start.5
  13.8 0.0 copy-start.4
  13.8 0.6 copy-done.6
  14.4 0.0 copy-done.7
  14.4 0.0 copy-done.8
  14.4 0.0 copy-done.5
  14.4 0.0 copy-done.4
  14.5 1.1 %pack_obs.1.obs = f32[64,1024]{1,0:T(8,128)S(1)} custom-call(s32[8,128]{1,0:T(8,128)S(1)} %bitcast.28, s32[8,128]{1,0:T(8,128)S(1)} %bitcast.29, f32[8,128]{1,0:T(8,128)S(1)} %bitcast.30, f32[8,128]{1,0:T(8,128)S(1)} %bitcast.31, f32[8,128]{1,0:T(8,128)S(1)} %bitcast.32), custom_call_target="tpu_custom_call" | custom-call | flops 200000000 | bytes 300000 | tf_op jit(solution)/shard_map/pack_obs/pallas_call | solution.py:233
  15.6 0.1 bitcast_dynamic-update-slice_fusion.3
  15.7 8.4 %all-to-all-done.arrived.own = bf16[8,128,128]{2,1,0:T(8,128)(2,1)S(1)} async-done(((bf16[8,128,128]{2,1,0:T(8,128)(2,1)}), bf16[8,128,128]{2,1,0:T(8,128)(2,1)S(1)}, u32[]{:S(2)}, u32[]{:S(2)}) %all-to-all-start) | async-done | bytes 262176 | tf_op jit(solution)/shard_map/all_to_all | solution.py:614
  24.0 0.9 %regroup.1 = bf16[1024,128]{1,0:T(8,128)(2,1)} custom-call(bf16[8,128,128]{2,1,0:T(8,128)(2,1)S(1)} %all-to-all-done.arrived.own, f32[64,1024]{1,0:T(8,128)S(1)} %pack_obs.1.obs), custom_call_target="tpu_custom_call" | custom-call | flops 300000 | bytes 800000 | tf_op jit(solution)/shard_map/regroup/pallas_call | solution.py:253
  25.0 12.6 %all-to-all-start.1 = ((bf16[64,16,128]{2,1,0:T(8,128)(2,1)}), bf16[64,16,128]{2,1,0:T(8,128)(2,1)S(1)}, u32[]{:S(2)}, u32[]{:S(2)}) async-start(bf16[64,16,128]{2,1,0:T(8,128)(2,1)} %bitcast.6), calls=%async_computation.1 | async-start | bytes 524288 | tf_op jit(solution)/shard_map/all_to_all | solution.py:622
  37.6 0.1 bitcast_dynamic-update-slice_fusion.2
  37.7 0.1 bitcast_dynamic-update-slice_fusion.1
  37.7 2.4 %collective-permute-start = (bf16[8,128,128]{2,1,0:T(8,128)(2,1)S(1)}, bf16[8,128,128]{2,1,0:T(8,128)(2,1)S(1)}, u32[]{:S(2)}, u32[]{:S(2)}) collective-permute-start(bf16[8,128,128]{2,1,0:T(8,128)(2,1)S(1)} %all-to-all-done.arrived.own), channel_id=1, source_target_pairs={{0,8},{8,0},{16,24},{24,16},{32,40},{40,32},{48,56},{56,48},{64,72... | collective-permute-start | bytes 786440 | tf_op jit(solution)/shard_map/ppermute | solution.py:623
  40.1 0.0 copy-start.11
  40.2 0.6 copy-done.11
  40.8 0.1 bitcast_dynamic-update-slice_fusion
  40.9 0.1 fusion.1.refs_9_
  41.0 0.0 copy-start.10
  41.0 0.3 collective-permute-done.other
  41.3 1.4 %prepare.1 = (bf16[80,768]{1,0:T(8,128)(2,1)S(1)}, bf16[768,128]{1,0:T(8,128)(2,1)S(1)}, bf16[80,768]{1,0:T(8,128)(2,1)S(1)}, bf16[768,128]{1,0:T(8,128)(2,1)S(1...) custom-call(bf16[8,128,128]{2,1,0:T(8,128)(2,1)S(1)} %all-to-all-done.arrived.own, ...), custom_call_target="tpu_custom_call" | custom-call | flops 1000000 | bytes 5000000 | tf_op jit(solution)/shard_map/prepare/pallas_call | solution.py:300
  42.7 0.0 copy-done.10
  42.7 6.9 %all-to-all-done.1.refs_0_ = bf16[64,16,128]{2,1,0:T(8,128)(2,1)S(1)} async-done(((bf16[64,16,128]{2,1,0:T(8,128)(2,1)}), bf16[64,16,128]{2,1,0:T(8,128)(2,1)S(1)}, u32[]{:S(2)}, u32[]{:S(2)}) %all-to-all-start.1) | async-done | bytes 262176 | tf_op jit(solution)/shard_map/all_to_all | solution.py:622
  49.6 0.1 broadcast_in_dim.2.refs_1_
  49.6 0.0 copy-start
  49.6 0.0 copy-start.1
  49.7 11.5 %cycle.1 = bf16[1024,128]{1,0:T(8,128)(2,1)S(1)} custom-call(bf16[64,16,128]{2,1,0:T(8,128)(2,1)S(1)} %all-to-all-done.1.refs_0_, f32[72,256]{1,0:T(8,128)S(1)} %broadcast_in_dim.2.refs_1_, bf16[80,768]{1,0:T(8,128)(2,1)S(1)} %get-tuple-element.12.refs_2_, bf16[768,128]{1,0:T(8,128)(2,1)S(1)} %get-tuple-element.13.refs_3_, ...), custom_call_target="tpu_custom_call" | custom-call | flops 8000000000 | bytes 4000000 | tf_op jit(solution)/shard_map/cycle/pallas_call | solution.py:543
  61.2 0.0 copy-start.2
  61.2 0.0 copy-start.3
  61.2 26.3 %all_to_all.15 = bf16[512,2,128]{2,1,0:T(2,128)(2,1)S(1)} all-to-all(bf16[512,2,128]{2,1,0:T(2,128)(2,1)S(1)} %bitcast.27), channel_id=1, replica_groups=mesh['band'=64,'tp'=8] {'band','tp'}, dimensions={0} | all-to-all | bytes 524288 | tf_op jit(solution)/shard_map/all_to_all | solution.py:632
  87.5 0.0 copy-done
  87.5 0.0 copy-done.1
  87.5 0.0 copy-done.2
  87.5 0.0 copy-done.3
  87.6 1.4 %analysis.1 = f32[69,2,1,384]{3,2,1,0:T(1,128)} custom-call(bf16[1024,128]{1,0:T(8,128)(2,1)S(1)} %bitcast.26, f32[69,2,1,384]{3,2,1,0:T(1,128)S(1)} %copy-done.2, f32[69,1,384]{2,1,0:T(1,128)S(1)} %copy-done.3, bf16[2,512,384]{2,1,0:T(8,128)(2,1)S(1)} %copy-done, bf16[2,512,384]{2,1,0:T(8,128)(2,1)S(1)} %copy-done.1), custom_call_target="tpu_custom_call" | custom-call | flops 400000000 | bytes 2000000 | tf_op jit(solution)/shard_map/analysis/pallas_call | solution.py:584
  (5 shorter events, 0.1 us)
Async XLA Ops:
  2.7 11.0 %copy-start.9 = (f32[69,1,1440]{2,1,0:T(1,128)S(1)}, f32[69,1,1440]{2,1,0:T(1,128)}, u32[]{:S(2)}) copy-start(f32[69,1,1440]{2,1,0:T(1,128)} %param.20) | copy-start | bytes 1192324
  2.7 21.4 %all-to-all-start = ((bf16[8,128,128]{2,1,0:T(8,128)(2,1)}), bf16[8,128,128]{2,1,0:T(8,128)(2,1)S(1)}, u32[]{:S(2)}, u32[]{:S(2)}) async-start(bf16[8,128,128]{2,1,0:T(8,128)(2,1)} %synthesis.1), calls=%async_computation | async-start | bytes 524288 | tf_op jit(solution)/shard_map/all_to_all | solution.py:614
  13.7 0.7 copy-start.6
  13.7 0.7 copy-start.7
  13.7 0.7 copy-start.8
  13.8 0.7 copy-start.5
  13.8 0.7 copy-start.4
  25.0 24.6 %all-to-all-start.1 = ((bf16[64,16,128]{2,1,0:T(8,128)(2,1)}), bf16[64,16,128]{2,1,0:T(8,128)(2,1)S(1)}, u32[]{:S(2)}, u32[]{:S(2)}) async-start(bf16[64,16,128]{2,1,0:T(8,128)(2,1)} %bitcast.6), calls=%async_computation.1 | async-start | bytes 524288 | tf_op jit(solution)/shard_map/all_to_all | solution.py:622
  37.7 3.5 %collective-permute-start = (bf16[8,128,128]{2,1,0:T(8,128)(2,1)S(1)}, bf16[8,128,128]{2,1,0:T(8,128)(2,1)S(1)}, u32[]{:S(2)}, u32[]{:S(2)}) collective-permute-start(bf16[8,128,128]{2,1,0:T(8,128)(2,1)S(1)} %all-to-all-done.arrived.own), channel_id=1, source_target_pairs={{0,8},{8,0},{16,24},{24,16},{32,40},{40,32},{48,56},{56,48},{64,72... | collective-permute-start | bytes 786440 | tf_op jit(solution)/shard_map/ppermute | solution.py:623
  40.1 0.7 copy-start.11
  41.0 1.7 %copy-start.10 = (f32[6,72,256]{2,1,0:T(8,128)}, f32[6,72,256]{2,1,0:T(8,128)S(1)}, u32[]{:S(2)}) copy-start(f32[6,72,256]{2,1,0:T(8,128)S(1)} %fusion.1.refs_9_) | copy-start | bytes 1327108
  49.6 37.9 %copy-start = (bf16[2,512,384]{2,1,0:T(8,128)(2,1)S(1)}, bf16[2,512,384]{2,1,0:T(8,128)(2,1)}, u32[]{:S(2)}) copy-start(bf16[2,512,384]{2,1,0:T(8,128)(2,1)} %constant.17.clone.high_hbm.table_high) | copy-start | bytes 2359300
  49.6 37.9 %copy-start.1 = (bf16[2,512,384]{2,1,0:T(8,128)(2,1)S(1)}, bf16[2,512,384]{2,1,0:T(8,128)(2,1)}, u32[]{:S(2)}) copy-start(bf16[2,512,384]{2,1,0:T(8,128)(2,1)} %constant.18.clone.low_hbm.table_low) | copy-start | bytes 2359300
  61.2 26.4 %copy-start.2 = (f32[69,2,1,384]{3,2,1,0:T(1,128)S(1)}, f32[69,2,1,384]{3,2,1,0:T(1,128)}, u32[]{:S(2)}) copy-start(f32[69,2,1,384]{3,2,1,0:T(1,128)} %control.1) | copy-start | bytes 635908
  61.2 26.4 %copy-start.3 = (f32[69,1,384]{2,1,0:T(1,128)S(1)}, f32[69,1,384]{2,1,0:T(1,128)}, u32[]{:S(2)}) copy-start(f32[69,1,384]{2,1,0:T(1,128)} %sigma.1) | copy-start | bytes 317956

commit v7 on v6

--- a/solution.py
+++ b/solution.py
@@ -25,6 +25,7 @@
 FIELDS = 8
 ROW_SHIFT = 256
 OBS_CHUNK = 512
+GROUP = 2
 MIB = 1024 * 1024
 
 
@@ -400,19 +401,23 @@
     state[...] = prior[...].reshape(BLOCKS * ROWS, WIDTH) + field
 
     forecast = []
-    for a in range(BLOCKS):
-        field = state[a * ROWS : (a + 1) * ROWS, :]
+    gain = jnp.concatenate([gains[...]] * GROUP, axis=1)
+    groups = [range(a, a + GROUP) for a in range(0, BLOCKS, GROUP)]
+    for g, group in enumerate(groups):
+        field = [state[a * ROWS : (a + 1) * ROWS, :] for a in group]
+        field = jnp.concatenate(field, axis=1)
         mean_sq = jnp.sum(field * field, axis=0, keepdims=True) * (1.0 / channels)
-        unit = (field * gains[...] * lax.rsqrt(mean_sq + EPSILON)).astype(BF16)
+        unit = (field * gain * lax.rsqrt(mean_sq + EPSILON)).astype(BF16)
         pre = dot(in_columns[:, 0:ROWS], unit)
         square = pre * pre
         inner = pre * (GELU_SCALE + (GELU_SCALE * GELU_CUBE) * square)
         gate = 0.5 + 0.5 * jnp.tanh(inner)
         hidden = pre * gate
-        slopes[a] = gate + hidden * (1.0 - gate) * (
+        slopes[g] = gate + hidden * (1.0 - gate) * (
             2.0 * GELU_SCALE + (6.0 * GELU_SCALE * GELU_CUBE) * square
         )
-        forecast.append(field + dot(out_rows[...], hidden.astype(BF16))[0:ROWS])
+        ahead = field + dot(out_rows[...], hidden.astype(BF16))[0:ROWS]
+        forecast += [ahead[:, i * WIDTH : (i + 1) * WIDTH] for i in range(GROUP)]
     forecast = split(jnp.concatenate(forecast, axis=0).T)
     forecast = jnp.concatenate(forecast, axis=0)
 
@@ -500,17 +505,20 @@
     halo = jnp.concatenate([halo[(BLOCKS - 1) * ROWS :], halo[: (BLOCKS - 1) * ROWS]], axis=0)
     forcing = jnp.where(lanes < STRIDE, forcing, 0.0) + jnp.where(lanes < 3, halo, 0.0)
     costate = []
-    for a in range(BLOCKS):
-        force = forcing[a * ROWS : (a + 1) * ROWS]
+    for g, group in enumerate(groups):
+        force = [forcing[a * ROWS : (a + 1) * ROWS] for a in group]
+        force = jnp.concatenate(force, axis=1)
         grad_hidden = dot(out_columns[:, 0:ROWS], force.astype(BF16))
-        grad_pre = (grad_hidden * slopes[a]).astype(BF16)
+        grad_pre = (grad_hidden * slopes[g]).astype(BF16)
         grad_unit = dot(in_rows[...], grad_pre)[0:ROWS]
-        field = state[a * ROWS : (a + 1) * ROWS, :]
+        field = [state[a * ROWS : (a + 1) * ROWS, :] for a in group]
+        field = jnp.concatenate(field, axis=1)
         mean_sq = jnp.sum(field * field, axis=0, keepdims=True) * (1.0 / channels)
         inverse = lax.rsqrt(mean_sq + EPSILON)
-        scaled = grad_unit * gains[...]
+        scaled = grad_unit * gain
         along = jnp.sum(scaled * field, axis=0, keepdims=True) * (1.0 / channels)
-        costate.append(force + scaled * inverse - field * (along * inverse * inverse * inverse))
+        total = force + scaled * inverse - field * (along * inverse * inverse * inverse)
+        costate += [total[:, i * WIDTH : (i + 1) * WIDTH] for i in range(GROUP)]
     near = jnp.concatenate(costate[:PAIRS], axis=0)
     far = jnp.concatenate(costate[PAIRS:], axis=0)
     for copy in copies[1:]:
@@ -550,7 +558,7 @@
             *(pltpu.VMEM(part.shape, BF16) for part in wide),
             pltpu.SemaphoreType.DMA((3,)),
             pltpu.VMEM((BLOCKS * ROWS, WIDTH), F32),
-            pltpu.VMEM((BLOCKS, hidden, WIDTH), F32),
+            pltpu.VMEM((BLOCKS // GROUP, hidden, GROUP * WIDTH), F32),
             pltpu.VMEM((BANDS // 2, FIELDS, LANES), F32),
             pltpu.VMEM((BLOCKS * ROWS, BANDS * SLOTS), BF16),
             pltpu.VMEM((2 * WIDTH, BANDS * SLOTS), BF16),

time: 89.4 us -> 88.2 us (0.987)
  Pallas kernels: 19 us -> 17.8 us
    pallas_call x1, Pallas kernels: 11.5 us -> 10.3 us  [run_cycle(): pl.pallas_call(lambda *refs: cycle_kernel(channels, *refs), out_shape=jax...]
where the time goes in v7:
time: 88.2 us; the launch traced here: 87.7 us
  blocking collectives  26.4 us (30%)
  starting transfers between devices  26 us (29%)
  Pallas kernels  17.8 us (20%)
  waiting for transfers between devices  15.5 us (18%)
  local copies, waits for them, and re-layouts  1.82 us (2%)
    all_to_all x1, blocking collectives, shards(): lax.all_to_all(modes.reshape(lat_count, 2, LANES), ('band', 'tp'), split_...  26.4 us
    all_to_all x1, starting transfers between devices, shards(): lax.all_to_all(send, 'band', split_axis=0, concat_axis=0, tiled=True)  12.6 us
    all_to_all x1, starting transfers between devices, shards(): got = lax.all_to_all(send, 'tp', split_axis=0, concat_axis=0, tiled=True)  11 us
    pallas_call x1, Pallas kernels, run_cycle(): pl.pallas_call(lambda *refs: cycle_kernel(channels, *refs), out_shape=jax...  10.3 us
    all_to_all x1, waiting for transfers between devices, shards(): got = lax.all_to_all(send, 'tp', split_axis=0, concat_axis=0, tiled=True)  8.36 us
    all_to_all x1, waiting for transfers between devices, shards(): lax.all_to_all(send, 'band', split_axis=0, concat_axis=0, tiled=True)  6.89 us
    pallas_call x1, Pallas kernels, synthesis(): pl.pallas_call(synthesis_kernel, out_shape=jax.ShapeDtypeStruct((TPS, SEN...  2.65 us
    ppermute x1, starting transfers between devices, shards(): other = lax.ppermute(got, 'band', [(i, i ^ 1) for i in range(BANDS)])  2.36 us
  transfers between devices with their start and end apart: 3, of which 3 were waited for; matrix products, arithmetic and copies ran while one was open for 1% of the time, Pallas kernels for 3%

profile of v7, /device:TPU:1, one launch (start us, length us, event | category | flops | bytes accessed | tf_op | source)
XLA Modules:
  0.0 87.7 jit_solution(11867827362151195865)
XLA Ops:
  0.0 2.6 %synthesis.1 = bf16[8,128,128]{2,1,0:T(8,128)(2,1)} custom-call(f32[69,2,1,384]{3,2,1,0:T(1,128)} %control.1, f32[69,1,384]{2,1,0:T(1,128)} %sigma.1, bf16[2,512,384]{2,1,0:T(8,128)(2,1)} %constant.17.clone.high_hbm.table_high, bf16[2,512,384]{2,1,0:T(8,128)(2,1)} %constant.18.clone.low_hbm.table_low, bf16[69,96]{1,0:T(8,128)(2,1)} %w_in_hbm.1, ...), custom_call_target="tpu_custom_call" | custom-call | flops 400000000 | bytes 2000000 | tf_op jit(solution)/shard_map/synthesis/pallas_call | solution.py:179
  2.7 0.0 copy-start.9
  2.7 11.0 %all-to-all-start = ((bf16[8,128,128]{2,1,0:T(8,128)(2,1)}), bf16[8,128,128]{2,1,0:T(8,128)(2,1)S(1)}, u32[]{:S(2)}, u32[]{:S(2)}) async-start(bf16[8,128,128]{2,1,0:T(8,128)(2,1)} %synthesis.1), calls=%async_computation | async-start | bytes 524288 | tf_op jit(solution)/shard_map/all_to_all | solution.py:622
  13.7 0.0 copy-done.9
  13.7 0.0 copy-start.6
  13.7 0.0 copy-start.7
  13.7 0.0 copy-start.8
  13.8 0.0 copy-start.5
  13.8 0.0 copy-start.4
  13.8 0.6 copy-done.6
  14.4 0.0 copy-done.7
  14.4 0.0 copy-done.8
  14.4 0.0 copy-done.5
  14.4 0.0 copy-done.4
  14.5 1.1 %pack_obs.1.obs = f32[64,1024]{1,0:T(8,128)S(1)} custom-call(s32[8,128]{1,0:T(8,128)S(1)} %bitcast.28, s32[8,128]{1,0:T(8,128)S(1)} %bitcast.29, f32[8,128]{1,0:T(8,128)S(1)} %bitcast.30, f32[8,128]{1,0:T(8,128)S(1)} %bitcast.31, f32[8,128]{1,0:T(8,128)S(1)} %bitcast.32), custom_call_target="tpu_custom_call" | custom-call | flops 200000000 | bytes 300000 | tf_op jit(solution)/shard_map/pack_obs/pallas_call | solution.py:234
  15.6 0.1 bitcast_dynamic-update-slice_fusion.3
  15.7 8.4 %all-to-all-done.arrived.own = bf16[8,128,128]{2,1,0:T(8,128)(2,1)S(1)} async-done(((bf16[8,128,128]{2,1,0:T(8,128)(2,1)}), bf16[8,128,128]{2,1,0:T(8,128)(2,1)S(1)}, u32[]{:S(2)}, u32[]{:S(2)}) %all-to-all-start) | async-done | bytes 262176 | tf_op jit(solution)/shard_map/all_to_all | solution.py:622
  24.0 0.9 %regroup.1 = bf16[1024,128]{1,0:T(8,128)(2,1)} custom-call(bf16[8,128,128]{2,1,0:T(8,128)(2,1)S(1)} %all-to-all-done.arrived.own, f32[64,1024]{1,0:T(8,128)S(1)} %pack_obs.1.obs), custom_call_target="tpu_custom_call" | custom-call | flops 300000 | bytes 800000 | tf_op jit(solution)/shard_map/regroup/pallas_call | solution.py:254
  25.0 12.6 %all-to-all-start.1 = ((bf16[64,16,128]{2,1,0:T(8,128)(2,1)}), bf16[64,16,128]{2,1,0:T(8,128)(2,1)S(1)}, u32[]{:S(2)}, u32[]{:S(2)}) async-start(bf16[64,16,128]{2,1,0:T(8,128)(2,1)} %bitcast.6), calls=%async_computation.1 | async-start | bytes 524288 | tf_op jit(solution)/shard_map/all_to_all | solution.py:630
  37.6 0.1 bitcast_dynamic-update-slice_fusion.2
  37.7 0.1 bitcast_dynamic-update-slice_fusion.1
  37.7 2.4 %collective-permute-start = (bf16[8,128,128]{2,1,0:T(8,128)(2,1)S(1)}, bf16[8,128,128]{2,1,0:T(8,128)(2,1)S(1)}, u32[]{:S(2)}, u32[]{:S(2)}) collective-permute-start(bf16[8,128,128]{2,1,0:T(8,128)(2,1)S(1)} %all-to-all-done.arrived.own), channel_id=1, source_target_pairs={{0,8},{8,0},{16,24},{24,16},{32,40},{40,32},{48,56},{56,48},{64,72... | collective-permute-start | bytes 786440 | tf_op jit(solution)/shard_map/ppermute | solution.py:631
  40.1 0.0 copy-start.11
  40.2 0.6 copy-done.11
  40.8 0.1 bitcast_dynamic-update-slice_fusion
  40.9 0.1 fusion.1.refs_9_
  41.0 0.0 copy-start.10
  41.0 0.3 collective-permute-done.other
  41.3 1.4 %prepare.1 = (bf16[80,768]{1,0:T(8,128)(2,1)S(1)}, bf16[768,128]{1,0:T(8,128)(2,1)S(1)}, bf16[80,768]{1,0:T(8,128)(2,1)S(1)}, bf16[768,128]{1,0:T(8,128)(2,1)S(1...) custom-call(bf16[8,128,128]{2,1,0:T(8,128)(2,1)S(1)} %all-to-all-done.arrived.own, ...), custom_call_target="tpu_custom_call" | custom-call | flops 1000000 | bytes 5000000 | tf_op jit(solution)/shard_map/prepare/pallas_call | solution.py:301
  42.7 0.0 copy-done.10
  42.7 6.9 %all-to-all-done.1.refs_0_ = bf16[64,16,128]{2,1,0:T(8,128)(2,1)S(1)} async-done(((bf16[64,16,128]{2,1,0:T(8,128)(2,1)}), bf16[64,16,128]{2,1,0:T(8,128)(2,1)S(1)}, u32[]{:S(2)}, u32[]{:S(2)}) %all-to-all-start.1) | async-done | bytes 262176 | tf_op jit(solution)/shard_map/all_to_all | solution.py:630
  49.6 0.1 broadcast_in_dim.2.refs_1_
  49.6 0.0 copy-start
  49.6 0.0 copy-start.1
  49.7 10.3 %cycle.1 = bf16[1024,128]{1,0:T(8,128)(2,1)S(1)} custom-call(bf16[64,16,128]{2,1,0:T(8,128)(2,1)S(1)} %all-to-all-done.1.refs_0_, f32[72,256]{1,0:T(8,128)S(1)} %broadcast_in_dim.2.refs_1_, bf16[80,768]{1,0:T(8,128)(2,1)S(1)} %get-tuple-element.12.refs_2_, bf16[768,128]{1,0:T(8,128)(2,1)S(1)} %get-tuple-element.13.refs_3_, ...), custom_call_target="tpu_custom_call" | custom-call | flops 8000000000 | bytes 4000000 | tf_op jit(solution)/shard_map/cycle/pallas_call | solution.py:551
  59.9 0.0 copy-start.2
  59.9 0.0 copy-start.3
  60.0 26.4 %all_to_all.15 = bf16[512,2,128]{2,1,0:T(2,128)(2,1)S(1)} all-to-all(bf16[512,2,128]{2,1,0:T(2,128)(2,1)S(1)} %bitcast.27), channel_id=1, replica_groups=mesh['band'=64,'tp'=8] {'band','tp'}, dimensions={0} | all-to-all | bytes 524288 | tf_op jit(solution)/shard_map/all_to_all | solution.py:640
  86.3 0.0 copy-done
  86.3 0.0 copy-done.1
  86.3 0.0 copy-done.2
  86.3 0.0 copy-done.3
  86.3 1.4 %analysis.1 = f32[69,2,1,384]{3,2,1,0:T(1,128)} custom-call(bf16[1024,128]{1,0:T(8,128)(2,1)S(1)} %bitcast.26, f32[69,2,1,384]{3,2,1,0:T(1,128)S(1)} %copy-done.2, f32[69,1,384]{2,1,0:T(1,128)S(1)} %copy-done.3, bf16[2,512,384]{2,1,0:T(8,128)(2,1)S(1)} %copy-done, bf16[2,512,384]{2,1,0:T(8,128)(2,1)S(1)} %copy-done.1), custom_call_target="tpu_custom_call" | custom-call | flops 400000000 | bytes 2000000 | tf_op jit(solution)/shard_map/analysis/pallas_call | solution.py:592
  (5 shorter events, 0.1 us)
Async XLA Ops:
  2.7 11.0 %copy-start.9 = (f32[69,1,1440]{2,1,0:T(1,128)S(1)}, f32[69,1,1440]{2,1,0:T(1,128)}, u32[]{:S(2)}) copy-start(f32[69,1,1440]{2,1,0:T(1,128)} %param.20) | copy-start | bytes 1192324
  2.7 21.4 %all-to-all-start = ((bf16[8,128,128]{2,1,0:T(8,128)(2,1)}), bf16[8,128,128]{2,1,0:T(8,128)(2,1)S(1)}, u32[]{:S(2)}, u32[]{:S(2)}) async-start(bf16[8,128,128]{2,1,0:T(8,128)(2,1)} %synthesis.1), calls=%async_computation | async-start | bytes 524288 | tf_op jit(solution)/shard_map/all_to_all | solution.py:622
  13.7 0.7 copy-start.6
  13.7 0.7 copy-start.7
  13.7 0.7 copy-start.8
  13.8 0.7 copy-start.5
  13.8 0.7 copy-start.4
  25.0 24.6 %all-to-all-start.1 = ((bf16[64,16,128]{2,1,0:T(8,128)(2,1)}), bf16[64,16,128]{2,1,0:T(8,128)(2,1)S(1)}, u32[]{:S(2)}, u32[]{:S(2)}) async-start(bf16[64,16,128]{2,1,0:T(8,128)(2,1)} %bitcast.6), calls=%async_computation.1 | async-start | bytes 524288 | tf_op jit(solution)/shard_map/all_to_all | solution.py:630
  37.7 3.5 %collective-permute-start = (bf16[8,128,128]{2,1,0:T(8,128)(2,1)S(1)}, bf16[8,128,128]{2,1,0:T(8,128)(2,1)S(1)}, u32[]{:S(2)}, u32[]{:S(2)}) collective-permute-start(bf16[8,128,128]{2,1,0:T(8,128)(2,1)S(1)} %all-to-all-done.arrived.own), channel_id=1, source_target_pairs={{0,8},{8,0},{16,24},{24,16},{32,40},{40,32},{48,56},{56,48},{64,72... | collective-permute-start | bytes 786440 | tf_op jit(solution)/shard_map/ppermute | solution.py:631
  40.1 0.7 copy-start.11
  41.0 1.7 %copy-start.10 = (f32[6,72,256]{2,1,0:T(8,128)}, f32[6,72,256]{2,1,0:T(8,128)S(1)}, u32[]{:S(2)}) copy-start(f32[6,72,256]{2,1,0:T(8,128)S(1)} %fusion.1.refs_9_) | copy-start | bytes 1327108
  49.6 36.7 %copy-start = (bf16[2,512,384]{2,1,0:T(8,128)(2,1)S(1)}, bf16[2,512,384]{2,1,0:T(8,128)(2,1)}, u32[]{:S(2)}) copy-start(bf16[2,512,384]{2,1,0:T(8,128)(2,1)} %constant.17.clone.high_hbm.table_high) | copy-start | bytes 2359300
  49.6 36.7 %copy-start.1 = (bf16[2,512,384]{2,1,0:T(8,128)(2,1)S(1)}, bf16[2,512,384]{2,1,0:T(8,128)(2,1)}, u32[]{:S(2)}) copy-start(bf16[2,512,384]{2,1,0:T(8,128)(2,1)} %constant.18.clone.low_hbm.table_low) | copy-start | bytes 2359300
  59.9 26.4 %copy-start.2 = (f32[69,2,1,384]{3,2,1,0:T(1,128)S(1)}, f32[69,2,1,384]{3,2,1,0:T(1,128)}, u32[]{:S(2)}) copy-start(f32[69,2,1,384]{3,2,1,0:T(1,128)} %control.1) | copy-start | bytes 635908
  59.9 26.4 %copy-start.3 = (f32[69,1,384]{2,1,0:T(1,128)S(1)}, f32[69,1,384]{2,1,0:T(1,128)}, u32[]{:S(2)}) copy-start(f32[69,1,384]{2,1,0:T(1,128)} %sigma.1) | copy-start | bytes 317956

commit v8 on v7

--- a/solution.py
+++ b/solution.py
@@ -144,7 +144,8 @@
     parts = split(coef[...])
     for copy in copies[2:]:
         copy.wait()
-    whole = dot3((table_high[...], table_low[...]), parts, NT)
+    whole = dot(table_high[...], jnp.concatenate(parts, axis=0), NT)
+    whole = whole[:, : 2 * LANES] + whole[:, 2 * LANES :] + dot(table_low[...], parts[0], NT)
     modes[0] = whole[:, 0:LANES]
     modes[1] = whole[:, LANES:]
     even = lax.rem(lax.axis_index("band"), 2) == 0
@@ -578,14 +579,18 @@
     orders = arrived.shape[0] // 2
     rows[...] = arrived[...].astype(F32)
     lanes = lane_ids((orders, LANES))
+    grads = []
     for r in range(2):
         both = rows[pl.ds(r, orders, stride=2), :]
         low = pltpu.roll(both, LANES - channels, 1)
         grad = jnp.where(lanes < channels, both, 0.0)
         grad = grad + jnp.where(lanes < LANES - channels, low, 0.0)
-        grad_t = split(grad.T[0:ROWS])
-        projected = dot3(grad_t, (table_high[parity], table_low[parity]))
-        out[:, r, 0, :] = control[:, r, 0, :] + sigma[:, 0, :] * projected[0:channels]
+        grads.append(grad.T[0:ROWS])
+    grads = split(jnp.concatenate(grads, axis=0))
+    projected = dot3(grads, (table_high[parity], table_low[parity]))
+    for r in range(2):
+        step = projected[r * ROWS : r * ROWS + channels]
+        out[:, r, 0, :] = control[:, r, 0, :] + sigma[:, 0, :] * step
 
 
 def analysis(arrived, control, sigma, table):

time: 88.2 us -> 88.2 us (level)
  no operation moved by 1% of the time
where the time goes in v8:
time: 88.2 us; the launch traced here: 87.7 us
  blocking collectives  26.4 us (30%)
  starting transfers between devices  25.9 us (29%)
  Pallas kernels  17.7 us (20%)
  waiting for transfers between devices  15.5 us (18%)
  local copies, waits for them, and re-layouts  1.82 us (2%)
    all_to_all x1, blocking collectives, shards(): lax.all_to_all(modes.reshape(lat_count, 2, LANES), ('band', 'tp'), split_...  26.4 us
    all_to_all x1, starting transfers between devices, shards(): lax.all_to_all(send, 'band', split_axis=0, concat_axis=0, tiled=True)  12.6 us
    all_to_all x1, starting transfers between devices, shards(): got = lax.all_to_all(send, 'tp', split_axis=0, concat_axis=0, tiled=True)  11 us
    pallas_call x1, Pallas kernels, run_cycle(): pl.pallas_call(lambda *refs: cycle_kernel(channels, *refs), out_shape=jax...  10.3 us
    all_to_all x1, waiting for transfers between devices, shards(): got = lax.all_to_all(send, 'tp', split_axis=0, concat_axis=0, tiled=True)  8.39 us
    all_to_all x1, waiting for transfers between devices, shards(): lax.all_to_all(send, 'band', split_axis=0, concat_axis=0, tiled=True)  6.89 us
    pallas_call x1, Pallas kernels, synthesis(): pl.pallas_call(synthesis_kernel, out_shape=jax.ShapeDtypeStruct((TPS, SEN...  2.65 us
    ppermute x1, starting transfers between devices, shards(): other = lax.ppermute(got, 'band', [(i, i ^ 1) for i in range(BANDS)])  2.36 us
  transfers between devices with their start and end apart: 3, of which 3 were waited for; matrix products, arithmetic and copies ran while one was open for 1% of the time, Pallas kernels for 3%

profile of v8, /device:TPU:1, one launch (start us, length us, event | category | flops | bytes accessed | tf_op | source)
XLA Modules:
  0.0 87.7 jit_solution(3505703583640017643)
XLA Ops:
  0.0 2.6 %synthesis.1 = bf16[8,128,128]{2,1,0:T(8,128)(2,1)} custom-call(f32[69,2,1,384]{3,2,1,0:T(1,128)} %control.1, f32[69,1,384]{2,1,0:T(1,128)} %sigma.1, bf16[2,512,384]{2,1,0:T(8,128)(2,1)} %constant.17.clone.high_hbm.table_high, bf16[2,512,384]{2,1,0:T(8,128)(2,1)} %constant.18.clone.low_hbm.table_low, bf16[69,96]{1,0:T(8,128)(2,1)} %w_in_hbm.1, ...), custom_call_target="tpu_custom_call" | custom-call | flops 400000000 | bytes 2000000 | tf_op jit(solution)/shard_map/synthesis/pallas_call | solution.py:180
  2.7 0.0 copy-start.9
  2.7 11.0 %all-to-all-start = ((bf16[8,128,128]{2,1,0:T(8,128)(2,1)}), bf16[8,128,128]{2,1,0:T(8,128)(2,1)S(1)}, u32[]{:S(2)}, u32[]{:S(2)}) async-start(bf16[8,128,128]{2,1,0:T(8,128)(2,1)} %synthesis.1), calls=%async_computation | async-start | bytes 524288 | tf_op jit(solution)/shard_map/all_to_all | solution.py:627
  13.7 0.0 copy-done.9
  13.7 0.0 copy-start.6
  13.7 0.0 copy-start.7
  13.7 0.0 copy-start.8
  13.8 0.0 copy-start.5
  13.8 0.0 copy-start.4
  13.8 0.6 copy-done.6
  14.4 0.0 copy-done.7
  14.4 0.0 copy-done.8
  14.4 0.0 copy-done.5
  14.5 0.0 copy-done.4
  14.5 1.1 %pack_obs.1.obs = f32[64,1024]{1,0:T(8,128)S(1)} custom-call(s32[8,128]{1,0:T(8,128)S(1)} %bitcast.28, s32[8,128]{1,0:T(8,128)S(1)} %bitcast.29, f32[8,128]{1,0:T(8,128)S(1)} %bitcast.30, f32[8,128]{1,0:T(8,128)S(1)} %bitcast.31, f32[8,128]{1,0:T(8,128)S(1)} %bitcast.32), custom_call_target="tpu_custom_call" | custom-call | flops 200000000 | bytes 300000 | tf_op jit(solution)/shard_map/pack_obs/pallas_call | solution.py:235
  15.6 0.1 bitcast_dynamic-update-slice_fusion.3
  15.7 8.4 %all-to-all-done.arrived.own = bf16[8,128,128]{2,1,0:T(8,128)(2,1)S(1)} async-done(((bf16[8,128,128]{2,1,0:T(8,128)(2,1)}), bf16[8,128,128]{2,1,0:T(8,128)(2,1)S(1)}, u32[]{:S(2)}, u32[]{:S(2)}) %all-to-all-start) | async-done | bytes 262176 | tf_op jit(solution)/shard_map/all_to_all | solution.py:627
  24.1 0.9 %regroup.1 = bf16[1024,128]{1,0:T(8,128)(2,1)} custom-call(bf16[8,128,128]{2,1,0:T(8,128)(2,1)S(1)} %all-to-all-done.arrived.own, f32[64,1024]{1,0:T(8,128)S(1)} %pack_obs.1.obs), custom_call_target="tpu_custom_call" | custom-call | flops 300000 | bytes 800000 | tf_op jit(solution)/shard_map/regroup/pallas_call | solution.py:255
  25.0 12.6 %all-to-all-start.1 = ((bf16[64,16,128]{2,1,0:T(8,128)(2,1)}), bf16[64,16,128]{2,1,0:T(8,128)(2,1)S(1)}, u32[]{:S(2)}, u32[]{:S(2)}) async-start(bf16[64,16,128]{2,1,0:T(8,128)(2,1)} %bitcast.6), calls=%async_computation.1 | async-start | bytes 524288 | tf_op jit(solution)/shard_map/all_to_all | solution.py:635
  37.6 0.1 bitcast_dynamic-update-slice_fusion.2
  37.7 0.1 bitcast_dynamic-update-slice_fusion.1
  37.7 2.4 %collective-permute-start = (bf16[8,128,128]{2,1,0:T(8,128)(2,1)S(1)}, bf16[8,128,128]{2,1,0:T(8,128)(2,1)S(1)}, u32[]{:S(2)}, u32[]{:S(2)}) collective-permute-start(bf16[8,128,128]{2,1,0:T(8,128)(2,1)S(1)} %all-to-all-done.arrived.own), channel_id=1, source_target_pairs={{0,8},{8,0},{16,24},{24,16},{32,40},{40,32},{48,56},{56,48},{64,72... | collective-permute-start | bytes 786440 | tf_op jit(solution)/shard_map/ppermute | solution.py:636
  40.1 0.0 copy-start.11
  40.2 0.6 copy-done.11
  40.8 0.1 bitcast_dynamic-update-slice_fusion
  40.9 0.1 fusion.1.refs_9_
  41.0 0.0 copy-start.10
  41.0 0.3 collective-permute-done.other
  41.3 1.4 %prepare.1 = (bf16[80,768]{1,0:T(8,128)(2,1)S(1)}, bf16[768,128]{1,0:T(8,128)(2,1)S(1)}, bf16[80,768]{1,0:T(8,128)(2,1)S(1)}, bf16[768,128]{1,0:T(8,128)(2,1)S(1...) custom-call(bf16[8,128,128]{2,1,0:T(8,128)(2,1)S(1)} %all-to-all-done.arrived.own, ...), custom_call_target="tpu_custom_call" | custom-call | flops 1000000 | bytes 5000000 | tf_op jit(solution)/shard_map/prepare/pallas_call | solution.py:302
  42.7 0.0 copy-done.10
  42.7 6.9 %all-to-all-done.1.refs_0_ = bf16[64,16,128]{2,1,0:T(8,128)(2,1)S(1)} async-done(((bf16[64,16,128]{2,1,0:T(8,128)(2,1)}), bf16[64,16,128]{2,1,0:T(8,128)(2,1)S(1)}, u32[]{:S(2)}, u32[]{:S(2)}) %all-to-all-start.1) | async-done | bytes 262176 | tf_op jit(solution)/shard_map/all_to_all | solution.py:635
  49.6 0.1 broadcast_in_dim.2.refs_1_
  49.6 0.0 copy-start
  49.7 0.0 copy-start.1
  49.7 10.3 %cycle.1 = bf16[1024,128]{1,0:T(8,128)(2,1)S(1)} custom-call(bf16[64,16,128]{2,1,0:T(8,128)(2,1)S(1)} %all-to-all-done.1.refs_0_, f32[72,256]{1,0:T(8,128)S(1)} %broadcast_in_dim.2.refs_1_, bf16[80,768]{1,0:T(8,128)(2,1)S(1)} %get-tuple-element.12.refs_2_, bf16[768,128]{1,0:T(8,128)(2,1)S(1)} %get-tuple-element.13.refs_3_, ...), custom_call_target="tpu_custom_call" | custom-call | flops 8000000000 | bytes 4000000 | tf_op jit(solution)/shard_map/cycle/pallas_call | solution.py:552
  59.9 0.0 copy-start.2
  59.9 0.0 copy-start.3
  59.9 26.4 %all_to_all.15 = bf16[512,2,128]{2,1,0:T(2,128)(2,1)S(1)} all-to-all(bf16[512,2,128]{2,1,0:T(2,128)(2,1)S(1)} %bitcast.27), channel_id=1, replica_groups=mesh['band'=64,'tp'=8] {'band','tp'}, dimensions={0} | all-to-all | bytes 524288 | tf_op jit(solution)/shard_map/all_to_all | solution.py:645
  86.3 0.0 copy-done
  86.3 0.0 copy-done.1
  86.3 0.0 copy-done.2
  86.3 0.0 copy-done.3
  86.3 1.4 %analysis.1 = f32[69,2,1,384]{3,2,1,0:T(1,128)} custom-call(bf16[1024,128]{1,0:T(8,128)(2,1)S(1)} %bitcast.26, f32[69,2,1,384]{3,2,1,0:T(1,128)S(1)} %copy-done.2, f32[69,1,384]{2,1,0:T(1,128)S(1)} %copy-done.3, bf16[2,512,384]{2,1,0:T(8,128)(2,1)S(1)} %copy-done, bf16[2,512,384]{2,1,0:T(8,128)(2,1)S(1)} %copy-done.1), custom_call_target="tpu_custom_call" | custom-call | flops 400000000 | bytes 2000000 | tf_op jit(solution)/shard_map/analysis/pallas_call | solution.py:597
  (5 shorter events, 0.1 us)
Async XLA Ops:
  2.7 11.0 %copy-start.9 = (f32[69,1,1440]{2,1,0:T(1,128)S(1)}, f32[69,1,1440]{2,1,0:T(1,128)}, u32[]{:S(2)}) copy-start(f32[69,1,1440]{2,1,0:T(1,128)} %param.20) | copy-start | bytes 1192324
  2.7 21.4 %all-to-all-start = ((bf16[8,128,128]{2,1,0:T(8,128)(2,1)}), bf16[8,128,128]{2,1,0:T(8,128)(2,1)S(1)}, u32[]{:S(2)}, u32[]{:S(2)}) async-start(bf16[8,128,128]{2,1,0:T(8,128)(2,1)} %synthesis.1), calls=%async_computation | async-start | bytes 524288 | tf_op jit(solution)/shard_map/all_to_all | solution.py:627
  13.7 0.7 copy-start.6
  13.7 0.7 copy-start.7
  13.7 0.7 copy-start.8
  13.8 0.7 copy-start.5
  13.8 0.7 copy-start.4
  25.0 24.6 %all-to-all-start.1 = ((bf16[64,16,128]{2,1,0:T(8,128)(2,1)}), bf16[64,16,128]{2,1,0:T(8,128)(2,1)S(1)}, u32[]{:S(2)}, u32[]{:S(2)}) async-start(bf16[64,16,128]{2,1,0:T(8,128)(2,1)} %bitcast.6), calls=%async_computation.1 | async-start | bytes 524288 | tf_op jit(solution)/shard_map/all_to_all | solution.py:635
  37.7 3.5 %collective-permute-start = (bf16[8,128,128]{2,1,0:T(8,128)(2,1)S(1)}, bf16[8,128,128]{2,1,0:T(8,128)(2,1)S(1)}, u32[]{:S(2)}, u32[]{:S(2)}) collective-permute-start(bf16[8,128,128]{2,1,0:T(8,128)(2,1)S(1)} %all-to-all-done.arrived.own), channel_id=1, source_target_pairs={{0,8},{8,0},{16,24},{24,16},{32,40},{40,32},{48,56},{56,48},{64,72... | collective-permute-start | bytes 786440 | tf_op jit(solution)/shard_map/ppermute | solution.py:636
  40.1 0.7 copy-start.11
  41.0 1.7 %copy-start.10 = (f32[6,72,256]{2,1,0:T(8,128)}, f32[6,72,256]{2,1,0:T(8,128)S(1)}, u32[]{:S(2)}) copy-start(f32[6,72,256]{2,1,0:T(8,128)S(1)} %fusion.1.refs_9_) | copy-start | bytes 1327108
  49.6 36.7 %copy-start = (bf16[2,512,384]{2,1,0:T(8,128)(2,1)S(1)}, bf16[2,512,384]{2,1,0:T(8,128)(2,1)}, u32[]{:S(2)}) copy-start(bf16[2,512,384]{2,1,0:T(8,128)(2,1)} %constant.17.clone.high_hbm.table_high) | copy-start | bytes 2359300
  49.7 36.7 %copy-start.1 = (bf16[2,512,384]{2,1,0:T(8,128)(2,1)S(1)}, bf16[2,512,384]{2,1,0:T(8,128)(2,1)}, u32[]{:S(2)}) copy-start(bf16[2,512,384]{2,1,0:T(8,128)(2,1)} %constant.18.clone.low_hbm.table_low) | copy-start | bytes 2359300
  59.9 26.4 %copy-start.2 = (f32[69,2,1,384]{3,2,1,0:T(1,128)S(1)}, f32[69,2,1,384]{3,2,1,0:T(1,128)}, u32[]{:S(2)}) copy-start(f32[69,2,1,384]{3,2,1,0:T(1,128)} %control.1) | copy-start | bytes 635908
  59.9 26.4 %copy-start.3 = (f32[69,1,384]{2,1,0:T(1,128)S(1)}, f32[69,1,384]{2,1,0:T(1,128)}, u32[]{:S(2)}) copy-start(f32[69,1,384]{2,1,0:T(1,128)} %sigma.1) | copy-start | bytes 317956
